TPU v7x, 32 devices: a whole 2x2x4 slice. The times are simulated.
32 devices in a mesh: row: 8 (over z, core), col: 4 (over y, x).
Axes of the slice: x: 2, y: 2, z: 4, core: 2. Of those that a mesh axis runs over, the one named last changes fastest.
Arguments:
- features: bfloat16 [4, 1024, 256], P('col', 'row'), may hold values from -6 to 6
- tiles: bfloat16 [8, 4, 3, 128, 128], P('row', 'col'), may hold values from -4 to 4
- tile_rows: int32 [8, 4, 3], P('row', 'col'), may hold values from 0 to 3, as said below
- tile_cols: int32 [8, 4, 3], P('row', 'col'), may hold values from 0 to 7, as said below
- tile_count: int32 [8, 4], P('row', 'col'), may hold values from 1 to 3, as said below
- weight: bfloat16 [256, 256], replicated, may hold values from -0.375 to 0.375
- bias: float32 [256], replicated, may hold values from -3 to 3
- cotangent: bfloat16 [8, 512, 256], P('row', 'col'), may hold values from -6 to 6
- label_mask: int32 [8, 512], P('row', 'col'), may hold values 0 or 1
Outputs:
- hidden: bfloat16 [8, 512, 256], P('row', 'col')
- grad_weight: float32 [256, 256], replicated
- grad_bias: float32 [256], replicated
- grad_features: bfloat16 [4, 1024, 256], P('col', 'row')
Inputs may be any that keep to these rules, and one draw needn't show every extreme that they name: `tile_rows`: tile row among the 4 tile rows of a block; the (row, column) positions of one block's slots are all distinct. `tile_cols`: tile column among the 8 tile columns of a block. The live slots of a block are its first tile_count slots; some block has all 3 slots live.
All inputs are finite; a program needn't handle non-finite values. No bound on the sum of `label_mask` on one device may be relied on, other than what follows from the above.
Results may differ from a plain program's by a relative error of at most 0.023.
Values may be sent and summed in bfloat16 or wider, within the bound.
No kernel may reach another device: no remote copies, remote signals or barrier semaphores. Data moves between devices by JAX's collectives and lax.ppermute only.
A program may use at most 64 MiB of HBM per device.

v0:
```python
import math

import jax
import jax.numpy as jnp
from jax import lax
from jax.sharding import PartitionSpec as P


def from_behind(shard, axis, by):
    size = lax.axis_size(axis)
    return lax.ppermute(shard, axis, [(i, (i + by) % size) for i in range(size)])


def tile_products(block_tiles, take_index, put_index, live_count, source, out_tiles, transpose):
    total_slots = block_tiles.shape[0]
    group = math.gcd(total_slots, 16)
    tile_size = block_tiles.shape[1]
    width = source.shape[-1]
    form = "sij,sif->sjf" if transpose else "sij,sjf->sif"

    def step(turn, accum):
        start = turn * group
        block = lax.dynamic_slice_in_dim(block_tiles, start, group, 0)
        take = lax.dynamic_slice_in_dim(take_index, start, group, 0)
        put = lax.dynamic_slice_in_dim(put_index, start, group, 0)
        live = start + jnp.arange(group, dtype=jnp.int32) < live_count
        picked = jnp.take(source, take, axis=0)
        product = jnp.einsum(form, block, picked, preferred_element_type=jnp.float32)
        product = jnp.where(live[:, None, None], product, 0.0)
        return accum.at[put].add(product)

    turns = (live_count + group - 1) // group
    start_value = jnp.zeros((out_tiles, tile_size, width), jnp.float32)
    return lax.fori_loop(0, turns, step, start_value)


def times_weight_t(values, weight):
    return lax.dot_general(
        values, weight, (((1,), (1,)), ((), ())), preferred_element_type=jnp.float32
    ).astype(jnp.bfloat16)


def on_device(
    features, tiles, tile_rows, tile_cols, tile_count, weight, bias, cotangent, label_mask
):
    tile_size = tiles.shape[-1]
    rows_dev = features.shape[1]
    width = features.shape[2]
    n_row = lax.axis_size("row")
    n_col = lax.axis_size("col")
    own_tiles = tiles[0, 0]
    rows_index = tile_rows[0, 0]
    cols_index = tile_cols[0, 0]
    live_count = tile_count[0, 0]
    gathered = lax.all_gather(features, "row", axis=1, tiled=True)
    source = gathered.reshape(n_row * rows_dev // tile_size, tile_size, width)
    partial_value = tile_products(
        own_tiles, cols_index, rows_index, live_count, source, n_col * rows_dev // tile_size, False
    )
    partial_value = partial_value.reshape(n_col * rows_dev, width)
    own_place = lax.axis_index("col")

    def carry_step(turn, running):
        target = (own_place + n_col - 1 - turn) % n_col
        running = running + lax.dynamic_slice_in_dim(partial_value, target * rows_dev, rows_dev, 0)
        return from_behind(running.astype(jnp.bfloat16), "col", 1).astype(running.dtype)

    running = lax.fori_loop(0, n_col - 1, carry_step, jnp.zeros((rows_dev, width), jnp.float32))
    summed = running + lax.dynamic_slice_in_dim(partial_value, own_place * rows_dev, rows_dev, 0)
    aggregated = summed.astype(jnp.bfloat16)
    pre_act = jnp.dot(aggregated, weight, preferred_element_type=jnp.float32) + bias
    sigma = jax.nn.sigmoid(pre_act)
    hidden = (pre_act * sigma).astype(jnp.bfloat16)
    kept = label_mask[0].astype(jnp.float32)[:, None]
    slope = sigma * (1.0 + pre_act * (1.0 - sigma))
    grad_pre = (cotangent[0].astype(jnp.float32) * kept * slope).astype(jnp.bfloat16)
    local_weight = lax.dot_general(
        aggregated, grad_pre, (((0,), (0,)), ((), ())), preferred_element_type=jnp.float32
    )
    local_bias = jnp.sum(grad_pre.astype(jnp.float32), axis=0)
    grad_weight, grad_bias = lax.psum((local_weight, local_bias), ("row", "col"))
    scale = 1.0 / math.sqrt(n_row * n_col * rows_dev)
    grad_agg = times_weight_t(grad_pre, weight)
    grad_rows = lax.all_gather(grad_agg[None], "col", axis=1, tiled=True)[0]
    back_source = grad_rows.reshape(n_col * rows_dev // tile_size, tile_size, width)
    back = tile_products(
        own_tiles,
        rows_index,
        cols_index,
        live_count,
        back_source,
        n_row * rows_dev // tile_size,
        True,
    )
    back = back.reshape(n_row * rows_dev, width)
    back = lax.optimization_barrier(back.astype(jnp.bfloat16)).astype(jnp.float32)
    grad_sum = lax.psum_scatter(back.astype(jnp.bfloat16), "row", scatter_dimension=0, tiled=True)
    return (hidden[None], grad_weight * scale, grad_bias * scale, grad_sum[None])


def solution(mesh):
    return jax.shard_map(
        on_device,
        mesh=mesh,
        in_specs=(
            P("col", "row", None),
            P("row", "col", None, None, None),
            P("row", "col", None),
            P("row", "col", None),
            P("row", "col"),
            P(),
            P(),
            P("row", "col", None),
            P("row", "col"),
        ),
        out_specs=(P("row", "col", None), P(), P(), P("col", "row", None)),
        check_vma=False,
    )
```

profile of v0, /device:TPU:0, one launch (start us, length us, event | category | flops | bytes accessed | tf_op | source)
XLA Modules:
  0.0 202.7 jit_solution(5363552572953003993)
XLA Ops:
  8.7 16.8 %all_gather.6 = bf16[1,1024,256]{2,1,0:T(8,128)(2,1)S(1)} all-gather(bf16[1,128,256]{2,1,0:T(8,128)(2,1)} %param.19), channel_id=1, replica_groups=mesh['row'=8,'col'=4] {'row'}, dimensions={1}, use_global_device_ids=true | all-gather | bytes 589824 | tf_op jit(solution)/shard_map/all_gather | solution.py:55
  25.6 0.8 copy-done.1
  26.4 15.9 %while.40 = (s32[]{:T(128)}, f32[4,128,256]{2,1,0:T(8,128)S(1)}, s32[]{:T(128)}, s32[3]{0:T(128)S(1)}, s32[1,1]{1,0:T(1,128)}, /*index=5*/bf16[3,128,128]{2,1,0:...) while((s32[]{:T(128)}, f32[4,128,256]{2,1,0:T(8,128)S(1)}, ...), condition=%wide.region_2.3_spmd, body=%wide.region_0.2_spmd.sunk | while | flops 8519712 | bytes 360797 | solution.py:34
  32.5 0.7 and_reduce_fusion.4
  33.3 0.8 fusion.43
  40.2 0.7 and_reduce_fusion.4
  40.9 0.8 fusion.43
  42.3 16.0 %while.42 = (s32[]{:T(128)}, f32[128,256]{1,0:T(8,128)S(1)}, s32[]{:T(128)}, f32[512,256]{1,0:T(8,128)S(1)}, s32[]{:T(128)}, /*index=5*/s32[]{:T(128)}, s32[]{:T(128)}, s32[]{:T(128)}, s32[]{:T(128)}, s32[]{:T(128)}) while((s32[]{:T(128)}, f32[128,256]{1,0:T(8,128)S(1)}, s32[]{:T(128)}, f32[512,256]{1,0:T(8,128)S(1)}, s32[]{:T(128)}, ...), condition=%wide.region_4.5_spmd.clone, body=%wide.region_3.4_spmd.clone.sunk | while | flops 131091 | bytes 786754 | solution.py:68
  42.4 5.2 %collective-permute-done = bf16[128,256]{1,0:T(8,128)(2,1)S(1)} collective-permute-done((bf16[128,256]{1,0:T(8,128)(2,1)S(1)}, bf16[128,256]{1,0:T(8,128)(2,1)S(1)}, u32[]{:S(2)}, u32[]{:S(2)}) %collective-permute-start) | collective-permute-done | bytes 65568 | tf_op jit(solution)/shard_map/while/body/eval_jaxpr/ppermute | solution.py:11
  47.8 5.2 %collective-permute-done = bf16[128,256]{1,0:T(8,128)(2,1)S(1)} collective-permute-done((bf16[128,256]{1,0:T(8,128)(2,1)S(1)}, bf16[128,256]{1,0:T(8,128)(2,1)S(1)}, u32[]{:S(2)}, u32[]{:S(2)}) %collective-permute-start) | collective-permute-done | bytes 65568 | tf_op jit(solution)/shard_map/while/body/eval_jaxpr/ppermute | solution.py:11
  53.1 5.2 %collective-permute-done = bf16[128,256]{1,0:T(8,128)(2,1)S(1)} collective-permute-done((bf16[128,256]{1,0:T(8,128)(2,1)S(1)}, bf16[128,256]{1,0:T(8,128)(2,1)S(1)}, u32[]{:S(2)}, u32[]{:S(2)}) %collective-permute-start) | collective-permute-done | bytes 65568 | tf_op jit(solution)/shard_map/while/body/eval_jaxpr/ppermute | solution.py:11
  58.3 0.8 copy-done.4
  59.1 0.8 convert_reduce_fusion
  60.0 0.9 fusion.27
  61.2 7.5 %all-gather = bf16[512,256]{1,0:T(8,128)(2,1)S(1)} all-gather(bf16[128,256]{1,0:T(8,128)(2,1)S(1)} %convolution_convert_fusion), channel_id=2, replica_groups=mesh['row'=8,'col'=4] {'col'}, dimensions={0}, use_global_device_ids=true | all-gather | bytes 327680 | tf_op jit(solution)/shard_map/all_gather | solution.py:84
  69.3 16.0 %while.41 = (s32[]{:T(128)}, f32[8,128,256]{2,1,0:T(8,128)S(1)}, s32[]{:T(128)}, s32[3]{0:T(128)S(1)}, s32[1,1]{1,0:T(1,128)}, /*index=5*/bf16[3,128,128]{2,1,0:...) while((s32[]{:T(128)}, f32[8,128,256]{2,1,0:T(8,128)S(1)}, ...), condition=%wide.region_10.11_spmd, body=%wide.region_8.10_spmd.sunk | while | flops 8519712 | bytes 360797 | solution.py:34
  75.4 0.7 and_reduce_fusion.5
  76.2 0.8 fusion.46
  83.1 0.7 and_reduce_fusion.5
  83.8 0.8 fusion.46
  85.3 0.8 convert_element_type.68
  86.2 54.9 %psum.15 = f32[256]{0:T(256)S(1)} all-reduce(f32[256]{0:T(256)S(1)} %get-tuple-element.309), channel_id=1, replica_groups=mesh['row'=8,'col'=4] {'row','col'}, use_global_device_ids=true, to_apply=%region_7.8 | all-reduce | flops 256 | bytes 2048 | tf_op jit(solution)/shard_map/psum | solution.py:81
  141.6 52.0 %all-reduce.2.cloned.1.call-done = f32[256,256]{1,0:T(8,128)} async-done(((f32[256,256]{1,0:T(8,128)}), f32[256,256]{1,0:T(8,128)}) %all-reduce.2.cloned.1.call-update) | async-done | bytes 262160 | tf_op jit(solution)/shard_map/psum | solution.py:81
  193.6 1.7 broadcast_multiply_fusion
  (45 shorter events, 7.2 us)
Async XLA Ops:
  8.0 50.3 %copy-start = (bf16[256,256]{1,0:T(8,128)(2,1)S(1)}, bf16[256,256]{1,0:T(8,128)(2,1)}, u32[]{:S(2)}) copy-start(bf16[256,256]{1,0:T(8,128)(2,1)} %param.24) | copy-start | bytes 393220
  8.0 185.5 %all-reduce.2.cloned.1.call-start = ((), (), s32[]{:S(2)}) async-start(), calls=%async_computation.1 | async-start | bytes 524288 | tf_op jit(solution)/shard_map/psum | solution.py:81
  8.1 0.7 copy-start.6
  25.5 0.9 copy-start.1
  25.5 0.9 copy-start.3
  25.5 0.9 copy-start.7
  25.5 0.9 copy-start.8
  42.4 5.3 %collective-permute-start = (bf16[128,256]{1,0:T(8,128)(2,1)S(1)}, bf16[128,256]{1,0:T(8,128)(2,1)S(1)}, u32[]{:S(2)}, u32[]{:S(2)}) collective-permute-start(bf16[128,256]{1,0:T(8,128)(2,1)S(1)} %fusion.47), channel_id=1, source_target_pairs={{0,1},{1,2},{2,3},{3,0},{4,5},{5,6},{6,7},{7,4},{8,9},{9,10},{10,1... | collective-permute-start | bytes 196616 | tf_op jit(solution)/shard_map/while/body/eval_jaxpr/ppermute | solution.py:11
  47.7 5.2 %collective-permute-start = (bf16[128,256]{1,0:T(8,128)(2,1)S(1)}, bf16[128,256]{1,0:T(8,128)(2,1)S(1)}, u32[]{:S(2)}, u32[]{:S(2)}) collective-permute-start(bf16[128,256]{1,0:T(8,128)(2,1)S(1)} %fusion.47), channel_id=1, source_target_pairs={{0,1},{1,2},{2,3},{3,0},{4,5},{5,6},{6,7},{7,4},{8,9},{9,10},{10,1... | collective-permute-start | bytes 196616 | tf_op jit(solution)/shard_map/while/body/eval_jaxpr/ppermute | solution.py:11
  53.0 5.2 %collective-permute-start = (bf16[128,256]{1,0:T(8,128)(2,1)S(1)}, bf16[128,256]{1,0:T(8,128)(2,1)S(1)}, u32[]{:S(2)}, u32[]{:S(2)}) collective-permute-start(bf16[128,256]{1,0:T(8,128)(2,1)S(1)} %fusion.47), channel_id=1, source_target_pairs={{0,1},{1,2},{2,3},{3,0},{4,5},{5,6},{6,7},{7,4},{8,9},{9,10},{10,1... | collective-permute-start | bytes 196616 | tf_op jit(solution)/shard_map/while/body/eval_jaxpr/ppermute | solution.py:11
  58.3 0.8 copy-start.4
  58.3 0.8 copy-start.5
  60.9 134.3 %reduce-scatter.2.cloned.1.call-start = ((), (), s32[]{:S(2)}) async-start(), calls=%async_computation.2 | async-start | bytes 589824 | tf_op jit(solution)/shard_map/reduce_scatter | solution.py:97
  68.7 0.7 copy-start.2
Sparse Core Ops, SparseCore 0:
  61.0 132.4 all-reduce.1
Sparse Core Ops, SparseCore 1:
  86.3 46.1 reduce-scatter.1
where the time goes:
time: 203 us
  blocking collectives  79.1 us (39%)
  waiting for transfers between devices  67.5 us (33%)
  loops' own time  21.3 us (10%)
  between operations  15.6 us (8%)
  local copies, waits for them, and re-layouts  7.66 us (4%)
  other arithmetic  6.07 us (3%)
  matrix products  5.13 us (3%)
    psum x1, blocking collectives, on_device(): lax.psum((local_weight, local_bias), ('row', 'col'))  54.9 us
    psum x1, waiting for transfers between devices, on_device(): lax.psum((local_weight, local_bias), ('row', 'col'))  52 us
    another operation x2, loops' own time, tile_products(): return lax.fori_loop(0, turns, step, start_value)  21.1 us
    all_gather x1, blocking collectives, on_device(): gathered = lax.all_gather(features, 'row', axis=1, tiled=True)  16.8 us
    ppermute x3, waiting for transfers between devices, from_behind(): lax.ppermute(shard, axis, [(i, (i + by) % size) for i in range(size)])  15.5 us
    all_gather x1, blocking collectives, on_device(): grad_rows = lax.all_gather(grad_agg[None], 'col', axis=1, tiled=True)[0]  7.5 us
  transfers between devices with their start and end apart: 5, of which 4 were waited for; matrix products, arithmetic and copies ran while one was open for 4% of the time, Pallas kernels for 0%

commit v1 on v0

v1 whole, which is shorter than its diff:
```python
import functools
import math

import jax
import jax.numpy as jnp
from jax import lax
from jax.experimental import pallas as pl
from jax.experimental.pallas import tpu as pltpu
from jax.sharding import PartitionSpec as P

F32 = jnp.float32
BF16 = jnp.bfloat16
PAD = 16
ROWS_ROWS = (((0,), (0,)), ((), ()))
COLS_COLS = (((1,), (1,)), ((), ()))


def each(count, body):
    if count <= 16:
        for i in range(count):
            body(i)
    else:
        lax.fori_loop(0, count, lambda i, carry: (body(i), carry)[1], 0)


def exchange(value, axis, mask):
    size = lax.axis_size(axis)
    return lax.ppermute(value, axis, [(i, i ^ mask) for i in range(size)])


def tree_sum(terms):
    terms = list(terms)
    while len(terms) > 1:
        terms = [a + b for a, b in zip(terms[::2], terms[1::2], strict=True)]
    return terms[0]


def two_halves(row):
    high = row.astype(BF16)
    low = (row - high.astype(F32)).astype(BF16)
    place = lax.broadcasted_iota(jnp.int32, (PAD, row.shape[-1]), 0)
    block = jnp.where(place == 0, high.astype(F32), jnp.where(place == 1, low.astype(F32), 0.0))
    return block.astype(BF16)


def joined(block):
    rows = block.astype(F32)
    return rows[0:1] + rows[1:2]


def forward_kernel(slots, n_col, blocks, ints, tiles, *refs):
    n_row = len(refs) - 3
    sources, out, held, total = refs[:n_row], refs[n_row], refs[n_row + 1], refs[n_row + 2]
    side = tiles.shape[-1]
    for q in range(n_row):
        held[q] = sources[q][...]
    me_row, live = ints[0], ints[2]

    def product(s):
        taken = held[ints[3 + slots + s] ^ me_row]
        value = jnp.dot(tiles[s], taken, preferred_element_type=F32)
        return jnp.where(s < live, value, 0.0)

    if blocks == slots:
        for s in range(slots):
            out[s * side : (s + 1) * side] = product(s).astype(BF16)
        return
    total[...] = jnp.zeros_like(total)

    def add(s):
        total[ints[3 + s]] += product(s)

    each(slots, add)
    for t in range(n_col):
        out[t * side : (t + 1) * side] = total[t].astype(BF16)


def middle_kernel(slots, n_row, n_col, blocks, ints, weight, bias, tiles, *refs):
    products, refs = refs[:n_col], refs[n_col:]
    cots, refs = refs[:n_col], refs[n_col:]
    hidden, sent, kept, kept_weight, prods, total, agg, grads, grad_agg, weights, back = refs
    side = tiles.shape[-1]
    half = weight.shape[0] // 2
    me_row, me_col, live = ints[0], ints[1], ints[2]
    for q in range(n_col):
        prods[q] = products[q][...]
    total[...] = jnp.zeros_like(total)

    def add(i):
        c, p = i // blocks, i % blocks
        q = me_col ^ c
        start = p * side
        place = ints[3 + 2 * slots + q * blocks + p]
        total[place] += prods[q, pl.ds(start, side), :].astype(F32)

    each(n_col * blocks, add)
    for q in range(n_col):
        t = me_col ^ q
        rows = pl.ds(pl.multiple_of(t * side, side), side)
        aggregated = total[t].astype(BF16)
        agg[rows, :] = aggregated
        pre_act = jnp.dot(aggregated, weight[...], preferred_element_type=F32) + bias[...]
        sigma = jax.nn.sigmoid(pre_act)
        if q == 0:
            hidden[...] = (pre_act * sigma).astype(BF16)
        slope = sigma * (1.0 + pre_act * (1.0 - sigma))
        grad_pre = (cots[q][0:side].astype(F32) * slope).astype(BF16)
        grads[rows, :] = grad_pre
        grad_agg[t] = lax.dot_general(
            grad_pre, weight[...], COLS_COLS, preferred_element_type=F32
        ).astype(BF16)
    back[...] = jnp.zeros_like(back)

    def put(s):
        value = lax.dot_general(
            tiles[s], grad_agg[ints[3 + s]], ROWS_ROWS, preferred_element_type=F32
        )
        back[ints[3 + slots + s] ^ me_row] += jnp.where(s < live, value, 0.0)

    each(slots, put)
    for m in range(n_row // 2):
        kept[m * side : (m + 1) * side] = back[2 * m]
        sent[m * side : (m + 1) * side] = back[2 * m + 1].astype(BF16)
    weights[...] = lax.dot_general(
        agg[...], grads[...], ROWS_ROWS, preferred_element_type=F32
    ).reshape(weights.shape)
    core = me_row % 2
    after = n_row // 2 * side
    kept_weight[...] = weights[core]
    sent[after : after + half] = weights[1 - core].astype(BF16)
    column_sum = jnp.sum(grads[...].astype(F32), axis=0, keepdims=True)
    sent[after + half : after + half + PAD] = two_halves(column_sum)


def chip_kernel(kept, kept_weight, own_sent, came, mine, *outs):
    half, side = kept_weight.shape[0], mine.shape[0]
    after = kept.shape[0]
    mine[...] = kept[0:side] + came[0:side].astype(F32)
    weights = (kept_weight[...] + came[after : after + half].astype(F32)).astype(BF16)
    ends = slice(after + half, after + half + PAD)
    column_sum = two_halves(joined(own_sent[ends]) + joined(came[ends]))
    for m, out in enumerate(outs, 1):
        part = slice(m * side, (m + 1) * side)
        out[0:side] = (kept[part] + came[part].astype(F32)).astype(BF16)
        out[side : side + half] = weights
        out[side + half : side + half + PAD] = column_sum


def line_kernel(scale, mine, own, *refs):
    came, (grad_features, weights, grad_bias) = refs[:-3], refs[-3:]
    side, half = mine.shape[0], weights.shape[0]
    total = mine[...]
    for block in came:
        total = total + block[0:side].astype(F32)
    grad_features[...] = total.astype(BF16)
    everyone = (own, *came)
    weights[...] = scale * tree_sum(b[side : side + half].astype(F32) for b in everyone)
    grad_bias[...] = scale * tree_sum(joined(b[side + half : side + half + PAD]) for b in everyone)


def call(kernel, name, outs, scratch, ints, *arrays):
    specs = [pl.BlockSpec(memory_space=pltpu.VMEM)] * len(arrays)
    if ints is not None:
        specs = [pl.BlockSpec(memory_space=pltpu.SMEM)] + specs
        arrays = (ints, *arrays)
    return pl.pallas_call(
        kernel,
        name=name,
        out_shape=[jax.ShapeDtypeStruct(shape, dtype) for shape, dtype in outs],
        in_specs=specs,
        out_specs=[pl.BlockSpec(memory_space=pltpu.VMEM)] * len(outs),
        scratch_shapes=[pltpu.VMEM(shape, dtype) for shape, dtype in scratch],
        compiler_params=pltpu.CompilerParams(vmem_limit_bytes=56 * 1024 * 1024),
    )(*arrays)


def on_device(
    features, tiles, tile_rows, tile_cols, tile_count, weight, bias, cotangent, label_mask
):
    side = tiles.shape[-1]
    slots = tiles.shape[2]
    width = features.shape[2]
    n_row = lax.axis_size("row")
    n_col = lax.axis_size("col")
    n_line = n_row // 2
    blocks = min(slots, n_col)
    own_tiles = tiles[0, 0]
    ints = jnp.concatenate(
        [
            lax.axis_index("row").astype(jnp.int32)[None],
            lax.axis_index("col").astype(jnp.int32)[None],
            tile_count[0],
            tile_rows[0, 0],
            tile_cols[0, 0],
        ]
    )

    own = features[0]
    along = [own] + [exchange(own, "row", 2 * m) for m in range(1, n_line)]
    sources = [part for block in along for part in (block, exchange(block, "row", 1))]

    kept = label_mask[0].astype(BF16)[:, None]
    if blocks == slots:
        places = tile_rows[0, 0]
    else:
        places = jnp.arange(blocks, dtype=jnp.int32)
    places = jnp.pad(places, (0, -blocks % PAD))[:, None].astype(BF16)
    with_places = jnp.concatenate([cotangent[0] * kept, jnp.broadcast_to(places, (places.shape[0], width))])
    cots = [with_places] + [exchange(with_places, "col", m) for m in range(1, n_col)]

    (product,) = call(
        functools.partial(forward_kernel, slots, n_col, blocks),
        "tile_products",
        [((blocks * side, width), BF16)],
        [((n_row, side, width), BF16), ((n_col, side, width), F32)],
        ints,
        own_tiles,
        *sources,
    )
    products = [product] + [exchange(product, "col", m) for m in range(1, n_col)]
    all_ints = jnp.concatenate([ints] + [c[side : side + blocks, 0].astype(jnp.int32) for c in cots])
    after = n_line * side
    half = width // 2
    hidden, sent, kept_back, kept_weight = call(
        functools.partial(middle_kernel, slots, n_row, n_col, blocks),
        "dense_layer",
        [
            ((side, width), BF16),
            ((after + half + PAD, width), BF16),
            ((after, width), F32),
            ((half, width), F32),
        ],
        [
            ((n_col, blocks * side, width), BF16),
            ((n_col, side, width), F32),
            ((n_col * side, width), BF16),
            ((n_col * side, width), BF16),
            ((n_col, side, width), BF16),
            ((2, half, width), F32),
            ((n_row, side, width), F32),
        ],
        all_ints,
        weight,
        bias[None],
        own_tiles,
        *products,
        *cots,
    )
    came = exchange(sent, "row", 1)
    mine, *parts = call(
        chip_kernel,
        "chip_sums",
        [((side, width), F32)] + [((side + half + PAD, width), BF16)] * (n_line - 1),
        [],
        None,
        kept_back,
        kept_weight,
        sent,
        came,
    )
    came = [exchange(part, "row", 2 * m) for m, part in enumerate(parts, 1)]
    scale = 1.0 / math.sqrt(n_row * n_col * side)
    grad_features, weights, grad_bias = call(
        functools.partial(line_kernel, scale),
        "line_sums",
        [((side, width), BF16), ((half, width), F32), ((1, width), F32)],
        [],
        None,
        mine,
        parts[0],
        *came,
    )
    other = exchange(weights, "row", 1)
    first = lax.axis_index("row") % 2 == 0
    grad_weight = jnp.concatenate([jnp.where(first, weights, other), jnp.where(first, other, weights)])
    return (hidden[None], grad_weight, grad_bias[0], grad_features[None])


def solution(mesh):
    return jax.shard_map(
        on_device,
        mesh=mesh,
        in_specs=(
            P("col", "row", None),
            P("row", "col", None, None, None),
            P("row", "col", None),
            P("row", "col", None),
            P("row", "col"),
            P(),
            P(),
            P("row", "col", None),
            P("row", "col"),
        ),
        out_specs=(P("row", "col", None), P(), P(), P("col", "row", None)),
        check_vma=False,
    )
```

time: 203 us -> 61.2 us (0.30)
  blocking collectives: 79.1 us -> 0 us
  waiting for transfers between devices: 67.5 us -> 24.5 us
  loops' own time: 21.3 us -> 0 us
  starting transfers between devices: 0.25 us -> 17 us
  between operations: 15.6 us -> 1.43 us
  Pallas kernels: 0 us -> 9.6 us
  matrix products: 5.13 us -> 0 us
  local copies, waits for them, and re-layouts: 7.66 us -> 4.66 us
  other arithmetic: 6.07 us -> 3.68 us
    psum x1 -> x0, blocking collectives: 54.9 us -> none  [on_device(): lax.psum((local_weight, local_bias), ('row', 'col'))]
    psum x1 -> x0, waiting for transfers between devices: 52 us -> none  [on_device(): lax.psum((local_weight, local_bias), ('row', 'col'))]
    all_gather x2 -> x0, blocking collectives: 24.3 us -> none  [the longest x1 16.8 us: on_device(): gathered = lax.all_gather(features, 'row', axis=1, tiled=True)]
    another operation x3 -> x0, loops' own time: 21.3 us -> none  [the longest x2 21.1 us: tile_products(): return lax.fori_loop(0, turns, step, start_value)]
    ppermute x3 -> x18, starting transfers between devices: 0.17 us -> 17 us  [exchange(): return lax.ppermute(value, axis, [(i, i ^ mask) for i in range(size)])]
    pallas_call x0 -> x4, Pallas kernels: none -> 9.6 us  [call(): pl.pallas_call(kernel, name=name, out_shape=[jax.ShapeDtypeStruct(shape,...]
    ppermute x3 -> x18, waiting for transfers between devices: 15.5 us -> 24.5 us  [exchange(): return lax.ppermute(value, axis, [(i, i ^ mask) for i in range(size)])]
    dot_general x7 -> x0, matrix products: 5.13 us -> none  [the longest x4 3.18 us: step(): jnp.einsum(form, block, picked, preferred_element_type=jnp.float32)]
  transfers between devices with their start and end apart: 5 -> 18, of which waited for: 4 -> 11; matrix products, arithmetic and copies ran while one was open for 4% -> 3% of each run, Pallas kernels for 0% -> 3%
where the time goes in v1:
time: 61.2 us; the launch traced here: 60.9 us
  waiting for transfers between devices  24.5 us (40%)
  starting transfers between devices  17 us (28%)
  Pallas kernels  9.6 us (16%)
  local copies, waits for them, and re-layouts  4.66 us (8%)
  other arithmetic  3.68 us (6%)
  between operations  1.43 us (2%)
    ppermute x18, waiting for transfers between devices, exchange(): return lax.ppermute(value, axis, [(i, i ^ mask) for i in range(size)])  24.5 us
    ppermute x18, starting transfers between devices, exchange(): return lax.ppermute(value, axis, [(i, i ^ mask) for i in range(size)])  17 us
    pallas_call x4, Pallas kernels, call(): pl.pallas_call(kernel, name=name, out_shape=[jax.ShapeDtypeStruct(shape,...  9.6 us
    unnamed x42, local copies, waits for them, and re-layouts  3.42 us
  transfers between devices with their start and end apart: 18, of which 11 were waited for; matrix products, arithmetic and copies ran while one was open for 3% of the time, Pallas kernels for 3%

profile of v1, /device:TPU:0, one launch (start us, length us, event | category | flops | bytes accessed | tf_op | source)
XLA Modules:
  0.0 60.9 jit_solution(3219637103426036765)
XLA Ops:
  0.6 0.7 %convert_bitcast_fusion = bf16[128]{0:T(256)(128)(2,1)S(1)} fusion(s32[1,128]{1,0:T(1,128)} %param.17), kind=kLoop, calls=%fused_computation.9 | loop fusion | flops 128 | bytes 768 | tf_op jit(solution)/shard_map/convert_element_type | solution.py:202
  1.3 0.9 %bitcast_multiply_fusion = bf16[128,256]{1,0:T(8,128)(2,1)S(1)} fusion(bf16[1,128,256]{2,1,0:T(8,128)(2,1)} %param.16, bf16[128]{0:T(256)(128)(2,1)S(1)} %convert_bitcast_fusion), kind=kLoop, calls=%fused_computation.2 | loop fusion | flops 32768 | bytes 131328 | tf_op jit(solution)/shard_map/mul | solution.py:208
  2.4 4.0 %collective-permute-start.2 = (bf16[144,256]{1,0:T(8,128)(2,1)S(1)}, bf16[144,256]{1,0:T(8,128)(2,1)S(1)}, u32[]{:S(2)}, u32[]{:S(2)}) collective-permute-start(bf16[144,256]{1,0:T(8,128)(2,1)S(1)} %pad_maximum_fusion.1.refs_4_), channel_id=1, source_target_pairs={{0,3},{1,2},{2,1},{3,0},{4,7},{5,6},{6,5},{7,4},{8,11},{9,10},{10,... | collective-permute-start | bytes 221192 | tf_op jit(solution)/shard_map/ppermute | solution.py:28
  6.3 3.6 %collective-permute-start.8 = (bf16[128,256]{1,0:T(8,128)(2,1)S(1)}, bf16[128,256]{1,0:T(8,128)(2,1)S(1)}, u32[]{:S(2)}, u32[]{:S(2)}) collective-permute-start(bf16[128,256]{1,0:T(8,128)(2,1)S(1)} %bitcast.23), channel_id=1, source_target_pairs={{0,24},{4,28},{8,16},{12,20},{16,8},{20,12},{24,0},{28,4},{1,25},{... | collective-permute-start | bytes 196616 | tf_op jit(solution)/shard_map/ppermute | solution.py:28
  9.9 0.8 %collective-permute-start.4 = (bf16[128,256]{1,0:T(8,128)(2,1)S(1)}, bf16[128,256]{1,0:T(8,128)(2,1)S(1)}, u32[]{:S(2)}, u32[]{:S(2)}) collective-permute-start(bf16[128,256]{1,0:T(8,128)(2,1)S(1)} %bitcast.25), channel_id=1, source_target_pairs={{0,8},{4,12},{8,0},{12,4},{16,24},{20,28},{24,16},{28,20},{1,9},{5... | collective-permute-start | bytes 196616 | tf_op jit(solution)/shard_map/ppermute | solution.py:28
  13.7 1.6 %collective-permute-done.6.refs_4_ = bf16[128,256]{1,0:T(8,128)(2,1)S(1)} collective-permute-done((bf16[128,256]{1,0:T(8,128)(2,1)S(1)}, bf16[128,256]{1,0:T(8,128)(2,1)S(1)}, u32[]{:S(2)}, u32[]{:S(2)}) %collective-permute-start.6) | collective-permute-done | bytes 65568 | tf_op jit(solution)/shard_map/ppermute | solution.py:28
  17.7 2.0 %tile_products.1.refs_0_ = bf16[384,256]{1,0:T(8,128)(2,1)} custom-call(s32[9]{0:T(128)} %concatenate.15.ints, bf16[3,128,128]{2,1,0:T(8,128)(2,1)} %bitcast.20, bf16[128,256]{1,0:T(8,128)(2,1)} %bitcast.22, bf16[128,256]{1,0:T(8,128)(2,1)} %copy-done.15, bf16[128,256]{1,0:T(8,128)(2,1)} %copy-done.14, bf16[128,256]{1,0:T(8,128)(2,1)} %copy-done.18, ...), custom_call_target="tpu_custom_call" | custom-call | tf_op jit(solution)/shard_map/tile_products/pallas_call | solution.py:166
  19.8 1.1 %collective-permute-start.12 = (bf16[384,256]{1,0:T(8,128)(2,1)}, bf16[384,256]{1,0:T(8,128)(2,1)S(1)}, u32[]{:S(2)}, u32[]{:S(2)}) collective-permute-start(bf16[384,256]{1,0:T(8,128)(2,1)} %tile_products.1.refs_0_), channel_id=1, source_target_pairs={{0,3},{1,2},{2,1},{3,0},{4,7},{5,6},{6,5},{7,4},{8,11},{9,10},{10,... | collective-permute-start | bytes 589832 | tf_op jit(solution)/shard_map/ppermute | solution.py:28
  20.9 1.5 %collective-permute-start.11 = (bf16[384,256]{1,0:T(8,128)(2,1)}, bf16[384,256]{1,0:T(8,128)(2,1)S(1)}, u32[]{:S(2)}, u32[]{:S(2)}) collective-permute-start(bf16[384,256]{1,0:T(8,128)(2,1)} %tile_products.1.refs_0_), channel_id=1, source_target_pairs={{0,2},{1,3},{2,0},{3,1},{4,6},{5,7},{6,4},{7,5},{8,10},{9,11},{10,... | collective-permute-start | bytes 589832 | tf_op jit(solution)/shard_map/ppermute | solution.py:28
  22.4 0.9 %collective-permute-start.10 = (bf16[384,256]{1,0:T(8,128)(2,1)}, bf16[384,256]{1,0:T(8,128)(2,1)S(1)}, u32[]{:S(2)}, u32[]{:S(2)}) collective-permute-start(bf16[384,256]{1,0:T(8,128)(2,1)} %tile_products.1.refs_0_), channel_id=1, source_target_pairs={{0,1},{1,0},{2,3},{3,2},{4,5},{5,4},{6,7},{7,6},{8,9},{9,8},{10,11... | collective-permute-start | bytes 589832 | tf_op jit(solution)/shard_map/ppermute | solution.py:28
  24.2 4.6 %collective-permute-done.12.refs_3_ = bf16[384,256]{1,0:T(8,128)(2,1)S(1)} collective-permute-done((bf16[384,256]{1,0:T(8,128)(2,1)}, bf16[384,256]{1,0:T(8,128)(2,1)S(1)}, u32[]{:S(2)}, u32[]{:S(2)}) %collective-permute-start.12) | collective-permute-done | bytes 196640 | tf_op jit(solution)/shard_map/ppermute | solution.py:28
  28.7 3.2 %collective-permute-done.11.refs_2_ = bf16[384,256]{1,0:T(8,128)(2,1)S(1)} collective-permute-done((bf16[384,256]{1,0:T(8,128)(2,1)}, bf16[384,256]{1,0:T(8,128)(2,1)S(1)}, u32[]{:S(2)}, u32[]{:S(2)}) %collective-permute-start.11) | collective-permute-done | bytes 196640 | tf_op jit(solution)/shard_map/ppermute | solution.py:28
  32.7 3.5 %dense_layer.1 = (bf16[128,256]{1,0:T(8,128)(2,1)}, bf16[656,256]{1,0:T(8,128)(2,1)}, f32[512,256]{1,0:T(8,128)}, f32[128,256]{1,0:T(8,128)}) custom-call(s32[21]{0:T(128)} %concatenate.14.ints, bf16[256,256]{1,0:T(8,128)(2,1)} %weight.1, f32[1,256]{1,0:T(1,128)} %bitcast.31, bf16[3,128,128]{2,1,0:T(8,128)(2,1)} %bitcast.21, ...), custom_call_target="tpu_custom_call" | custom-call | tf_op jit(solution)/shard_map/dense_layer/pallas_call | solution.py:166
  36.3 1.8 %collective-permute-done.13.came = bf16[656,256]{1,0:T(8,128)(2,1)S(1)} collective-permute-done((bf16[656,256]{1,0:T(8,128)(2,1)}, bf16[656,256]{1,0:T(8,128)(2,1)S(1)}, u32[]{:S(2)}, u32[]{:S(2)}) %collective-permute-start.13) | collective-permute-done | bytes 335904 | tf_op jit(solution)/shard_map/ppermute | solution.py:28
  38.1 0.7 %copy-done = bf16[656,256]{1,0:T(8,128)(2,1)} copy-done((bf16[656,256]{1,0:T(8,128)(2,1)}, bf16[656,256]{1,0:T(8,128)(2,1)S(1)}, u32[]{:S(2)}) %copy-start) | copy-done | bytes 335896
  38.9 2.1 %chip_sums.1 = (f32[128,256]{1,0:T(8,128)}, bf16[272,256]{1,0:T(8,128)(2,1)}, bf16[272,256]{1,0:T(8,128)(2,1)}, bf16[272,256]{1,0:T(8,128)(2,1)}) custom-call(f32[512,256]{1,0:T(8,128)} %get-tuple-element.16.kept, f32[128,256]{1,0:T(8,128)} %get-tuple-element.17.kept_weight, bf16[656,256]{1,0:T(8,128)(2,1)} %get-tuple-element.18.own_sent, ...), custom_call_target="tpu_custom_call" | custom-call | tf_op jit(solution)/shard_map/chip_sums/pallas_call | solution.py:166
  41.0 1.5 %collective-permute-start.15 = (bf16[272,256]{1,0:T(8,128)(2,1)}, bf16[272,256]{1,0:T(8,128)(2,1)S(1)}, u32[]{:S(2)}, u32[]{:S(2)}) collective-permute-start(bf16[272,256]{1,0:T(8,128)(2,1)} %get-tuple-element.21), channel_id=1, source_target_pairs={{0,16},{4,20},{8,24},{12,28},{16,0},{20,4},{24,8},{28,12},{1,17},{... | collective-permute-start | bytes 417800 | tf_op jit(solution)/shard_map/ppermute | solution.py:28
  42.5 1.6 %collective-permute-start.16 = (bf16[272,256]{1,0:T(8,128)(2,1)}, bf16[272,256]{1,0:T(8,128)(2,1)S(1)}, u32[]{:S(2)}, u32[]{:S(2)}) collective-permute-start(bf16[272,256]{1,0:T(8,128)(2,1)} %get-tuple-element.22), channel_id=1, source_target_pairs={{0,24},{4,28},{8,16},{12,20},{16,8},{20,12},{24,0},{28,4},{1,25},{... | collective-permute-start | bytes 417800 | tf_op jit(solution)/shard_map/ppermute | solution.py:28
  44.5 9.6 %collective-permute-done.15.refs_1_ = bf16[272,256]{1,0:T(8,128)(2,1)S(1)} collective-permute-done((bf16[272,256]{1,0:T(8,128)(2,1)}, bf16[272,256]{1,0:T(8,128)(2,1)S(1)}, u32[]{:S(2)}, u32[]{:S(2)}) %collective-permute-start.15) | collective-permute-done | bytes 139296 | tf_op jit(solution)/shard_map/ppermute | solution.py:28
  54.1 1.0 %collective-permute-done.14.refs_0_ = bf16[272,256]{1,0:T(8,128)(2,1)S(1)} collective-permute-done((bf16[272,256]{1,0:T(8,128)(2,1)}, bf16[272,256]{1,0:T(8,128)(2,1)S(1)}, u32[]{:S(2)}, u32[]{:S(2)}) %collective-permute-start.14) | collective-permute-done | bytes 139296 | tf_op jit(solution)/shard_map/ppermute | solution.py:28
  55.8 1.9 %line_sums.1 = (bf16[128,256]{1,0:T(8,128)(2,1)}, f32[128,256]{1,0:T(8,128)}, f32[1,256]{1,0:T(1,128)}) custom-call(f32[128,256]{1,0:T(8,128)} %get-tuple-element.19.mine, bf16[272,256]{1,0:T(8,128)(2,1)} %get-tuple-element.20.own, bf16[272,256]{1,0:T(8,128)(2,1)} %copy-done.7, bf16[272,256]{1,0:T(8,128)(2,1)} %copy-done.5, bf16[272,256]{1,0:T(8,128)(2,1)} %copy-done.6), custom_call_target="tpu_custom_call" | custom-call | tf_op jit(solution)/shard_map/line_sums/pallas_call | solution.py:166
  57.7 1.6 %collective-permute-done.17 = f32[128,256]{1,0:T(8,128)S(1)} collective-permute-done((f32[128,256]{1,0:T(8,128)}, f32[128,256]{1,0:T(8,128)S(1)}, u32[]{:S(2)}, u32[]{:S(2)}) %collective-permute-start.17) | collective-permute-done | bytes 131104 | tf_op jit(solution)/shard_map/ppermute | solution.py:28
  59.3 0.9 %broadcast_select_fusion.1 = (f32[128,256]{1,0:T(8,128)S(1)}, f32[128,256]{1,0:T(8,128)S(1)}) fusion(f32[128,256]{1,0:T(8,128)} %get-tuple-element.23, f32[128,256]{1,0:T(8,128)S(1)} %collective-permute-done.17, pred[]{:T(512)S(6)} %eq.5), kind=kLoop, calls=%fused_computation.4 | loop fusion | flops 65536 | bytes 524289 | tf_op jit(solution)/shard_map/jit(_where)/select_n | solution.py:275
  60.2 0.7 %pad_maximum_fusion = f32[256,256]{1,0:T(8,128)} fusion(f32[128,256]{1,0:T(8,128)S(1)} %get-tuple-element.27, f32[128,256]{1,0:T(8,128)S(1)} %get-tuple-element.26), kind=kLoop, calls=%fused_computation | loop fusion | flops 65536 | bytes 524288 | tf_op jit(solution)/shard_map/concatenate | solution.py:275
  (70 shorter events, 7.4 us)
Async XLA Ops:
  2.3 4.1 %copy-start.11 = (bf16[1,128,256]{2,1,0:T(8,128)(2,1)S(1)}, bf16[1,128,256]{2,1,0:T(8,128)(2,1)}, u32[]{:S(2)}) copy-start(bf16[1,128,256]{2,1,0:T(8,128)(2,1)} %param.9) | copy-start | bytes 196612
  2.4 17.4 %copy-start.1 = (bf16[144,256]{1,0:T(8,128)(2,1)}, bf16[144,256]{1,0:T(8,128)(2,1)S(1)}, u32[]{:S(2)}) copy-start(bf16[144,256]{1,0:T(8,128)(2,1)S(1)} %pad_maximum_fusion.1.refs_4_) | copy-start | bytes 221188
  2.4 13.5 %collective-permute-start.2 = (bf16[144,256]{1,0:T(8,128)(2,1)S(1)}, bf16[144,256]{1,0:T(8,128)(2,1)S(1)}, u32[]{:S(2)}, u32[]{:S(2)}) collective-permute-start(bf16[144,256]{1,0:T(8,128)(2,1)S(1)} %pad_maximum_fusion.1.refs_4_), channel_id=1, source_target_pairs={{0,3},{1,2},{2,1},{3,0},{4,7},{5,6},{6,5},{7,4},{8,11},{9,10},{10,... | collective-permute-start | bytes 221192 | tf_op jit(solution)/shard_map/ppermute | solution.py:28
  6.3 6.9 %collective-permute-start.8 = (bf16[128,256]{1,0:T(8,128)(2,1)S(1)}, bf16[128,256]{1,0:T(8,128)(2,1)S(1)}, u32[]{:S(2)}, u32[]{:S(2)}) collective-permute-start(bf16[128,256]{1,0:T(8,128)(2,1)S(1)} %bitcast.23), channel_id=1, source_target_pairs={{0,24},{4,28},{8,16},{12,20},{16,8},{20,12},{24,0},{28,4},{1,25},{... | collective-permute-start | bytes 196616 | tf_op jit(solution)/shard_map/ppermute | solution.py:28
  9.9 5.4 %collective-permute-start.6 = (bf16[128,256]{1,0:T(8,128)(2,1)S(1)}, bf16[128,256]{1,0:T(8,128)(2,1)S(1)}, u32[]{:S(2)}, u32[]{:S(2)}) collective-permute-start(bf16[128,256]{1,0:T(8,128)(2,1)S(1)} %bitcast.24), channel_id=1, source_target_pairs={{0,16},{4,20},{8,24},{12,28},{16,0},{20,4},{24,8},{28,12},{1,17},{... | collective-permute-start | bytes 196616 | tf_op jit(solution)/shard_map/ppermute | solution.py:28
  9.9 5.4 %collective-permute-start.4 = (bf16[128,256]{1,0:T(8,128)(2,1)S(1)}, bf16[128,256]{1,0:T(8,128)(2,1)S(1)}, u32[]{:S(2)}, u32[]{:S(2)}) collective-permute-start(bf16[128,256]{1,0:T(8,128)(2,1)S(1)} %bitcast.25), channel_id=1, source_target_pairs={{0,8},{4,12},{8,0},{12,4},{16,24},{20,28},{24,16},{28,20},{1,9},{5... | collective-permute-start | bytes 196616 | tf_op jit(solution)/shard_map/ppermute | solution.py:28
  10.7 5.3 %collective-permute-start.3 = (bf16[128,256]{1,0:T(8,128)(2,1)S(1)}, bf16[128,256]{1,0:T(8,128)(2,1)S(1)}, u32[]{:S(2)}, u32[]{:S(2)}) collective-permute-start(bf16[128,256]{1,0:T(8,128)(2,1)S(1)} %bitcast.26), channel_id=1, source_target_pairs={{0,4},{4,0},{8,12},{12,8},{16,20},{20,16},{24,28},{28,24},{1,5},{5... | collective-permute-start | bytes 196616 | tf_op jit(solution)/shard_map/ppermute | solution.py:28
  13.2 3.9 %copy-start.12 = (bf16[128,256]{1,0:T(8,128)(2,1)}, bf16[128,256]{1,0:T(8,128)(2,1)S(1)}, u32[]{:S(2)}) copy-start(bf16[128,256]{1,0:T(8,128)(2,1)S(1)} %collective-permute-done.8.refs_6_) | copy-start | bytes 196612
  13.2 10.1 %collective-permute-start.1 = (bf16[144,256]{1,0:T(8,128)(2,1)S(1)}, bf16[144,256]{1,0:T(8,128)(2,1)S(1)}, u32[]{:S(2)}, u32[]{:S(2)}) collective-permute-start(bf16[144,256]{1,0:T(8,128)(2,1)S(1)} %pad_maximum_fusion.1.refs_4_), channel_id=1, source_target_pairs={{0,2},{1,3},{2,0},{3,1},{4,6},{5,7},{6,4},{7,5},{8,10},{9,11},{10,... | collective-permute-start | bytes 221192 | tf_op jit(solution)/shard_map/ppermute | solution.py:28
  15.3 1.3 %collective-permute-start.9 = (bf16[128,256]{1,0:T(8,128)(2,1)S(1)}, bf16[128,256]{1,0:T(8,128)(2,1)S(1)}, u32[]{:S(2)}, u32[]{:S(2)}) collective-permute-start(bf16[128,256]{1,0:T(8,128)(2,1)S(1)} %collective-permute-done.8.refs_6_), channel_id=1, source_target_pairs={{0,4},{4,0},{8,12},{12,8},{16,20},{20,16},{24,28},{28,24},{1,5},{5... | collective-permute-start | bytes 196616 | tf_op jit(solution)/shard_map/ppermute | solution.py:28
  15.4 1.4 %collective-permute-start.7 = (bf16[128,256]{1,0:T(8,128)(2,1)S(1)}, bf16[128,256]{1,0:T(8,128)(2,1)S(1)}, u32[]{:S(2)}, u32[]{:S(2)}) collective-permute-start(bf16[128,256]{1,0:T(8,128)(2,1)S(1)} %collective-permute-done.6.refs_4_), channel_id=1, source_target_pairs={{0,4},{4,0},{8,12},{12,8},{16,20},{20,16},{24,28},{28,24},{1,5},{5... | collective-permute-start | bytes 196616 | tf_op jit(solution)/shard_map/ppermute | solution.py:28
  15.8 3.9 %copy-start.8 = (bf16[144,256]{1,0:T(8,128)(2,1)}, bf16[144,256]{1,0:T(8,128)(2,1)S(1)}, u32[]{:S(2)}) copy-start(bf16[144,256]{1,0:T(8,128)(2,1)S(1)} %collective-permute-done.2.refs_7_) | copy-start | bytes 221188
  15.8 1.3 %collective-permute-start.5 = (bf16[128,256]{1,0:T(8,128)(2,1)S(1)}, bf16[128,256]{1,0:T(8,128)(2,1)S(1)}, u32[]{:S(2)}, u32[]{:S(2)}) collective-permute-start(bf16[128,256]{1,0:T(8,128)(2,1)S(1)} %collective-permute-done.4.refs_2_), channel_id=1, source_target_pairs={{0,4},{4,0},{8,12},{12,8},{16,20},{20,16},{24,28},{28,24},{1,5},{5... | collective-permute-start | bytes 196616 | tf_op jit(solution)/shard_map/ppermute | solution.py:28
  16.1 7.4 %collective-permute-start = (bf16[144,256]{1,0:T(8,128)(2,1)S(1)}, bf16[144,256]{1,0:T(8,128)(2,1)S(1)}, u32[]{:S(2)}, u32[]{:S(2)}) collective-permute-start(bf16[144,256]{1,0:T(8,128)(2,1)S(1)} %pad_maximum_fusion.1.refs_4_), channel_id=1, source_target_pairs={{0,1},{1,0},{2,3},{3,2},{4,5},{5,4},{6,7},{7,6},{8,9},{9,8},{10,11... | collective-permute-start | bytes 221192 | tf_op jit(solution)/shard_map/ppermute | solution.py:28
  19.8 9.0 %collective-permute-start.12 = (bf16[384,256]{1,0:T(8,128)(2,1)}, bf16[384,256]{1,0:T(8,128)(2,1)S(1)}, u32[]{:S(2)}, u32[]{:S(2)}) collective-permute-start(bf16[384,256]{1,0:T(8,128)(2,1)} %tile_products.1.refs_0_), channel_id=1, source_target_pairs={{0,3},{1,2},{2,1},{3,0},{4,7},{5,6},{6,5},{7,4},{8,11},{9,10},{10,... | collective-permute-start | bytes 589832 | tf_op jit(solution)/shard_map/ppermute | solution.py:28
  20.9 11.1 %collective-permute-start.11 = (bf16[384,256]{1,0:T(8,128)(2,1)}, bf16[384,256]{1,0:T(8,128)(2,1)S(1)}, u32[]{:S(2)}, u32[]{:S(2)}) collective-permute-start(bf16[384,256]{1,0:T(8,128)(2,1)} %tile_products.1.refs_0_), channel_id=1, source_target_pairs={{0,2},{1,3},{2,0},{3,1},{4,6},{5,7},{6,4},{7,5},{8,10},{9,11},{10,... | collective-permute-start | bytes 589832 | tf_op jit(solution)/shard_map/ppermute | solution.py:28
  22.4 9.6 %collective-permute-start.10 = (bf16[384,256]{1,0:T(8,128)(2,1)}, bf16[384,256]{1,0:T(8,128)(2,1)S(1)}, u32[]{:S(2)}, u32[]{:S(2)}) collective-permute-start(bf16[384,256]{1,0:T(8,128)(2,1)} %tile_products.1.refs_0_), channel_id=1, source_target_pairs={{0,1},{1,0},{2,3},{3,2},{4,5},{5,4},{6,7},{7,6},{8,9},{9,8},{10,11... | collective-permute-start | bytes 589832 | tf_op jit(solution)/shard_map/ppermute | solution.py:28
  23.3 8.7 %copy-start.9 = (bf16[144,256]{1,0:T(8,128)(2,1)}, bf16[144,256]{1,0:T(8,128)(2,1)S(1)}, u32[]{:S(2)}) copy-start(bf16[144,256]{1,0:T(8,128)(2,1)S(1)} %collective-permute-done.1.refs_6_) | copy-start | bytes 221188
  23.4 8.6 %copy-start.10 = (bf16[144,256]{1,0:T(8,128)(2,1)}, bf16[144,256]{1,0:T(8,128)(2,1)S(1)}, u32[]{:S(2)}) copy-start(bf16[144,256]{1,0:T(8,128)(2,1)S(1)} %collective-permute-done.refs_5_) | copy-start | bytes 221188
  36.3 1.9 %collective-permute-start.13 = (bf16[656,256]{1,0:T(8,128)(2,1)}, bf16[656,256]{1,0:T(8,128)(2,1)S(1)}, u32[]{:S(2)}, u32[]{:S(2)}) collective-permute-start(bf16[656,256]{1,0:T(8,128)(2,1)} %get-tuple-element.18.own_sent), channel_id=1, source_target_pairs={{0,4},{4,0},{8,12},{12,8},{16,20},{20,16},{24,28},{28,24},{1,5},{5... | collective-permute-start | bytes 1007624 | tf_op jit(solution)/shard_map/ppermute | solution.py:28
  41.0 13.1 %collective-permute-start.15 = (bf16[272,256]{1,0:T(8,128)(2,1)}, bf16[272,256]{1,0:T(8,128)(2,1)S(1)}, u32[]{:S(2)}, u32[]{:S(2)}) collective-permute-start(bf16[272,256]{1,0:T(8,128)(2,1)} %get-tuple-element.21), channel_id=1, source_target_pairs={{0,16},{4,20},{8,24},{12,28},{16,0},{20,4},{24,8},{28,12},{1,17},{... | collective-permute-start | bytes 417800 | tf_op jit(solution)/shard_map/ppermute | solution.py:28
  42.5 11.6 %collective-permute-start.16 = (bf16[272,256]{1,0:T(8,128)(2,1)}, bf16[272,256]{1,0:T(8,128)(2,1)S(1)}, u32[]{:S(2)}, u32[]{:S(2)}) collective-permute-start(bf16[272,256]{1,0:T(8,128)(2,1)} %get-tuple-element.22), channel_id=1, source_target_pairs={{0,24},{4,28},{8,16},{12,20},{16,8},{20,12},{24,0},{28,4},{1,25},{... | collective-permute-start | bytes 417800 | tf_op jit(solution)/shard_map/ppermute | solution.py:28
  44.1 11.0 %collective-permute-start.14 = (bf16[272,256]{1,0:T(8,128)(2,1)}, bf16[272,256]{1,0:T(8,128)(2,1)S(1)}, u32[]{:S(2)}, u32[]{:S(2)}) collective-permute-start(bf16[272,256]{1,0:T(8,128)(2,1)} %get-tuple-element.20.own), channel_id=1, source_target_pairs={{0,8},{4,12},{8,0},{12,4},{16,24},{20,28},{24,16},{28,20},{1,9},{5... | collective-permute-start | bytes 417800 | tf_op jit(solution)/shard_map/ppermute | solution.py:28
  57.7 1.6 %collective-permute-start.17 = (f32[128,256]{1,0:T(8,128)}, f32[128,256]{1,0:T(8,128)S(1)}, u32[]{:S(2)}, u32[]{:S(2)}) collective-permute-start(f32[128,256]{1,0:T(8,128)} %get-tuple-element.23), channel_id=1, source_target_pairs={{0,4},{4,0},{8,12},{12,8},{16,20},{20,16},{24,28},{28,24},{1,5},{5... | collective-permute-start | bytes 393224 | tf_op jit(solution)/shard_map/ppermute | solution.py:28
  (15 other events, 16.0 us)

commit v2 on v1

--- a/solution.py
+++ b/solution.py
@@ -46,6 +46,20 @@
 def joined(block):
     rows = block.astype(F32)
     return rows[0:1] + rows[1:2]
+
+
+def cotangent_kernel(ints, mask, cotangent, out):
+    side, width = cotangent.shape
+    shape = (side, side)
+    diagonal = lax.broadcasted_iota(jnp.int32, shape, 0) == lax.broadcasted_iota(jnp.int32, shape, 1)
+    spread = jnp.where(diagonal, mask[...].astype(F32), 0.0).astype(BF16)
+    out[0:side] = jnp.dot(spread, cotangent[...], preferred_element_type=F32).astype(BF16)
+    rows = out.shape[0] - side
+    index = lax.broadcasted_iota(jnp.int32, (rows, width), 0)
+    places = jnp.zeros((rows, width), jnp.int32)
+    for p in range(ints.shape[0]):
+        places = jnp.where(index == p, ints[p], places)
+    out[side:] = places.astype(F32).astype(BF16)
 
 
 def forward_kernel(slots, n_col, blocks, ints, tiles, *refs):
@@ -146,31 +160,40 @@
         out[side + half : side + half + PAD] = column_sum
 
 
-def line_kernel(scale, mine, own, *refs):
-    came, (grad_features, weights, grad_bias) = refs[:-3], refs[-3:]
-    side, half = mine.shape[0], weights.shape[0]
+def line_kernel(scale, core, mine, *refs):
+    blocks, (grad_features, grad_weight, grad_bias) = refs[:-3], refs[-3:]
+    side, half = mine.shape[0], grad_weight.shape[0] // 2
+    own, other = blocks[: len(blocks) // 2], blocks[len(blocks) // 2 :]
     total = mine[...]
-    for block in came:
+    for block in own[1:]:
         total = total + block[0:side].astype(F32)
     grad_features[...] = total.astype(BF16)
-    everyone = (own, *came)
-    weights[...] = scale * tree_sum(b[side : side + half].astype(F32) for b in everyone)
-    grad_bias[...] = scale * tree_sum(joined(b[side + half : side + half + PAD]) for b in everyone)
+    for shift, group in enumerate((own, other)):
+        start = pl.multiple_of((core[0] ^ shift) * half, half)
+        grad_weight[pl.ds(start, half), :] = scale * tree_sum(
+            b[side : side + half].astype(F32) for b in group
+        )
+    grad_bias[...] = scale * tree_sum(joined(b[side + half : side + half + PAD]) for b in own)
 
 
 def call(kernel, name, outs, scratch, ints, *arrays):
+    arrays = [pltpu.with_memory_space_constraint(array, pltpu.VMEM) for array in arrays]
     specs = [pl.BlockSpec(memory_space=pltpu.VMEM)] * len(arrays)
     if ints is not None:
         specs = [pl.BlockSpec(memory_space=pltpu.SMEM)] + specs
         arrays = (ints, *arrays)
+    need = sum(math.prod(shape) * jnp.dtype(dtype).itemsize for shape, dtype in scratch)
     return pl.pallas_call(
         kernel,
         name=name,
-        out_shape=[jax.ShapeDtypeStruct(shape, dtype) for shape, dtype in outs],
+        out_shape=[
+            pltpu.VMEM(shape, dtype) if stays else jax.ShapeDtypeStruct(shape, dtype)
+            for shape, dtype, stays in outs
+        ],
         in_specs=specs,
         out_specs=[pl.BlockSpec(memory_space=pltpu.VMEM)] * len(outs),
         scratch_shapes=[pltpu.VMEM(shape, dtype) for shape, dtype in scratch],
-        compiler_params=pltpu.CompilerParams(vmem_limit_bytes=56 * 1024 * 1024),
+        compiler_params=pltpu.CompilerParams(vmem_limit_bytes=need + 8 * 1024 * 1024),
     )(*arrays)
 
 
@@ -185,33 +208,34 @@
     n_line = n_row // 2
     blocks = min(slots, n_col)
     own_tiles = tiles[0, 0]
-    ints = jnp.concatenate(
-        [
-            lax.axis_index("row").astype(jnp.int32)[None],
-            lax.axis_index("col").astype(jnp.int32)[None],
-            tile_count[0],
-            tile_rows[0, 0],
-            tile_cols[0, 0],
-        ]
-    )
+    me_row = lax.axis_index("row").astype(jnp.int32)[None]
+    me_col = lax.axis_index("col").astype(jnp.int32)[None]
+    ints = jnp.concatenate([me_row, me_col, tile_count[0], tile_rows[0, 0], tile_cols[0, 0]])
 
     own = features[0]
     along = [own] + [exchange(own, "row", 2 * m) for m in range(1, n_line)]
     sources = [part for block in along for part in (block, exchange(block, "row", 1))]
 
-    kept = label_mask[0].astype(BF16)[:, None]
     if blocks == slots:
         places = tile_rows[0, 0]
     else:
         places = jnp.arange(blocks, dtype=jnp.int32)
-    places = jnp.pad(places, (0, -blocks % PAD))[:, None].astype(BF16)
-    with_places = jnp.concatenate([cotangent[0] * kept, jnp.broadcast_to(places, (places.shape[0], width))])
+    cotangent, _ = lax.optimization_barrier((cotangent[0], sources[1]))
+    (with_places,) = call(
+        cotangent_kernel,
+        "masked_cotangent",
+        [((side + blocks + -blocks % PAD, width), BF16, True)],
+        [],
+        places,
+        label_mask,
+        cotangent,
+    )
     cots = [with_places] + [exchange(with_places, "col", m) for m in range(1, n_col)]
 
     (product,) = call(
         functools.partial(forward_kernel, slots, n_col, blocks),
         "tile_products",
-        [((blocks * side, width), BF16)],
+        [((blocks * side, width), BF16, True)],
         [((n_row, side, width), BF16), ((n_col, side, width), F32)],
         ints,
         own_tiles,
@@ -225,10 +249,10 @@
         functools.partial(middle_kernel, slots, n_row, n_col, blocks),
         "dense_layer",
         [
-            ((side, width), BF16),
-            ((after + half + PAD, width), BF16),
-            ((after, width), F32),
-            ((half, width), F32),
+            ((side, width), BF16, False),
+            ((after + half + PAD, width), BF16, True),
+            ((after, width), F32, True),
+            ((half, width), F32, True),
         ],
         [
             ((n_col, blocks * side, width), BF16),
@@ -250,7 +274,7 @@
     mine, *parts = call(
         chip_kernel,
         "chip_sums",
-        [((side, width), F32)] + [((side + half + PAD, width), BF16)] * (n_line - 1),
+        [((side, width), F32, True)] + [((side + half + PAD, width), BF16, True)] * (n_line - 1),
         [],
         None,
         kept_back,
@@ -258,21 +282,19 @@
         sent,
         came,
     )
-    came = [exchange(part, "row", 2 * m) for m, part in enumerate(parts, 1)]
+    line = [parts[0]] + [exchange(part, "row", 2 * m) for m, part in enumerate(parts, 1)]
+    other = [exchange(block, "row", 1) for block in line]
     scale = 1.0 / math.sqrt(n_row * n_col * side)
-    grad_features, weights, grad_bias = call(
+    grad_features, grad_weight, grad_bias = call(
         functools.partial(line_kernel, scale),
         "line_sums",
-        [((side, width), BF16), ((half, width), F32), ((1, width), F32)],
+        [((side, width), BF16, False), ((width, width), F32, False), ((1, width), F32, False)],
         [],
-        None,
+        me_row % 2,
         mine,
-        parts[0],
-        *came,
-    )
-    other = exchange(weights, "row", 1)
-    first = lax.axis_index("row") % 2 == 0
-    grad_weight = jnp.concatenate([jnp.where(first, weights, other), jnp.where(first, other, weights)])
+        *line,
+        *other,
+    )
     return (hidden[None], grad_weight, grad_bias[0], grad_features[None])
 
 

time: 61.2 us -> 49.7 us (0.81)
  Pallas kernels: 9.6 us -> 4.54 us
  waiting for transfers between devices: 24.5 us -> 20.8 us
  other arithmetic: 3.68 us -> 0.47 us
  starting transfers between devices: 17 us -> 18.3 us
  local copies, waits for them, and re-layouts: 4.66 us -> 3.65 us
    pallas_call x4 -> x5, Pallas kernels: 9.6 us -> 4.54 us  [call(): pl.pallas_call(kernel, name=name, out_shape=[pltpu.VMEM(shape, dtype) if...]
    ppermute x18 -> x21, waiting for transfers between devices: 24.5 us -> 20.8 us  [exchange(): return lax.ppermute(value, axis, [(i, i ^ mask) for i in range(size)])]
    ppermute x18 -> x21, starting transfers between devices: 17 us -> 18.3 us  [exchange(): return lax.ppermute(value, axis, [(i, i ^ mask) for i in range(size)])]
    select_n x1 -> x0, other arithmetic: 0.92 us -> none  [on_device(): jnp.where(first, weights, other)]
    mul x1 -> x0, other arithmetic: 0.92 us -> none  [on_device(): cotangent[0] * kept]
    concatenate x3 -> x0, other arithmetic: 0.82 us -> none  [the longest x1 0.72 us: on_device(): jnp.concatenate([jnp.where(first, weights, other), jnp.where(first, other...]
    convert_element_type x1 -> x0, other arithmetic: 0.66 us -> none  [on_device(): kept = label_mask[0].astype(BF16)[:, None]]
    unnamed x42 -> x18, local copies, waits for them, and re-layouts: 3.42 us -> 2.83 us
  transfers between devices with their start and end apart: 18 -> 21, of which waited for: 11 -> 10; matrix products, arithmetic and copies ran while one was open for 3% -> 3% of each run, Pallas kernels for 3% -> 3%
where the time goes in v2:
time: 49.7 us; the launch traced here: 49.1 us
  waiting for transfers between devices  20.8 us (42%)
  starting transfers between devices  18.3 us (37%)
  Pallas kernels  4.54 us (9%)
  local copies, waits for them, and re-layouts  3.65 us (7%)
  between operations  1.37 us (3%)
    ppermute x21, waiting for transfers between devices, exchange(): return lax.ppermute(value, axis, [(i, i ^ mask) for i in range(size)])  20.8 us
    ppermute x21, starting transfers between devices, exchange(): return lax.ppermute(value, axis, [(i, i ^ mask) for i in range(size)])  18.3 us
    pallas_call x5, Pallas kernels, call(): pl.pallas_call(kernel, name=name, out_shape=[pltpu.VMEM(shape, dtype) if...  4.54 us
    unnamed x18, local copies, waits for them, and re-layouts  2.83 us
  transfers between devices with their start and end apart: 21, of which 10 were waited for; matrix products, arithmetic and copies ran while one was open for 3% of the time, Pallas kernels for 3%

profile of v2, /device:TPU:0, one launch (start us, length us, event | category | flops | bytes accessed | tf_op | source)
XLA Modules:
  0.0 49.1 jit_solution(17921174873103039899)
XLA Ops:
  0.6 0.5 %collective-permute-start = (bf16[128,256]{1,0:T(8,128)(2,1)}, bf16[128,256]{1,0:T(8,128)(2,1)S(1)}, u32[]{:S(2)}, u32[]{:S(2)}) collective-permute-start(bf16[128,256]{1,0:T(8,128)(2,1)} %bitcast.17), channel_id=1, source_target_pairs={{0,4},{4,0},{8,12},{12,8},{16,20},{20,16},{24,28},{28,24},{1,5},{5... | collective-permute-start | bytes 196616 | tf_op jit(solution)/shard_map/ppermute | solution.py:28
  1.2 4.7 %collective-permute-start.8 = (bf16[128,256]{1,0:T(8,128)(2,1)}, bf16[128,256]{1,0:T(8,128)(2,1)S(1)}, u32[]{:S(2)}, u32[]{:S(2)}) collective-permute-start(bf16[128,256]{1,0:T(8,128)(2,1)} %bitcast.18), channel_id=1, source_target_pairs={{0,24},{4,28},{8,16},{12,20},{16,8},{20,12},{24,0},{28,4},{1,25},{... | collective-permute-start | bytes 196616 | tf_op jit(solution)/shard_map/ppermute | solution.py:28
  5.8 0.6 %collective-permute-start.4 = (bf16[128,256]{1,0:T(8,128)(2,1)}, bf16[128,256]{1,0:T(8,128)(2,1)S(1)}, u32[]{:S(2)}, u32[]{:S(2)}) collective-permute-start(bf16[128,256]{1,0:T(8,128)(2,1)} %bitcast.20), channel_id=1, source_target_pairs={{0,8},{4,12},{8,0},{12,4},{16,24},{20,28},{24,16},{28,20},{1,9},{5... | collective-permute-start | bytes 196616 | tf_op jit(solution)/shard_map/ppermute | solution.py:28
  7.1 0.7 %concatenate.8.ints = s32[9]{0:T(128)S(1)} concatenate(s32[1]{0:T(128)} %bitcast, s32[1]{0:T(128)} %bitcast.1, s32[1]{0:T(128)} %bitcast.13, s32[3]{0:T(128)} %bitcast.22, s32[3]{0:T(128)} %bitcast.26), dimensions={0} | concatenate | bytes 72 | tf_op jit(solution)/shard_map/concatenate | solution.py:213
  7.9 0.8 %copy-done.2 = bf16[1,128,256]{2,1,0:T(8,128)(2,1)S(1)} copy-done((bf16[1,128,256]{2,1,0:T(8,128)(2,1)S(1)}, bf16[1,128,256]{2,1,0:T(8,128)(2,1)}, u32[]{:S(2)}) %copy-start.2) | copy-done | bytes 65560
  8.7 0.7 %copy-done.4 = s32[1,1,3]{2,1,0:T(1,128)S(1)} copy-done((s32[1,1,3]{2,1,0:T(1,128)S(1)}, s32[1,1,3]{2,1,0:T(1,128)}, u32[]{:S(2)}) %copy-start.4) | copy-done | bytes 36
  9.4 0.7 %copy-done.7 = s32[1,128]{1,0:T(1,128)S(1)} copy-done((s32[1,128]{1,0:T(1,128)S(1)}, s32[1,128]{1,0:T(1,128)}, u32[]{:S(2)}) %copy-start.7) | copy-done | bytes 536
  10.0 0.7 %masked_cotangent.1.refs_4_ = bf16[144,256]{1,0:T(8,128)(2,1)S(1)} custom-call(s32[3]{0:T(128)S(1)} %bitcast.23, s32[1,128]{1,0:T(1,128)S(1)} %copy-done.7, bf16[128,256]{1,0:T(8,128)(2,1)S(1)} %bitcast.16), custom_call_target="tpu_custom_call" | custom-call | tf_op jit(solution)/shard_map/masked_cotangent/pallas_call | solution.py:186
  10.7 2.7 %collective-permute-start.3 = (bf16[144,256]{1,0:T(8,128)(2,1)S(1)}, bf16[144,256]{1,0:T(8,128)(2,1)S(1)}, u32[]{:S(2)}, u32[]{:S(2)}) collective-permute-start(bf16[144,256]{1,0:T(8,128)(2,1)S(1)} %masked_cotangent.1.refs_4_), channel_id=1, source_target_pairs={{0,3},{1,2},{2,1},{3,0},{4,7},{5,6},{6,5},{7,4},{8,11},{9,10},{10,... | collective-permute-start | bytes 221192 | tf_op jit(solution)/shard_map/ppermute | solution.py:28
  13.4 0.5 %collective-permute-start.2 = (bf16[144,256]{1,0:T(8,128)(2,1)S(1)}, bf16[144,256]{1,0:T(8,128)(2,1)S(1)}, u32[]{:S(2)}, u32[]{:S(2)}) collective-permute-start(bf16[144,256]{1,0:T(8,128)(2,1)S(1)} %masked_cotangent.1.refs_4_), channel_id=1, source_target_pairs={{0,2},{1,3},{2,0},{3,1},{4,6},{5,7},{6,4},{7,5},{8,10},{9,11},{10,... | collective-permute-start | bytes 221192 | tf_op jit(solution)/shard_map/ppermute | solution.py:28
  14.6 0.5 %collective-permute-done.9.refs_7_ = bf16[128,256]{1,0:T(8,128)(2,1)S(1)} collective-permute-done((bf16[128,256]{1,0:T(8,128)(2,1)S(1)}, bf16[128,256]{1,0:T(8,128)(2,1)S(1)}, u32[]{:S(2)}, u32[]{:S(2)}) %collective-permute-start.9) | collective-permute-done | bytes 65568 | tf_op jit(solution)/shard_map/ppermute | solution.py:28
  15.7 0.8 %tile_products.1.refs_0_ = bf16[384,256]{1,0:T(8,128)(2,1)S(1)} custom-call(s32[9]{0:T(128)S(1)} %concatenate.8.ints, bf16[3,128,128]{2,1,0:T(8,128)(2,1)S(1)} %bitcast.14, bf16[128,256]{1,0:T(8,128)(2,1)S(1)} %bitcast.21, bf16[128,256]{1,0:T(8,128)(2,1)S(1)} %collective-permute-done.refs_1_, bf16[128,256]{1,0:T(8,128)(2,1)S(1)} %collective-permute-done.4.refs_2_, ...), custom_call_target="tpu_custom_call" | custom-call | tf_op jit(solution)/shard_map/tile_products/pallas_call | solution.py:186
  16.5 2.6 %collective-permute-start.12 = (bf16[384,256]{1,0:T(8,128)(2,1)S(1)}, bf16[384,256]{1,0:T(8,128)(2,1)S(1)}, u32[]{:S(2)}, u32[]{:S(2)}) collective-permute-start(bf16[384,256]{1,0:T(8,128)(2,1)S(1)} %tile_products.1.refs_0_), channel_id=1, source_target_pairs={{0,3},{1,2},{2,1},{3,0},{4,7},{5,6},{6,5},{7,4},{8,11},{9,10},{10,... | collective-permute-start | bytes 589832 | tf_op jit(solution)/shard_map/ppermute | solution.py:28
  20.4 0.6 %copy-done.5 = s32[1,1,3]{2,1,0:T(1,128)S(1)} copy-done((s32[1,1,3]{2,1,0:T(1,128)S(1)}, s32[1,1,3]{2,1,0:T(1,128)}, u32[]{:S(2)}) %copy-start.5) | copy-done | bytes 36
  21.1 4.1 %collective-permute-done.12.refs_3_ = bf16[384,256]{1,0:T(8,128)(2,1)S(1)} collective-permute-done((bf16[384,256]{1,0:T(8,128)(2,1)S(1)}, bf16[384,256]{1,0:T(8,128)(2,1)S(1)}, u32[]{:S(2)}, u32[]{:S(2)}) %collective-permute-start.12) | collective-permute-done | bytes 196640 | tf_op jit(solution)/shard_map/ppermute | solution.py:28
  25.2 3.7 %collective-permute-done.11.refs_2_ = bf16[384,256]{1,0:T(8,128)(2,1)S(1)} collective-permute-done((bf16[384,256]{1,0:T(8,128)(2,1)S(1)}, bf16[384,256]{1,0:T(8,128)(2,1)S(1)}, u32[]{:S(2)}, u32[]{:S(2)}) %collective-permute-start.11) | collective-permute-done | bytes 196640 | tf_op jit(solution)/shard_map/ppermute | solution.py:28
  28.9 2.2 %dense_layer.1 = (bf16[128,256]{1,0:T(8,128)(2,1)}, bf16[656,256]{1,0:T(8,128)(2,1)S(1)}, f32[512,256]{1,0:T(8,128)S(1)}, f32[128,256]{1,0:T(8,128)S(1)}) custom-call(s32[21]{0:T(128)S(1)} %concatenate.7.ints, bf16[256,256]{1,0:T(8,128)(2,1)S(1)} %copy-done.1, f32[1,256]{1,0:T(1,128)S(1)} %bitcast.25, bf16[3,128,128]{2,1,0:T(8,128)(2,1)S(1)} %bitcast.15, ...), custom_call_target="tpu_custom_call" | custom-call | tf_op jit(solution)/shard_map/dense_layer/pallas_call | solution.py:186
  31.2 1.6 %collective-permute-done.13.came = bf16[656,256]{1,0:T(8,128)(2,1)S(1)} collective-permute-done((bf16[656,256]{1,0:T(8,128)(2,1)S(1)}, bf16[656,256]{1,0:T(8,128)(2,1)S(1)}, u32[]{:S(2)}, u32[]{:S(2)}) %collective-permute-start.13) | collective-permute-done | bytes 335904 | tf_op jit(solution)/shard_map/ppermute | solution.py:28
  32.8 2.2 %collective-permute-start.15 = (bf16[272,256]{1,0:T(8,128)(2,1)S(1)}, bf16[272,256]{1,0:T(8,128)(2,1)S(1)}, u32[]{:S(2)}, u32[]{:S(2)}) collective-permute-start(bf16[272,256]{1,0:T(8,128)(2,1)S(1)} %get-tuple-element.23), channel_id=1, source_target_pairs={{0,16},{4,20},{8,24},{12,28},{16,0},{20,4},{24,8},{28,12},{1,17},{... | collective-permute-start | bytes 417800 | tf_op jit(solution)/shard_map/ppermute | solution.py:28
  35.0 1.5 %collective-permute-start.16 = (bf16[272,256]{1,0:T(8,128)(2,1)S(1)}, bf16[272,256]{1,0:T(8,128)(2,1)S(1)}, u32[]{:S(2)}, u32[]{:S(2)}) collective-permute-start(bf16[272,256]{1,0:T(8,128)(2,1)S(1)} %get-tuple-element.24), channel_id=1, source_target_pairs={{0,24},{4,28},{8,16},{12,20},{16,8},{20,12},{24,0},{28,4},{1,25},{... | collective-permute-start | bytes 417800 | tf_op jit(solution)/shard_map/ppermute | solution.py:28
  37.1 9.3 %collective-permute-done.15.refs_2_ = bf16[272,256]{1,0:T(8,128)(2,1)S(1)} collective-permute-done((bf16[272,256]{1,0:T(8,128)(2,1)S(1)}, bf16[272,256]{1,0:T(8,128)(2,1)S(1)}, u32[]{:S(2)}, u32[]{:S(2)}) %collective-permute-start.15) | collective-permute-done | bytes 139296 | tf_op jit(solution)/shard_map/ppermute | solution.py:28
  46.3 0.5 %collective-permute-start.20 = (bf16[272,256]{1,0:T(8,128)(2,1)S(1)}, bf16[272,256]{1,0:T(8,128)(2,1)S(1)}, u32[]{:S(2)}, u32[]{:S(2)}) collective-permute-start(bf16[272,256]{1,0:T(8,128)(2,1)S(1)} %collective-permute-done.16.refs_3_), channel_id=1, source_target_pairs={{0,4},{4,0},{8,12},{12,8},{16,20},{20,16},{24,28},{28,24},{1,5},{5... | collective-permute-start | bytes 417800 | tf_op jit(solution)/shard_map/ppermute | solution.py:28
  46.9 0.8 %collective-permute-done.19.refs_6_ = bf16[272,256]{1,0:T(8,128)(2,1)S(1)} collective-permute-done((bf16[272,256]{1,0:T(8,128)(2,1)S(1)}, bf16[272,256]{1,0:T(8,128)(2,1)S(1)}, u32[]{:S(2)}, u32[]{:S(2)}) %collective-permute-start.19) | collective-permute-done | bytes 139296 | tf_op jit(solution)/shard_map/ppermute | solution.py:28
  48.3 0.8 %line_sums.1 = (bf16[128,256]{1,0:T(8,128)(2,1)}, f32[256,256]{1,0:T(8,128)}, f32[1,256]{1,0:T(1,128)}) custom-call(s32[1]{0:T(128)S(6)} %select_n.7.core, f32[128,256]{1,0:T(8,128)S(1)} %get-tuple-element.21.mine, bf16[272,256]{1,0:T(8,128)(2,1)S(1)} %get-tuple-element.22.refs_0_, bf16[272,256]{1,0:T(8,128)(2,1)S(1)} %collective-permute-done.14.refs_1_, ...), custom_call_target="tpu_custom_call" | custom-call | tf_op jit(solution)/shard_map/line_sums/pallas_call | solution.py:186
  (47 shorter events, 3.9 us)
Async XLA Ops:
  0.6 15.0 %copy-start = (bf16[1,1,3,128,128]{4,3,2,1,0:T(8,128)(2,1)S(1)}, bf16[1,1,3,128,128]{4,3,2,1,0:T(8,128)(2,1)}, u32[]{:S(2)}) copy-start(bf16[1,1,3,128,128]{4,3,2,1,0:T(8,128)(2,1)} %param.10) | copy-start | bytes 294916
  0.6 7.2 %collective-permute-start = (bf16[128,256]{1,0:T(8,128)(2,1)}, bf16[128,256]{1,0:T(8,128)(2,1)S(1)}, u32[]{:S(2)}, u32[]{:S(2)}) collective-permute-start(bf16[128,256]{1,0:T(8,128)(2,1)} %bitcast.17), channel_id=1, source_target_pairs={{0,4},{4,0},{8,12},{12,8},{16,20},{20,16},{24,28},{28,24},{1,5},{5... | collective-permute-start | bytes 196616 | tf_op jit(solution)/shard_map/ppermute | solution.py:28
  1.2 12.7 %collective-permute-start.8 = (bf16[128,256]{1,0:T(8,128)(2,1)}, bf16[128,256]{1,0:T(8,128)(2,1)S(1)}, u32[]{:S(2)}, u32[]{:S(2)}) collective-permute-start(bf16[128,256]{1,0:T(8,128)(2,1)} %bitcast.18), channel_id=1, source_target_pairs={{0,24},{4,28},{8,16},{12,20},{16,8},{20,12},{24,0},{28,4},{1,25},{... | collective-permute-start | bytes 196616 | tf_op jit(solution)/shard_map/ppermute | solution.py:28
  5.8 8.1 %collective-permute-start.6 = (bf16[128,256]{1,0:T(8,128)(2,1)}, bf16[128,256]{1,0:T(8,128)(2,1)S(1)}, u32[]{:S(2)}, u32[]{:S(2)}) collective-permute-start(bf16[128,256]{1,0:T(8,128)(2,1)} %bitcast.19), channel_id=1, source_target_pairs={{0,16},{4,20},{8,24},{12,28},{16,0},{20,4},{24,8},{28,12},{1,17},{... | collective-permute-start | bytes 196616 | tf_op jit(solution)/shard_map/ppermute | solution.py:28
  5.8 8.6 %collective-permute-start.4 = (bf16[128,256]{1,0:T(8,128)(2,1)}, bf16[128,256]{1,0:T(8,128)(2,1)S(1)}, u32[]{:S(2)}, u32[]{:S(2)}) collective-permute-start(bf16[128,256]{1,0:T(8,128)(2,1)} %bitcast.20), channel_id=1, source_target_pairs={{0,8},{4,12},{8,0},{12,4},{16,24},{20,28},{24,16},{28,20},{1,9},{5... | collective-permute-start | bytes 196616 | tf_op jit(solution)/shard_map/ppermute | solution.py:28
  10.7 8.8 %collective-permute-start.3 = (bf16[144,256]{1,0:T(8,128)(2,1)S(1)}, bf16[144,256]{1,0:T(8,128)(2,1)S(1)}, u32[]{:S(2)}, u32[]{:S(2)}) collective-permute-start(bf16[144,256]{1,0:T(8,128)(2,1)S(1)} %masked_cotangent.1.refs_4_), channel_id=1, source_target_pairs={{0,3},{1,2},{2,1},{3,0},{4,7},{5,6},{6,5},{7,4},{8,11},{9,10},{10,... | collective-permute-start | bytes 221192 | tf_op jit(solution)/shard_map/ppermute | solution.py:28
  13.4 6.7 %collective-permute-start.2 = (bf16[144,256]{1,0:T(8,128)(2,1)S(1)}, bf16[144,256]{1,0:T(8,128)(2,1)S(1)}, u32[]{:S(2)}, u32[]{:S(2)}) collective-permute-start(bf16[144,256]{1,0:T(8,128)(2,1)S(1)} %masked_cotangent.1.refs_4_), channel_id=1, source_target_pairs={{0,2},{1,3},{2,0},{3,1},{4,6},{5,7},{6,4},{7,5},{8,10},{9,11},{10,... | collective-permute-start | bytes 221192 | tf_op jit(solution)/shard_map/ppermute | solution.py:28
  13.9 1.3 %collective-permute-start.9 = (bf16[128,256]{1,0:T(8,128)(2,1)S(1)}, bf16[128,256]{1,0:T(8,128)(2,1)S(1)}, u32[]{:S(2)}, u32[]{:S(2)}) collective-permute-start(bf16[128,256]{1,0:T(8,128)(2,1)S(1)} %collective-permute-done.8.refs_6_), channel_id=1, source_target_pairs={{0,4},{4,0},{8,12},{12,8},{16,20},{20,16},{24,28},{28,24},{1,5},{5... | collective-permute-start | bytes 196616 | tf_op jit(solution)/shard_map/ppermute | solution.py:28
  13.9 1.6 %collective-permute-start.7 = (bf16[128,256]{1,0:T(8,128)(2,1)S(1)}, bf16[128,256]{1,0:T(8,128)(2,1)S(1)}, u32[]{:S(2)}, u32[]{:S(2)}) collective-permute-start(bf16[128,256]{1,0:T(8,128)(2,1)S(1)} %collective-permute-done.6.refs_4_), channel_id=1, source_target_pairs={{0,4},{4,0},{8,12},{12,8},{16,20},{20,16},{24,28},{28,24},{1,5},{5... | collective-permute-start | bytes 196616 | tf_op jit(solution)/shard_map/ppermute | solution.py:28
  14.4 1.3 %collective-permute-start.5 = (bf16[128,256]{1,0:T(8,128)(2,1)S(1)}, bf16[128,256]{1,0:T(8,128)(2,1)S(1)}, u32[]{:S(2)}, u32[]{:S(2)}) collective-permute-start(bf16[128,256]{1,0:T(8,128)(2,1)S(1)} %collective-permute-done.4.refs_2_), channel_id=1, source_target_pairs={{0,4},{4,0},{8,12},{12,8},{16,20},{20,16},{24,28},{28,24},{1,5},{5... | collective-permute-start | bytes 196616 | tf_op jit(solution)/shard_map/ppermute | solution.py:28
  15.2 5.1 %collective-permute-start.1 = (bf16[144,256]{1,0:T(8,128)(2,1)S(1)}, bf16[144,256]{1,0:T(8,128)(2,1)S(1)}, u32[]{:S(2)}, u32[]{:S(2)}) collective-permute-start(bf16[144,256]{1,0:T(8,128)(2,1)S(1)} %masked_cotangent.1.refs_4_), channel_id=1, source_target_pairs={{0,1},{1,0},{2,3},{3,2},{4,5},{5,4},{6,7},{7,6},{8,9},{9,8},{10,11... | collective-permute-start | bytes 221192 | tf_op jit(solution)/shard_map/ppermute | solution.py:28
  15.7 13.2 %copy-start.1 = (bf16[256,256]{1,0:T(8,128)(2,1)S(1)}, bf16[256,256]{1,0:T(8,128)(2,1)}, u32[]{:S(2)}) copy-start(bf16[256,256]{1,0:T(8,128)(2,1)} %weight.1) | copy-start | bytes 393220
  16.5 8.8 %collective-permute-start.12 = (bf16[384,256]{1,0:T(8,128)(2,1)S(1)}, bf16[384,256]{1,0:T(8,128)(2,1)S(1)}, u32[]{:S(2)}, u32[]{:S(2)}) collective-permute-start(bf16[384,256]{1,0:T(8,128)(2,1)S(1)} %tile_products.1.refs_0_), channel_id=1, source_target_pairs={{0,3},{1,2},{2,1},{3,0},{4,7},{5,6},{6,5},{7,4},{8,11},{9,10},{10,... | collective-permute-start | bytes 589832 | tf_op jit(solution)/shard_map/ppermute | solution.py:28
  19.0 9.9 %collective-permute-start.11 = (bf16[384,256]{1,0:T(8,128)(2,1)S(1)}, bf16[384,256]{1,0:T(8,128)(2,1)S(1)}, u32[]{:S(2)}, u32[]{:S(2)}) collective-permute-start(bf16[384,256]{1,0:T(8,128)(2,1)S(1)} %tile_products.1.refs_0_), channel_id=1, source_target_pairs={{0,2},{1,3},{2,0},{3,1},{4,6},{5,7},{6,4},{7,5},{8,10},{9,11},{10,... | collective-permute-start | bytes 589832 | tf_op jit(solution)/shard_map/ppermute | solution.py:28
  19.5 9.4 %collective-permute-start.10 = (bf16[384,256]{1,0:T(8,128)(2,1)S(1)}, bf16[384,256]{1,0:T(8,128)(2,1)S(1)}, u32[]{:S(2)}, u32[]{:S(2)}) collective-permute-start(bf16[384,256]{1,0:T(8,128)(2,1)S(1)} %tile_products.1.refs_0_), channel_id=1, source_target_pairs={{0,1},{1,0},{2,3},{3,2},{4,5},{5,4},{6,7},{7,6},{8,9},{9,8},{10,11... | collective-permute-start | bytes 589832 | tf_op jit(solution)/shard_map/ppermute | solution.py:28
  21.1 7.8 %copy-start.6 = (f32[256]{0:T(256)S(1)}, f32[256]{0:T(256)}, u32[]{:S(2)}) copy-start(f32[256]{0:T(256)} %param.15) | copy-start | bytes 3076
  31.1 1.6 %collective-permute-start.13 = (bf16[656,256]{1,0:T(8,128)(2,1)S(1)}, bf16[656,256]{1,0:T(8,128)(2,1)S(1)}, u32[]{:S(2)}, u32[]{:S(2)}) collective-permute-start(bf16[656,256]{1,0:T(8,128)(2,1)S(1)} %get-tuple-element.20.own_sent), channel_id=1, source_target_pairs={{0,4},{4,0},{8,12},{12,8},{16,20},{20,16},{24,28},{28,24},{1,5},{5... | collective-permute-start | bytes 1007624 | tf_op jit(solution)/shard_map/ppermute | solution.py:28
  32.8 13.5 %collective-permute-start.15 = (bf16[272,256]{1,0:T(8,128)(2,1)S(1)}, bf16[272,256]{1,0:T(8,128)(2,1)S(1)}, u32[]{:S(2)}, u32[]{:S(2)}) collective-permute-start(bf16[272,256]{1,0:T(8,128)(2,1)S(1)} %get-tuple-element.23), channel_id=1, source_target_pairs={{0,16},{4,20},{8,24},{12,28},{16,0},{20,4},{24,8},{28,12},{1,17},{... | collective-permute-start | bytes 417800 | tf_op jit(solution)/shard_map/ppermute | solution.py:28
  35.0 11.3 %collective-permute-start.16 = (bf16[272,256]{1,0:T(8,128)(2,1)S(1)}, bf16[272,256]{1,0:T(8,128)(2,1)S(1)}, u32[]{:S(2)}, u32[]{:S(2)}) collective-permute-start(bf16[272,256]{1,0:T(8,128)(2,1)S(1)} %get-tuple-element.24), channel_id=1, source_target_pairs={{0,24},{4,28},{8,16},{12,20},{16,8},{20,12},{24,0},{28,4},{1,25},{... | collective-permute-start | bytes 417800 | tf_op jit(solution)/shard_map/ppermute | solution.py:28
  36.6 10.3 %collective-permute-start.14 = (bf16[272,256]{1,0:T(8,128)(2,1)S(1)}, bf16[272,256]{1,0:T(8,128)(2,1)S(1)}, u32[]{:S(2)}, u32[]{:S(2)}) collective-permute-start(bf16[272,256]{1,0:T(8,128)(2,1)S(1)} %get-tuple-element.22.refs_0_), channel_id=1, source_target_pairs={{0,8},{4,12},{8,0},{12,4},{16,24},{20,28},{24,16},{28,20},{1,9},{5... | collective-permute-start | bytes 417800 | tf_op jit(solution)/shard_map/ppermute | solution.py:28
  37.1 9.9 %collective-permute-start.17 = (bf16[272,256]{1,0:T(8,128)(2,1)S(1)}, bf16[272,256]{1,0:T(8,128)(2,1)S(1)}, u32[]{:S(2)}, u32[]{:S(2)}) collective-permute-start(bf16[272,256]{1,0:T(8,128)(2,1)S(1)} %get-tuple-element.22.refs_0_), channel_id=1, source_target_pairs={{0,4},{4,0},{8,12},{12,8},{16,20},{20,16},{24,28},{28,24},{1,5},{5... | collective-permute-start | bytes 417800 | tf_op jit(solution)/shard_map/ppermute | solution.py:28
  46.3 1.4 %collective-permute-start.19 = (bf16[272,256]{1,0:T(8,128)(2,1)S(1)}, bf16[272,256]{1,0:T(8,128)(2,1)S(1)}, u32[]{:S(2)}, u32[]{:S(2)}) collective-permute-start(bf16[272,256]{1,0:T(8,128)(2,1)S(1)} %collective-permute-done.15.refs_2_), channel_id=1, source_target_pairs={{0,4},{4,0},{8,12},{12,8},{16,20},{20,16},{24,28},{28,24},{1,5},{5... | collective-permute-start | bytes 417800 | tf_op jit(solution)/shard_map/ppermute | solution.py:28
  46.3 1.6 %collective-permute-start.20 = (bf16[272,256]{1,0:T(8,128)(2,1)S(1)}, bf16[272,256]{1,0:T(8,128)(2,1)S(1)}, u32[]{:S(2)}, u32[]{:S(2)}) collective-permute-start(bf16[272,256]{1,0:T(8,128)(2,1)S(1)} %collective-permute-done.16.refs_3_), channel_id=1, source_target_pairs={{0,4},{4,0},{8,12},{12,8},{16,20},{20,16},{24,28},{28,24},{1,5},{5... | collective-permute-start | bytes 417800 | tf_op jit(solution)/shard_map/ppermute | solution.py:28
  46.9 1.4 %collective-permute-start.18 = (bf16[272,256]{1,0:T(8,128)(2,1)S(1)}, bf16[272,256]{1,0:T(8,128)(2,1)S(1)}, u32[]{:S(2)}, u32[]{:S(2)}) collective-permute-start(bf16[272,256]{1,0:T(8,128)(2,1)S(1)} %collective-permute-done.14.refs_1_), channel_id=1, source_target_pairs={{0,4},{4,0},{8,12},{12,8},{16,20},{20,16},{24,28},{28,24},{1,5},{5... | collective-permute-start | bytes 417800 | tf_op jit(solution)/shard_map/ppermute | solution.py:28
  (6 other events, 9.1 us)

commit v3 on v2

--- a/solution.py
+++ b/solution.py
@@ -48,7 +48,7 @@
     return rows[0:1] + rows[1:2]
 
 
-def cotangent_kernel(ints, mask, cotangent, out):
+def cotangent_kernel(places, mask, cotangent, out):
     side, width = cotangent.shape
     shape = (side, side)
     diagonal = lax.broadcasted_iota(jnp.int32, shape, 0) == lax.broadcasted_iota(jnp.int32, shape, 1)
@@ -56,22 +56,29 @@
     out[0:side] = jnp.dot(spread, cotangent[...], preferred_element_type=F32).astype(BF16)
     rows = out.shape[0] - side
     index = lax.broadcasted_iota(jnp.int32, (rows, width), 0)
-    places = jnp.zeros((rows, width), jnp.int32)
-    for p in range(ints.shape[0]):
-        places = jnp.where(index == p, ints[p], places)
-    out[side:] = places.astype(F32).astype(BF16)
-
-
-def forward_kernel(slots, n_col, blocks, ints, tiles, *refs):
+    block = jnp.zeros((rows, width), jnp.int32)
+    for p in range(places.shape[0]):
+        block = jnp.where(index == p, places[p], block)
+    out[side:] = block.astype(F32).astype(BF16)
+
+
+def stack_kernel(*refs):
+    out, start = refs[-1], 0
+    for block in refs[:-1]:
+        out[start : start + block.shape[0]] = block[...]
+        start += block.shape[0]
+
+
+def forward_kernel(slots, n_col, blocks, row, count, tile_rows, tile_cols, tiles, *refs):
     n_row = len(refs) - 3
     sources, out, held, total = refs[:n_row], refs[n_row], refs[n_row + 1], refs[n_row + 2]
     side = tiles.shape[-1]
     for q in range(n_row):
         held[q] = sources[q][...]
-    me_row, live = ints[0], ints[2]
+    me_row, live = row[0], count[0]
 
     def product(s):
-        taken = held[ints[3 + slots + s] ^ me_row]
+        taken = held[tile_cols[s] ^ me_row]
         value = jnp.dot(tiles[s], taken, preferred_element_type=F32)
         return jnp.where(s < live, value, 0.0)
 
@@ -82,30 +89,33 @@
     total[...] = jnp.zeros_like(total)
 
     def add(s):
-        total[ints[3 + s]] += product(s)
+        total[tile_rows[s]] += product(s)
 
     each(slots, add)
     for t in range(n_col):
         out[t * side : (t + 1) * side] = total[t].astype(BF16)
 
 
-def middle_kernel(slots, n_row, n_col, blocks, ints, weight, bias, tiles, *refs):
-    products, refs = refs[:n_col], refs[n_col:]
-    cots, refs = refs[:n_col], refs[n_col:]
-    hidden, sent, kept, kept_weight, prods, total, agg, grads, grad_agg, weights, back = refs
+def middle_kernel(slots, n_row, n_col, blocks, *refs):
+    (row, col, count, tile_rows, tile_cols), refs = refs[:5], refs[5:]
+    places, refs = refs[:n_col], refs[n_col:]
+    (weight, bias, tiles, products), refs = refs[:4], refs[4:]
+    steps = n_col.bit_length()
+    cots, refs = refs[:steps], refs[steps:]
+    hidden, sent, kept, kept_weight, total, agg, grads, grad_agg, weights, back, target = refs
     side = tiles.shape[-1]
     half = weight.shape[0] // 2
-    me_row, me_col, live = ints[0], ints[1], ints[2]
+    me_row, me_col, live = row[0], col[0], count[0]
+    total[...] = jnp.zeros_like(total)
+
     for q in range(n_col):
-        prods[q] = products[q][...]
-    total[...] = jnp.zeros_like(total)
+        for p in range(blocks):
+            target[q, p] = places[q][p]
 
     def add(i):
         c, p = i // blocks, i % blocks
         q = me_col ^ c
-        start = p * side
-        place = ints[3 + 2 * slots + q * blocks + p]
-        total[place] += prods[q, pl.ds(start, side), :].astype(F32)
+        total[target[q, p]] += products[c, pl.ds(p * side, side), :].astype(F32)
 
     each(n_col * blocks, add)
     for q in range(n_col):
@@ -118,7 +128,10 @@
         if q == 0:
             hidden[...] = (pre_act * sigma).astype(BF16)
         slope = sigma * (1.0 + pre_act * (1.0 - sigma))
-        grad_pre = (cots[q][0:side].astype(F32) * slope).astype(BF16)
+        step = q.bit_length()
+        start = (q - (1 << step >> 1)) * cots[0].shape[0]
+        cotangent = cots[step][start : start + side]
+        grad_pre = (cotangent.astype(F32) * slope).astype(BF16)
         grads[rows, :] = grad_pre
         grad_agg[t] = lax.dot_general(
             grad_pre, weight[...], COLS_COLS, preferred_element_type=F32
@@ -127,9 +140,9 @@
 
     def put(s):
         value = lax.dot_general(
-            tiles[s], grad_agg[ints[3 + s]], ROWS_ROWS, preferred_element_type=F32
+            tiles[s], grad_agg[tile_rows[s]], ROWS_ROWS, preferred_element_type=F32
         )
-        back[ints[3 + slots + s] ^ me_row] += jnp.where(s < live, value, 0.0)
+        back[tile_cols[s] ^ me_row] += jnp.where(s < live, value, 0.0)
 
     each(slots, put)
     for m in range(n_row // 2):
@@ -160,7 +173,7 @@
         out[side + half : side + half + PAD] = column_sum
 
 
-def line_kernel(scale, core, mine, *refs):
+def line_kernel(scale, row, mine, *refs):
     blocks, (grad_features, grad_weight, grad_bias) = refs[:-3], refs[-3:]
     side, half = mine.shape[0], grad_weight.shape[0] // 2
     own, other = blocks[: len(blocks) // 2], blocks[len(blocks) // 2 :]
@@ -169,7 +182,7 @@
         total = total + block[0:side].astype(F32)
     grad_features[...] = total.astype(BF16)
     for shift, group in enumerate((own, other)):
-        start = pl.multiple_of((core[0] ^ shift) * half, half)
+        start = pl.multiple_of((row[0] % 2 ^ shift) * half, half)
         grad_weight[pl.ds(start, half), :] = scale * tree_sum(
             b[side : side + half].astype(F32) for b in group
         )
@@ -177,11 +190,6 @@
 
 
 def call(kernel, name, outs, scratch, ints, *arrays):
-    arrays = [pltpu.with_memory_space_constraint(array, pltpu.VMEM) for array in arrays]
-    specs = [pl.BlockSpec(memory_space=pltpu.VMEM)] * len(arrays)
-    if ints is not None:
-        specs = [pl.BlockSpec(memory_space=pltpu.SMEM)] + specs
-        arrays = (ints, *arrays)
     need = sum(math.prod(shape) * jnp.dtype(dtype).itemsize for shape, dtype in scratch)
     return pl.pallas_call(
         kernel,
@@ -190,11 +198,22 @@
             pltpu.VMEM(shape, dtype) if stays else jax.ShapeDtypeStruct(shape, dtype)
             for shape, dtype, stays in outs
         ],
-        in_specs=specs,
+        in_specs=[pl.BlockSpec(memory_space=pltpu.SMEM)] * len(ints)
+        + [pl.BlockSpec(memory_space=pltpu.VMEM)] * len(arrays),
         out_specs=[pl.BlockSpec(memory_space=pltpu.VMEM)] * len(outs),
-        scratch_shapes=[pltpu.VMEM(shape, dtype) for shape, dtype in scratch],
+        scratch_shapes=[
+            (pltpu.SMEM if dtype == jnp.int32 else pltpu.VMEM)(shape, dtype) for shape, dtype in scratch
+        ],
         compiler_params=pltpu.CompilerParams(vmem_limit_bytes=need + 8 * 1024 * 1024),
-    )(*arrays)
+    )(*ints, *arrays)
+
+
+def near(array):
+    return pltpu.with_memory_space_constraint(array, pltpu.VMEM)
+
+
+def far(array):
+    return pltpu.with_memory_space_constraint(array, pltpu.HBM)
 
 
 def on_device(
@@ -207,42 +226,57 @@
     n_col = lax.axis_size("col")
     n_line = n_row // 2
     blocks = min(slots, n_col)
-    own_tiles = tiles[0, 0]
-    me_row = lax.axis_index("row").astype(jnp.int32)[None]
-    me_col = lax.axis_index("col").astype(jnp.int32)[None]
-    ints = jnp.concatenate([me_row, me_col, tile_count[0], tile_rows[0, 0], tile_cols[0, 0]])
+    own_tiles = near(tiles[0, 0])
+    row = lax.axis_index("row").astype(jnp.int32)[None]
+    col = lax.axis_index("col").astype(jnp.int32)[None]
+    ints = (tile_count[0], far(tile_rows[0, 0]), far(tile_cols[0, 0]))
 
     own = features[0]
     along = [own] + [exchange(own, "row", 2 * m) for m in range(1, n_line)]
-    sources = [part for block in along for part in (block, exchange(block, "row", 1))]
 
     if blocks == slots:
         places = tile_rows[0, 0]
     else:
         places = jnp.arange(blocks, dtype=jnp.int32)
-    cotangent, _ = lax.optimization_barrier((cotangent[0], sources[1]))
     (with_places,) = call(
         cotangent_kernel,
         "masked_cotangent",
         [((side + blocks + -blocks % PAD, width), BF16, True)],
         [],
-        places,
-        label_mask,
-        cotangent,
-    )
-    cots = [with_places] + [exchange(with_places, "col", m) for m in range(1, n_col)]
-
+        [far(places)],
+        far(label_mask),
+        far(cotangent[0]),
+    )
+    cots, reach = [with_places], 1
+    while reach < n_col:
+        (held,) = call(
+            stack_kernel,
+            "cotangents_so_far",
+            [((reach * with_places.shape[0], width), BF16, True)],
+            [],
+            [],
+            *map(near, cots),
+        ) if reach > 1 else cots
+        cots, reach = cots + [exchange(held, "col", reach)], 2 * reach
+
+    along, cots[0] = lax.optimization_barrier((along, cots[0]))
+    sources = [part for block in along for part in (block, exchange(block, "row", 1))]
     (product,) = call(
         functools.partial(forward_kernel, slots, n_col, blocks),
         "tile_products",
         [((blocks * side, width), BF16, True)],
         [((n_row, side, width), BF16), ((n_col, side, width), F32)],
-        ints,
+        [row, *ints],
         own_tiles,
-        *sources,
-    )
-    products = [product] + [exchange(product, "col", m) for m in range(1, n_col)]
-    all_ints = jnp.concatenate([ints] + [c[side : side + blocks, 0].astype(jnp.int32) for c in cots])
+        *map(near, sources),
+    )
+    products = lax.all_gather(product, "col")
+    each_rows = with_places.shape[0]
+    everyones = [
+        block[start + side : start + side + blocks, 0].astype(jnp.int32)
+        for block in cots
+        for start in range(0, block.shape[0], each_rows)
+    ]
     after = n_line * side
     half = width // 2
     hidden, sent, kept_back, kept_weight = call(
@@ -255,20 +289,20 @@
             ((half, width), F32, True),
         ],
         [
-            ((n_col, blocks * side, width), BF16),
             ((n_col, side, width), F32),
             ((n_col * side, width), BF16),
             ((n_col * side, width), BF16),
             ((n_col, side, width), BF16),
             ((2, half, width), F32),
             ((n_row, side, width), F32),
+            ((n_col, blocks), jnp.int32),
         ],
-        all_ints,
-        weight,
-        bias[None],
+        [row, col, *ints, *everyones],
+        near(weight),
+        far(bias[None]),
         own_tiles,
-        *products,
-        *cots,
+        near(products),
+        *map(near, cots),
     )
     came = exchange(sent, "row", 1)
     mine, *parts = call(
@@ -276,11 +310,8 @@
         "chip_sums",
         [((side, width), F32, True)] + [((side + half + PAD, width), BF16, True)] * (n_line - 1),
         [],
-        None,
-        kept_back,
-        kept_weight,
-        sent,
-        came,
+        [],
+        *map(near, (kept_back, kept_weight, sent, came)),
     )
     line = [parts[0]] + [exchange(part, "row", 2 * m) for m, part in enumerate(parts, 1)]
     other = [exchange(block, "row", 1) for block in line]
@@ -290,10 +321,8 @@
         "line_sums",
         [((side, width), BF16, False), ((width, width), F32, False), ((1, width), F32, False)],
         [],
-        me_row % 2,
-        mine,
-        *line,
-        *other,
+        [row],
+        *map(near, (mine, *line, *other)),
     )
     return (hidden[None], grad_weight, grad_bias[0], grad_features[None])
 

time: 49.7 us -> 47.5 us (0.956)
  blocking collectives: 0 us -> 11.3 us
  waiting for transfers between devices: 20.8 us -> 14.7 us
  starting transfers between devices: 18.3 us -> 14.1 us
  local copies, waits for them, and re-layouts: 3.65 us -> 0.01 us
  Pallas kernels: 4.54 us -> 5.18 us
    all_gather x0 -> x1, blocking collectives: none -> 11.3 us  [on_device(): products = lax.all_gather(product, 'col')]
    ppermute x21 -> x17, waiting for transfers between devices: 20.8 us -> 14.7 us  [exchange(): return lax.ppermute(value, axis, [(i, i ^ mask) for i in range(size)])]
    ppermute x21 -> x17, starting transfers between devices: 18.3 us -> 14.1 us  [exchange(): return lax.ppermute(value, axis, [(i, i ^ mask) for i in range(size)])]
    unnamed x18 -> x6, local copies, waits for them, and re-layouts: 2.83 us -> 0.01 us
    concatenate x2 -> x0, local copies, waits for them, and re-layouts: 0.82 us -> none  [the longest x1 0.75 us: on_device(): jnp.concatenate([me_row, me_col, tile_count[0], tile_rows[0, 0], tile_col...]
    pallas_call x5 -> x6, Pallas kernels: 4.54 us -> 5.18 us  [call(): pl.pallas_call(kernel, name=name, out_shape=[pltpu.VMEM(shape, dtype) if...]
  transfers between devices with their start and end apart: 21 -> 17, of which waited for: 10 -> 7; matrix products, arithmetic and copies ran while one was open for 3% -> 0% of each run, Pallas kernels for 3% -> 4%
where the time goes in v3:
time: 47.5 us; the launch traced here: 47.1 us
  waiting for transfers between devices  14.7 us (31%)
  starting transfers between devices  14.1 us (30%)
  blocking collectives  11.3 us (24%)
  Pallas kernels  5.18 us (11%)
  between operations  1.4 us (3%)
    ppermute x17, waiting for transfers between devices, exchange(): return lax.ppermute(value, axis, [(i, i ^ mask) for i in range(size)])  14.7 us
    ppermute x17, starting transfers between devices, exchange(): return lax.ppermute(value, axis, [(i, i ^ mask) for i in range(size)])  14.1 us
    all_gather x1, blocking collectives, on_device(): products = lax.all_gather(product, 'col')  11.3 us
    pallas_call x6, Pallas kernels, call(): pl.pallas_call(kernel, name=name, out_shape=[pltpu.VMEM(shape, dtype) if...  5.18 us
  transfers between devices with their start and end apart: 17, of which 7 were waited for; matrix products, arithmetic and copies ran while one was open for 0% of the time, Pallas kernels for 4%

profile of v3, /device:TPU:0, one launch (start us, length us, event | category | flops | bytes accessed | tf_op | source)
XLA Modules:
  0.0 47.1 jit_solution(15302171134239362751)
XLA Ops:
  0.6 5.1 %collective-permute-start.2 = (bf16[128,256]{1,0:T(8,128)(2,1)}, bf16[128,256]{1,0:T(8,128)(2,1)S(1)}, u32[]{:S(2)}, u32[]{:S(2)}) collective-permute-start(bf16[128,256]{1,0:T(8,128)(2,1)} %bitcast.18), channel_id=1, source_target_pairs={{0,24},{4,28},{8,16},{12,20},{16,8},{20,12},{24,0},{28,4},{1,25},{... | collective-permute-start | bytes 196616 | tf_op jit(solution)/shard_map/ppermute | solution.py:28
  5.7 0.6 %collective-permute-start = (bf16[128,256]{1,0:T(8,128)(2,1)}, bf16[128,256]{1,0:T(8,128)(2,1)S(1)}, u32[]{:S(2)}, u32[]{:S(2)}) collective-permute-start(bf16[128,256]{1,0:T(8,128)(2,1)} %bitcast.20), channel_id=1, source_target_pairs={{0,8},{4,12},{8,0},{12,4},{16,24},{20,28},{24,16},{28,20},{1,9},{5... | collective-permute-start | bytes 196616 | tf_op jit(solution)/shard_map/ppermute | solution.py:28
  6.4 1.0 %masked_cotangent.1.refs_0_.refs_13_ = bf16[144,256]{1,0:T(8,128)(2,1)S(1)} custom-call(s32[3]{0:T(128)} %bitcast.24, s32[1,128]{1,0:T(1,128)} %mask.1, bf16[128,256]{1,0:T(8,128)(2,1)} %bitcast.23), custom_call_target="tpu_custom_call" | custom-call | tf_op jit(solution)/shard_map/masked_cotangent/pallas_call | solution.py:194
  7.4 1.7 %collective-permute-start.3 = (bf16[144,256]{1,0:T(8,128)(2,1)S(1)}, bf16[144,256]{1,0:T(8,128)(2,1)S(1)}, u32[]{:S(2)}, u32[]{:S(2)}) collective-permute-start(bf16[144,256]{1,0:T(8,128)(2,1)S(1)} %masked_cotangent.1.refs_0_.refs_13_), channel_id=1, source_target_pairs={{0,1},{1,0},{2,3},{3,2},{4,5},{5,4},{6,7},{7,6},{8,9},{9,8},{10,11... | collective-permute-start | bytes 221192 | tf_op jit(solution)/shard_map/ppermute | solution.py:28
  9.8 1.8 %collective-permute-done.1.refs_4_ = bf16[128,256]{1,0:T(8,128)(2,1)S(1)} collective-permute-done((bf16[128,256]{1,0:T(8,128)(2,1)}, bf16[128,256]{1,0:T(8,128)(2,1)S(1)}, u32[]{:S(2)}, u32[]{:S(2)}) %collective-permute-start.1) | collective-permute-done | bytes 65568 | tf_op jit(solution)/shard_map/ppermute | solution.py:28
  11.6 0.5 %collective-permute-start.6 = (bf16[128,256]{1,0:T(8,128)(2,1)S(1)}, bf16[128,256]{1,0:T(8,128)(2,1)S(1)}, u32[]{:S(2)}, u32[]{:S(2)}) collective-permute-start(bf16[128,256]{1,0:T(8,128)(2,1)S(1)} %collective-permute-done.refs_2_), channel_id=1, source_target_pairs={{0,4},{4,0},{8,12},{12,8},{16,20},{20,16},{24,28},{28,24},{1,5},{5... | collective-permute-start | bytes 196616 | tf_op jit(solution)/shard_map/ppermute | solution.py:28
  12.2 0.4 collective-permute-start.8
  12.6 0.1 convert_reduce_fusion.3.refs_5_
  12.7 1.6 %collective-permute-start.4 = (bf16[288,256]{1,0:T(8,128)(2,1)S(1)}, bf16[288,256]{1,0:T(8,128)(2,1)S(1)}, u32[]{:S(2)}, u32[]{:S(2)}) collective-permute-start(bf16[288,256]{1,0:T(8,128)(2,1)S(1)} %cotangents_so_far.1), channel_id=1, source_target_pairs={{0,2},{1,3},{2,0},{3,1},{4,6},{5,7},{6,4},{7,5},{8,10},{9,11},{10,... | collective-permute-start | bytes 442376 | tf_op jit(solution)/shard_map/ppermute | solution.py:28
  14.3 0.1 convert_reduce_fusion.2.refs_6_
  14.5 0.9 %tile_products.1 = bf16[384,256]{1,0:T(8,128)(2,1)S(1)} custom-call(s32[1]{0:T(128)} %bitcast.row.refs_0_, s32[1]{0:T(128)} %bitcast.13.count, s32[3]{0:T(128)} %bitcast.25, s32[3]{0:T(128)} %bitcast.27, bf16[3,128,128]{2,1,0:T(8,128)(2,1)S(1)} %bitcast.16, bf16[128,256]{1,0:T(8,128)(2,1)S(1)} %bitcast.22, ...), custom_call_target="tpu_custom_call" | custom-call | tf_op jit(solution)/shard_map/tile_products/pallas_call | solution.py:194
  15.4 11.3 %all-gather = bf16[1536,256]{1,0:T(8,128)(2,1)S(1)} all-gather(bf16[384,256]{1,0:T(8,128)(2,1)S(1)} %tile_products.1), channel_id=2, replica_groups=mesh['row'=8,'col'=4] {'col'}, dimensions={0}, use_global_device_ids=true | all-gather | bytes 983040 | tf_op jit(solution)/shard_map/all_gather | solution.py:273
  26.7 0.1 convert_reduce_fusion
  26.8 2.4 %dense_layer.1 = (bf16[128,256]{1,0:T(8,128)(2,1)}, bf16[656,256]{1,0:T(8,128)(2,1)S(1)}, f32[512,256]{1,0:T(8,128)S(1)}, f32[128,256]{1,0:T(8,128)S(1)}) custom-call(s32[1]{0:T(128)} %bitcast.row.refs_0_, s32[1]{0:T(128)} %bitcast.1.refs_1_, s32[1]{0:T(128)} %bitcast.14.refs_2_, s32[3]{0:T(128)} %bitcast.26, s32[3]{0:T(128)} %bitcast.28, ...), custom_call_target="tpu_custom_call" | custom-call | tf_op jit(solution)/shard_map/dense_layer/pallas_call | solution.py:194
  29.2 1.6 %collective-permute-done.9.came = bf16[656,256]{1,0:T(8,128)(2,1)S(1)} collective-permute-done((bf16[656,256]{1,0:T(8,128)(2,1)S(1)}, bf16[656,256]{1,0:T(8,128)(2,1)S(1)}, u32[]{:S(2)}, u32[]{:S(2)}) %collective-permute-start.9) | collective-permute-done | bytes 335904 | tf_op jit(solution)/shard_map/ppermute | solution.py:28
  30.9 1.6 %collective-permute-start.11 = (bf16[272,256]{1,0:T(8,128)(2,1)S(1)}, bf16[272,256]{1,0:T(8,128)(2,1)S(1)}, u32[]{:S(2)}, u32[]{:S(2)}) collective-permute-start(bf16[272,256]{1,0:T(8,128)(2,1)S(1)} %get-tuple-element.31), channel_id=1, source_target_pairs={{0,16},{4,20},{8,24},{12,28},{16,0},{20,4},{24,8},{28,12},{1,17},{... | collective-permute-start | bytes 417800 | tf_op jit(solution)/shard_map/ppermute | solution.py:28
  32.5 1.9 %collective-permute-start.12 = (bf16[272,256]{1,0:T(8,128)(2,1)S(1)}, bf16[272,256]{1,0:T(8,128)(2,1)S(1)}, u32[]{:S(2)}, u32[]{:S(2)}) collective-permute-start(bf16[272,256]{1,0:T(8,128)(2,1)S(1)} %get-tuple-element.32), channel_id=1, source_target_pairs={{0,24},{4,28},{8,16},{12,20},{16,8},{20,12},{24,0},{28,4},{1,25},{... | collective-permute-start | bytes 417800 | tf_op jit(solution)/shard_map/ppermute | solution.py:28
  34.5 9.7 %collective-permute-done.11.refs_2_ = bf16[272,256]{1,0:T(8,128)(2,1)S(1)} collective-permute-done((bf16[272,256]{1,0:T(8,128)(2,1)S(1)}, bf16[272,256]{1,0:T(8,128)(2,1)S(1)}, u32[]{:S(2)}, u32[]{:S(2)}) %collective-permute-start.11) | collective-permute-done | bytes 139296 | tf_op jit(solution)/shard_map/ppermute | solution.py:28
  44.1 0.5 %collective-permute-start.16 = (bf16[272,256]{1,0:T(8,128)(2,1)S(1)}, bf16[272,256]{1,0:T(8,128)(2,1)S(1)}, u32[]{:S(2)}, u32[]{:S(2)}) collective-permute-start(bf16[272,256]{1,0:T(8,128)(2,1)S(1)} %collective-permute-done.12.refs_3_), channel_id=1, source_target_pairs={{0,4},{4,0},{8,12},{12,8},{16,20},{20,16},{24,28},{28,24},{1,5},{5... | collective-permute-start | bytes 417800 | tf_op jit(solution)/shard_map/ppermute | solution.py:28
  44.7 0.3 collective-permute-done.10.refs_1_
  44.9 0.6 %collective-permute-done.15.refs_6_ = bf16[272,256]{1,0:T(8,128)(2,1)S(1)} collective-permute-done((bf16[272,256]{1,0:T(8,128)(2,1)S(1)}, bf16[272,256]{1,0:T(8,128)(2,1)S(1)}, u32[]{:S(2)}, u32[]{:S(2)}) %collective-permute-start.15) | collective-permute-done | bytes 139296 | tf_op jit(solution)/shard_map/ppermute | solution.py:28
  45.5 0.2 collective-permute-done.16.refs_7_
  45.7 0.6 %collective-permute-done.14.refs_5_ = bf16[272,256]{1,0:T(8,128)(2,1)S(1)} collective-permute-done((bf16[272,256]{1,0:T(8,128)(2,1)S(1)}, bf16[272,256]{1,0:T(8,128)(2,1)S(1)}, u32[]{:S(2)}, u32[]{:S(2)}) %collective-permute-start.14) | collective-permute-done | bytes 139296 | tf_op jit(solution)/shard_map/ppermute | solution.py:28
  46.3 0.8 %line_sums.1 = (bf16[128,256]{1,0:T(8,128)(2,1)}, f32[256,256]{1,0:T(8,128)}, f32[1,256]{1,0:T(1,128)}) custom-call(s32[1]{0:T(128)} %bitcast.row.refs_0_, f32[128,256]{1,0:T(8,128)S(1)} %get-tuple-element.29.mine, bf16[272,256]{1,0:T(8,128)(2,1)S(1)} %get-tuple-element.30.refs_0_, bf16[272,256]{1,0:T(8,128)(2,1)S(1)} %collective-permute-done.10.refs_1_, ...), custom_call_target="tpu_custom_call" | custom-call | tf_op jit(solution)/shard_map/line_sums/pallas_call | solution.py:194
  (26 shorter events, 0.3 us)
Async XLA Ops:
  0.6 9.2 %collective-permute-start.2 = (bf16[128,256]{1,0:T(8,128)(2,1)}, bf16[128,256]{1,0:T(8,128)(2,1)S(1)}, u32[]{:S(2)}, u32[]{:S(2)}) collective-permute-start(bf16[128,256]{1,0:T(8,128)(2,1)} %bitcast.18), channel_id=1, source_target_pairs={{0,24},{4,28},{8,16},{12,20},{16,8},{20,12},{24,0},{28,4},{1,25},{... | collective-permute-start | bytes 196616 | tf_op jit(solution)/shard_map/ppermute | solution.py:28
  5.7 5.8 %collective-permute-start.1 = (bf16[128,256]{1,0:T(8,128)(2,1)}, bf16[128,256]{1,0:T(8,128)(2,1)S(1)}, u32[]{:S(2)}, u32[]{:S(2)}) collective-permute-start(bf16[128,256]{1,0:T(8,128)(2,1)} %bitcast.19), channel_id=1, source_target_pairs={{0,16},{4,20},{8,24},{12,28},{16,0},{20,4},{24,8},{28,12},{1,17},{... | collective-permute-start | bytes 196616 | tf_op jit(solution)/shard_map/ppermute | solution.py:28
  5.7 5.8 %collective-permute-start = (bf16[128,256]{1,0:T(8,128)(2,1)}, bf16[128,256]{1,0:T(8,128)(2,1)S(1)}, u32[]{:S(2)}, u32[]{:S(2)}) collective-permute-start(bf16[128,256]{1,0:T(8,128)(2,1)} %bitcast.20), channel_id=1, source_target_pairs={{0,8},{4,12},{8,0},{12,4},{16,24},{20,28},{24,16},{28,20},{1,9},{5... | collective-permute-start | bytes 196616 | tf_op jit(solution)/shard_map/ppermute | solution.py:28
  6.4 5.2 %copy-start.2 = (bf16[1,128,256]{2,1,0:T(8,128)(2,1)S(1)}, bf16[1,128,256]{2,1,0:T(8,128)(2,1)}, u32[]{:S(2)}) copy-start(bf16[1,128,256]{2,1,0:T(8,128)(2,1)} %param.9) | copy-start | bytes 196612
  7.4 5.3 %collective-permute-start.3 = (bf16[144,256]{1,0:T(8,128)(2,1)S(1)}, bf16[144,256]{1,0:T(8,128)(2,1)S(1)}, u32[]{:S(2)}, u32[]{:S(2)}) collective-permute-start(bf16[144,256]{1,0:T(8,128)(2,1)S(1)} %masked_cotangent.1.refs_0_.refs_13_), channel_id=1, source_target_pairs={{0,1},{1,0},{2,3},{3,2},{4,5},{5,4},{6,7},{7,6},{8,9},{9,8},{10,11... | collective-permute-start | bytes 221192 | tf_op jit(solution)/shard_map/ppermute | solution.py:28
  11.6 2.9 %collective-permute-start.5 = (bf16[128,256]{1,0:T(8,128)(2,1)S(1)}, bf16[128,256]{1,0:T(8,128)(2,1)S(1)}, u32[]{:S(2)}, u32[]{:S(2)}) collective-permute-start(bf16[128,256]{1,0:T(8,128)(2,1)S(1)} %bitcast.21), channel_id=1, source_target_pairs={{0,4},{4,0},{8,12},{12,8},{16,20},{20,16},{24,28},{28,24},{1,5},{5... | collective-permute-start | bytes 196616 | tf_op jit(solution)/shard_map/ppermute | solution.py:28
  11.6 2.9 %collective-permute-start.6 = (bf16[128,256]{1,0:T(8,128)(2,1)S(1)}, bf16[128,256]{1,0:T(8,128)(2,1)S(1)}, u32[]{:S(2)}, u32[]{:S(2)}) collective-permute-start(bf16[128,256]{1,0:T(8,128)(2,1)S(1)} %collective-permute-done.refs_2_), channel_id=1, source_target_pairs={{0,4},{4,0},{8,12},{12,8},{16,20},{20,16},{24,28},{28,24},{1,5},{5... | collective-permute-start | bytes 196616 | tf_op jit(solution)/shard_map/ppermute | solution.py:28
  12.1 2.4 %collective-permute-start.7 = (bf16[128,256]{1,0:T(8,128)(2,1)S(1)}, bf16[128,256]{1,0:T(8,128)(2,1)S(1)}, u32[]{:S(2)}, u32[]{:S(2)}) collective-permute-start(bf16[128,256]{1,0:T(8,128)(2,1)S(1)} %collective-permute-done.1.refs_4_), channel_id=1, source_target_pairs={{0,4},{4,0},{8,12},{12,8},{16,20},{20,16},{24,28},{28,24},{1,5},{5... | collective-permute-start | bytes 196616 | tf_op jit(solution)/shard_map/ppermute | solution.py:28
  12.2 2.3 %collective-permute-start.8 = (bf16[128,256]{1,0:T(8,128)(2,1)S(1)}, bf16[128,256]{1,0:T(8,128)(2,1)S(1)}, u32[]{:S(2)}, u32[]{:S(2)}) collective-permute-start(bf16[128,256]{1,0:T(8,128)(2,1)S(1)} %collective-permute-done.2.refs_6_), channel_id=1, source_target_pairs={{0,4},{4,0},{8,12},{12,8},{16,20},{20,16},{24,28},{28,24},{1,5},{5... | collective-permute-start | bytes 196616 | tf_op jit(solution)/shard_map/ppermute | solution.py:28
  12.7 1.8 %copy-start = (bf16[1,1,3,128,128]{4,3,2,1,0:T(8,128)(2,1)S(1)}, bf16[1,1,3,128,128]{4,3,2,1,0:T(8,128)(2,1)}, u32[]{:S(2)}) copy-start(bf16[1,1,3,128,128]{4,3,2,1,0:T(8,128)(2,1)} %param.10) | copy-start | bytes 294916
  12.7 13.9 %collective-permute-start.4 = (bf16[288,256]{1,0:T(8,128)(2,1)S(1)}, bf16[288,256]{1,0:T(8,128)(2,1)S(1)}, u32[]{:S(2)}, u32[]{:S(2)}) collective-permute-start(bf16[288,256]{1,0:T(8,128)(2,1)S(1)} %cotangents_so_far.1), channel_id=1, source_target_pairs={{0,2},{1,3},{2,0},{3,1},{4,6},{5,7},{6,4},{7,5},{8,10},{9,11},{10,... | collective-permute-start | bytes 442376 | tf_op jit(solution)/shard_map/ppermute | solution.py:28
  15.4 11.4 %copy-start.1 = (bf16[256,256]{1,0:T(8,128)(2,1)S(1)}, bf16[256,256]{1,0:T(8,128)(2,1)}, u32[]{:S(2)}) copy-start(bf16[256,256]{1,0:T(8,128)(2,1)} %refs_9_.1) | copy-start | bytes 393220
  29.2 1.6 %collective-permute-start.9 = (bf16[656,256]{1,0:T(8,128)(2,1)S(1)}, bf16[656,256]{1,0:T(8,128)(2,1)S(1)}, u32[]{:S(2)}, u32[]{:S(2)}) collective-permute-start(bf16[656,256]{1,0:T(8,128)(2,1)S(1)} %get-tuple-element.28.own_sent), channel_id=1, source_target_pairs={{0,4},{4,0},{8,12},{12,8},{16,20},{20,16},{24,28},{28,24},{1,5},{5... | collective-permute-start | bytes 1007624 | tf_op jit(solution)/shard_map/ppermute | solution.py:28
  30.9 13.2 %collective-permute-start.11 = (bf16[272,256]{1,0:T(8,128)(2,1)S(1)}, bf16[272,256]{1,0:T(8,128)(2,1)S(1)}, u32[]{:S(2)}, u32[]{:S(2)}) collective-permute-start(bf16[272,256]{1,0:T(8,128)(2,1)S(1)} %get-tuple-element.31), channel_id=1, source_target_pairs={{0,16},{4,20},{8,24},{12,28},{16,0},{20,4},{24,8},{28,12},{1,17},{... | collective-permute-start | bytes 417800 | tf_op jit(solution)/shard_map/ppermute | solution.py:28
  32.5 11.6 %collective-permute-start.12 = (bf16[272,256]{1,0:T(8,128)(2,1)S(1)}, bf16[272,256]{1,0:T(8,128)(2,1)S(1)}, u32[]{:S(2)}, u32[]{:S(2)}) collective-permute-start(bf16[272,256]{1,0:T(8,128)(2,1)S(1)} %get-tuple-element.32), channel_id=1, source_target_pairs={{0,24},{4,28},{8,16},{12,20},{16,8},{20,12},{24,0},{28,4},{1,25},{... | collective-permute-start | bytes 417800 | tf_op jit(solution)/shard_map/ppermute | solution.py:28
  34.4 10.6 %collective-permute-start.10 = (bf16[272,256]{1,0:T(8,128)(2,1)S(1)}, bf16[272,256]{1,0:T(8,128)(2,1)S(1)}, u32[]{:S(2)}, u32[]{:S(2)}) collective-permute-start(bf16[272,256]{1,0:T(8,128)(2,1)S(1)} %get-tuple-element.30.refs_0_), channel_id=1, source_target_pairs={{0,8},{4,12},{8,0},{12,4},{16,24},{20,28},{24,16},{28,20},{1,9},{5... | collective-permute-start | bytes 417800 | tf_op jit(solution)/shard_map/ppermute | solution.py:28
  34.5 10.5 %collective-permute-start.13 = (bf16[272,256]{1,0:T(8,128)(2,1)S(1)}, bf16[272,256]{1,0:T(8,128)(2,1)S(1)}, u32[]{:S(2)}, u32[]{:S(2)}) collective-permute-start(bf16[272,256]{1,0:T(8,128)(2,1)S(1)} %get-tuple-element.30.refs_0_), channel_id=1, source_target_pairs={{0,4},{4,0},{8,12},{12,8},{16,20},{20,16},{24,28},{28,24},{1,5},{5... | collective-permute-start | bytes 417800 | tf_op jit(solution)/shard_map/ppermute | solution.py:28
  44.1 1.4 %collective-permute-start.15 = (bf16[272,256]{1,0:T(8,128)(2,1)S(1)}, bf16[272,256]{1,0:T(8,128)(2,1)S(1)}, u32[]{:S(2)}, u32[]{:S(2)}) collective-permute-start(bf16[272,256]{1,0:T(8,128)(2,1)S(1)} %collective-permute-done.11.refs_2_), channel_id=1, source_target_pairs={{0,4},{4,0},{8,12},{12,8},{16,20},{20,16},{24,28},{28,24},{1,5},{5... | collective-permute-start | bytes 417800 | tf_op jit(solution)/shard_map/ppermute | solution.py:28
  44.1 1.6 %collective-permute-start.16 = (bf16[272,256]{1,0:T(8,128)(2,1)S(1)}, bf16[272,256]{1,0:T(8,128)(2,1)S(1)}, u32[]{:S(2)}, u32[]{:S(2)}) collective-permute-start(bf16[272,256]{1,0:T(8,128)(2,1)S(1)} %collective-permute-done.12.refs_3_), channel_id=1, source_target_pairs={{0,4},{4,0},{8,12},{12,8},{16,20},{20,16},{24,28},{28,24},{1,5},{5... | collective-permute-start | bytes 417800 | tf_op jit(solution)/shard_map/ppermute | solution.py:28
  44.9 1.4 %collective-permute-start.14 = (bf16[272,256]{1,0:T(8,128)(2,1)S(1)}, bf16[272,256]{1,0:T(8,128)(2,1)S(1)}, u32[]{:S(2)}, u32[]{:S(2)}) collective-permute-start(bf16[272,256]{1,0:T(8,128)(2,1)S(1)} %collective-permute-done.10.refs_1_), channel_id=1, source_target_pairs={{0,4},{4,0},{8,12},{12,8},{16,20},{20,16},{24,28},{28,24},{1,5},{5... | collective-permute-start | bytes 417800 | tf_op jit(solution)/shard_map/ppermute | solution.py:28

commit v4 on v3

--- a/solution.py
+++ b/solution.py
@@ -48,7 +48,13 @@
     return rows[0:1] + rows[1:2]
 
 
-def cotangent_kernel(places, mask, cotangent, out):
+def cotangent_kernel(blocks, tile_rows, tile_cols, count, mask, cotangent, bias, out, own_bias, ints):
+    own_bias[...] = bias[...]
+    slots = tile_rows.shape[0]
+    ints[2 * slots] = jnp.max(count[...])
+    for s in range(slots):
+        ints[s] = tile_rows[s]
+        ints[slots + s] = tile_cols[s]
     side, width = cotangent.shape
     shape = (side, side)
     diagonal = lax.broadcasted_iota(jnp.int32, shape, 0) == lax.broadcasted_iota(jnp.int32, shape, 1)
@@ -57,8 +63,8 @@
     rows = out.shape[0] - side
     index = lax.broadcasted_iota(jnp.int32, (rows, width), 0)
     block = jnp.zeros((rows, width), jnp.int32)
-    for p in range(places.shape[0]):
-        block = jnp.where(index == p, places[p], block)
+    for p in range(blocks):
+        block = jnp.where(index == p, tile_rows[p] if blocks == slots else p, block)
     out[side:] = block.astype(F32).astype(BF16)
 
 
@@ -69,16 +75,16 @@
         start += block.shape[0]
 
 
-def forward_kernel(slots, n_col, blocks, row, count, tile_rows, tile_cols, tiles, *refs):
+def forward_kernel(slots, n_col, blocks, ints, tiles, *refs):
     n_row = len(refs) - 3
     sources, out, held, total = refs[:n_row], refs[n_row], refs[n_row + 1], refs[n_row + 2]
     side = tiles.shape[-1]
     for q in range(n_row):
         held[q] = sources[q][...]
-    me_row, live = row[0], count[0]
+    me_row, live = lax.axis_index("row"), ints[2 * slots]
 
     def product(s):
-        taken = held[tile_cols[s] ^ me_row]
+        taken = held[ints[slots + s] ^ me_row]
         value = jnp.dot(tiles[s], taken, preferred_element_type=F32)
         return jnp.where(s < live, value, 0.0)
 
@@ -89,7 +95,7 @@
     total[...] = jnp.zeros_like(total)
 
     def add(s):
-        total[tile_rows[s]] += product(s)
+        total[ints[s]] += product(s)
 
     each(slots, add)
     for t in range(n_col):
@@ -97,20 +103,26 @@
 
 
 def middle_kernel(slots, n_row, n_col, blocks, *refs):
-    (row, col, count, tile_rows, tile_cols), refs = refs[:5], refs[5:]
-    places, refs = refs[:n_col], refs[n_col:]
+    ints, refs = refs[0], refs[1:]
     (weight, bias, tiles, products), refs = refs[:4], refs[4:]
     steps = n_col.bit_length()
     cots, refs = refs[:steps], refs[steps:]
     hidden, sent, kept, kept_weight, total, agg, grads, grad_agg, weights, back, target = refs
     side = tiles.shape[-1]
     half = weight.shape[0] // 2
-    me_row, me_col, live = row[0], col[0], count[0]
+    me_row, me_col, live = lax.axis_index("row"), lax.axis_index("col"), ints[2 * slots]
+    each_rows = cots[0].shape[0]
+
+    def cotangent(q, start, stop):
+        step = q.bit_length()
+        first = (q - (1 << step >> 1)) * each_rows
+        return cots[step][first + start : first + stop]
+
+    for q in range(n_col):
+        places = cotangent(q, side, each_rows)[:, 0:128].astype(F32).astype(jnp.int32)
+        for p in range(blocks):
+            target[q, p] = jnp.max(places[p : p + 1])
     total[...] = jnp.zeros_like(total)
-
-    for q in range(n_col):
-        for p in range(blocks):
-            target[q, p] = places[q][p]
 
     def add(i):
         c, p = i // blocks, i % blocks
@@ -128,10 +140,7 @@
         if q == 0:
             hidden[...] = (pre_act * sigma).astype(BF16)
         slope = sigma * (1.0 + pre_act * (1.0 - sigma))
-        step = q.bit_length()
-        start = (q - (1 << step >> 1)) * cots[0].shape[0]
-        cotangent = cots[step][start : start + side]
-        grad_pre = (cotangent.astype(F32) * slope).astype(BF16)
+        grad_pre = (cotangent(q, 0, side).astype(F32) * slope).astype(BF16)
         grads[rows, :] = grad_pre
         grad_agg[t] = lax.dot_general(
             grad_pre, weight[...], COLS_COLS, preferred_element_type=F32
@@ -140,9 +149,9 @@
 
     def put(s):
         value = lax.dot_general(
-            tiles[s], grad_agg[tile_rows[s]], ROWS_ROWS, preferred_element_type=F32
+            tiles[s], grad_agg[ints[s]], ROWS_ROWS, preferred_element_type=F32
         )
-        back[tile_cols[s] ^ me_row] += jnp.where(s < live, value, 0.0)
+        back[ints[slots + s] ^ me_row] += jnp.where(s < live, value, 0.0)
 
     each(slots, put)
     for m in range(n_row // 2):
@@ -173,8 +182,9 @@
         out[side + half : side + half + PAD] = column_sum
 
 
-def line_kernel(scale, row, mine, *refs):
-    blocks, (grad_features, grad_weight, grad_bias) = refs[:-3], refs[-3:]
+def line_kernel(scale, own_hidden, mine, *refs):
+    blocks, (hidden, grad_features, grad_weight, grad_bias) = refs[:-4], refs[-4:]
+    hidden[...] = own_hidden[...]
     side, half = mine.shape[0], grad_weight.shape[0] // 2
     own, other = blocks[: len(blocks) // 2], blocks[len(blocks) // 2 :]
     total = mine[...]
@@ -182,7 +192,7 @@
         total = total + block[0:side].astype(F32)
     grad_features[...] = total.astype(BF16)
     for shift, group in enumerate((own, other)):
-        start = pl.multiple_of((row[0] % 2 ^ shift) * half, half)
+        start = pl.multiple_of((lax.axis_index("row") % 2 ^ shift) * half, half)
         grad_weight[pl.ds(start, half), :] = scale * tree_sum(
             b[side : side + half].astype(F32) for b in group
         )
@@ -191,19 +201,21 @@
 
 def call(kernel, name, outs, scratch, ints, *arrays):
     need = sum(math.prod(shape) * jnp.dtype(dtype).itemsize for shape, dtype in scratch)
+
+    def space(dtype):
+        return pltpu.SMEM if dtype == jnp.int32 else pltpu.VMEM
+
     return pl.pallas_call(
         kernel,
         name=name,
         out_shape=[
-            pltpu.VMEM(shape, dtype) if stays else jax.ShapeDtypeStruct(shape, dtype)
+            space(dtype)(shape, dtype) if stays else jax.ShapeDtypeStruct(shape, dtype)
             for shape, dtype, stays in outs
         ],
         in_specs=[pl.BlockSpec(memory_space=pltpu.SMEM)] * len(ints)
         + [pl.BlockSpec(memory_space=pltpu.VMEM)] * len(arrays),
-        out_specs=[pl.BlockSpec(memory_space=pltpu.VMEM)] * len(outs),
-        scratch_shapes=[
-            (pltpu.SMEM if dtype == jnp.int32 else pltpu.VMEM)(shape, dtype) for shape, dtype in scratch
-        ],
+        out_specs=[pl.BlockSpec(memory_space=space(dtype)) for _, dtype, _ in outs],
+        scratch_shapes=[space(dtype)(shape, dtype) for shape, dtype in scratch],
         compiler_params=pltpu.CompilerParams(vmem_limit_bytes=need + 8 * 1024 * 1024),
     )(*ints, *arrays)
 
@@ -227,26 +239,22 @@
     n_line = n_row // 2
     blocks = min(slots, n_col)
     own_tiles = near(tiles[0, 0])
-    row = lax.axis_index("row").astype(jnp.int32)[None]
-    col = lax.axis_index("col").astype(jnp.int32)[None]
-    ints = (tile_count[0], far(tile_rows[0, 0]), far(tile_cols[0, 0]))
 
     own = features[0]
     along = [own] + [exchange(own, "row", 2 * m) for m in range(1, n_line)]
 
-    if blocks == slots:
-        places = tile_rows[0, 0]
-    else:
-        places = jnp.arange(blocks, dtype=jnp.int32)
-    (with_places,) = call(
-        cotangent_kernel,
+    with_places, own_bias, ints = call(
+        functools.partial(cotangent_kernel, blocks),
         "masked_cotangent",
-        [((side + blocks + -blocks % PAD, width), BF16, True)],
-        [],
-        [far(places)],
+        [((side + blocks + -blocks % PAD, width), BF16, True), ((1, width), F32, True), ((2 * slots + 1,), jnp.int32, True)],
+        [],
+        [far(tile_rows[0, 0]), far(tile_cols[0, 0])],
+        tile_count,
         far(label_mask),
         far(cotangent[0]),
-    )
+        far(bias[None]),
+    )
+    ints = pltpu.with_memory_space_constraint(ints, pltpu.SMEM)
     cots, reach = [with_places], 1
     while reach < n_col:
         (held,) = call(
@@ -259,31 +267,24 @@
         ) if reach > 1 else cots
         cots, reach = cots + [exchange(held, "col", reach)], 2 * reach
 
-    along, cots[0] = lax.optimization_barrier((along, cots[0]))
     sources = [part for block in along for part in (block, exchange(block, "row", 1))]
     (product,) = call(
         functools.partial(forward_kernel, slots, n_col, blocks),
         "tile_products",
         [((blocks * side, width), BF16, True)],
         [((n_row, side, width), BF16), ((n_col, side, width), F32)],
-        [row, *ints],
+        [ints],
         own_tiles,
         *map(near, sources),
     )
     products = lax.all_gather(product, "col")
-    each_rows = with_places.shape[0]
-    everyones = [
-        block[start + side : start + side + blocks, 0].astype(jnp.int32)
-        for block in cots
-        for start in range(0, block.shape[0], each_rows)
-    ]
     after = n_line * side
     half = width // 2
     hidden, sent, kept_back, kept_weight = call(
         functools.partial(middle_kernel, slots, n_row, n_col, blocks),
         "dense_layer",
         [
-            ((side, width), BF16, False),
+            ((side, width), BF16, True),
             ((after + half + PAD, width), BF16, True),
             ((after, width), F32, True),
             ((half, width), F32, True),
@@ -297,9 +298,9 @@
             ((n_row, side, width), F32),
             ((n_col, blocks), jnp.int32),
         ],
-        [row, col, *ints, *everyones],
+        [ints],
         near(weight),
-        far(bias[None]),
+        near(own_bias),
         own_tiles,
         near(products),
         *map(near, cots),
@@ -316,13 +317,18 @@
     line = [parts[0]] + [exchange(part, "row", 2 * m) for m, part in enumerate(parts, 1)]
     other = [exchange(block, "row", 1) for block in line]
     scale = 1.0 / math.sqrt(n_row * n_col * side)
-    grad_features, grad_weight, grad_bias = call(
+    hidden, grad_features, grad_weight, grad_bias = call(
         functools.partial(line_kernel, scale),
         "line_sums",
-        [((side, width), BF16, False), ((width, width), F32, False), ((1, width), F32, False)],
-        [],
-        [row],
-        *map(near, (mine, *line, *other)),
+        [
+            ((side, width), BF16, False),
+            ((side, width), BF16, False),
+            ((width, width), F32, False),
+            ((1, width), F32, False),
+        ],
+        [],
+        [],
+        *map(near, (hidden, mine, *line, *other)),
     )
     return (hidden[None], grad_weight, grad_bias[0], grad_features[None])
 

time: 47.5 us -> 46.1 us (0.971)
  the two profiles are of different devices: /device:TPU:0 before, /device:TPU:17 now
where the time goes in v4:
time: 46.1 us; the launch traced here: 45.9 us
  starting transfers between devices  20.1 us (44%)
  waiting for transfers between devices  11.2 us (24%)
  blocking collectives  9.89 us (21%)
  Pallas kernels  3.37 us (7%)
  between operations  1.38 us (3%)
    ppermute x17, starting transfers between devices, exchange(): return lax.ppermute(value, axis, [(i, i ^ mask) for i in range(size)])  20.1 us
    ppermute x17, waiting for transfers between devices, exchange(): return lax.ppermute(value, axis, [(i, i ^ mask) for i in range(size)])  11.2 us
    all_gather x1, blocking collectives, on_device(): products = lax.all_gather(product, 'col')  9.89 us
    pallas_call x6, Pallas kernels, call(): pl.pallas_call(kernel, name=name, out_shape=[space(dtype)(shape, dtype) i...  3.37 us
  transfers between devices with their start and end apart: 17, of which 5 were waited for; matrix products, arithmetic and copies ran while one was open for 0% of the time, Pallas kernels for 3%

profile of v4, /device:TPU:17, one launch (start us, length us, event | category | flops | bytes accessed | tf_op | source)
XLA Modules:
  0.0 45.9 jit_solution(7203209783473623741)
XLA Ops:
  0.6 0.2 collective-permute-start.5
  0.9 3.2 %collective-permute-start.3 = (bf16[128,256]{1,0:T(8,128)(2,1)}, bf16[128,256]{1,0:T(8,128)(2,1)S(1)}, u32[]{:S(2)}, u32[]{:S(2)}) collective-permute-start(bf16[128,256]{1,0:T(8,128)(2,1)} %bitcast.14), channel_id=1, source_target_pairs={{0,16},{4,20},{8,24},{12,28},{16,0},{20,4},{24,8},{28,12},{1,17},{... | collective-permute-start | bytes 196616 | tf_op jit(solution)/shard_map/ppermute | solution.py:28
  4.7 1.0 %masked_cotangent.1 = (bf16[144,256]{1,0:T(8,128)(2,1)S(1)}, f32[1,256]{1,0:T(1,128)S(1)}, s32[7]{0:T(128)S(4)}) custom-call(s32[3]{0:T(128)} %bitcast.20, s32[3]{0:T(128)} %bitcast.21, s32[1,1]{1,0:T(1,128)S(6)} %copy.13.count, s32[1,128]{1,0:T(1,128)} %mask.1, bf16[128,256]{1,0:T(8,128)(2,1)} %bitcast.18, f32[1,256]{1,0:T(1,128)} %bitcast.19), custom_call_target="tpu_custom_call" | custom-call | tf_op jit(solution)/shard_map/masked_cotangent/pallas_call | solution.py:208
  5.8 1.3 %collective-permute-start.7 = (bf16[144,256]{1,0:T(8,128)(2,1)S(1)}, bf16[144,256]{1,0:T(8,128)(2,1)S(1)}, u32[]{:S(2)}, u32[]{:S(2)}) collective-permute-start(bf16[144,256]{1,0:T(8,128)(2,1)S(1)} %get-tuple-element.21.refs_0_.refs_5_), channel_id=1, source_target_pairs={{0,1},{1,0},{2,3},{3,2},{4,5},{5,4},{6,7},{7,6},{8,9},{9,8},{10,11... | collective-permute-start | bytes 221192 | tf_op jit(solution)/shard_map/ppermute | solution.py:28
  7.0 1.5 %collective-permute-start = (bf16[128,256]{1,0:T(8,128)(2,1)S(1)}, bf16[128,256]{1,0:T(8,128)(2,1)S(1)}, u32[]{:S(2)}, u32[]{:S(2)}) collective-permute-start(bf16[128,256]{1,0:T(8,128)(2,1)S(1)} %bitcast.16), channel_id=1, source_target_pairs={{0,4},{4,0},{8,12},{12,8},{16,20},{20,16},{24,28},{28,24},{1,5},{5... | collective-permute-start | bytes 196616 | tf_op jit(solution)/shard_map/ppermute | solution.py:28
  8.6 0.2 collective-permute-start.6
  8.8 0.7 %collective-permute-start.4 = (bf16[128,256]{1,0:T(8,128)(2,1)S(1)}, bf16[128,256]{1,0:T(8,128)(2,1)S(1)}, u32[]{:S(2)}, u32[]{:S(2)}) collective-permute-start(bf16[128,256]{1,0:T(8,128)(2,1)S(1)} %collective-permute-done.3.refs_4_), channel_id=1, source_target_pairs={{0,4},{4,0},{8,12},{12,8},{16,20},{20,16},{24,28},{28,24},{1,5},{5... | collective-permute-start | bytes 196616 | tf_op jit(solution)/shard_map/ppermute | solution.py:28
  9.5 0.3 collective-permute-start.2
  9.8 1.3 %collective-permute-start.8 = (bf16[288,256]{1,0:T(8,128)(2,1)S(1)}, bf16[288,256]{1,0:T(8,128)(2,1)S(1)}, u32[]{:S(2)}, u32[]{:S(2)}) collective-permute-start(bf16[288,256]{1,0:T(8,128)(2,1)S(1)} %cotangents_so_far.1), channel_id=1, source_target_pairs={{0,2},{1,3},{2,0},{3,1},{4,6},{5,7},{6,4},{7,5},{8,10},{9,11},{10,... | collective-permute-start | bytes 442376 | tf_op jit(solution)/shard_map/ppermute | solution.py:28
  11.2 0.2 tile_products.1
  11.4 9.9 %all-gather = bf16[1536,256]{1,0:T(8,128)(2,1)S(1)} all-gather(bf16[384,256]{1,0:T(8,128)(2,1)S(1)} %tile_products.1), channel_id=2, replica_groups=mesh['row'=8,'col'=4] {'col'}, dimensions={0}, use_global_device_ids=true | all-gather | bytes 983040 | tf_op jit(solution)/shard_map/all_gather | solution.py:280
  21.3 1.2 %dense_layer.1 = (bf16[128,256]{1,0:T(8,128)(2,1)S(1)}, bf16[656,256]{1,0:T(8,128)(2,1)S(1)}, f32[512,256]{1,0:T(8,128)S(1)}, f32[128,256]{1,0:T(8,128)S(1)}) custom-call(s32[7]{0:T(128)S(4)} %get-tuple-element.19.ints.refs_0_, bf16[256,256]{1,0:T(8,128)(2,1)S(1)} %copy-done.1, f32[1,256]{1,0:T(1,128)S(1)} %get-tuple-element.20.refs_2_, ...), custom_call_target="tpu_custom_call" | custom-call | tf_op jit(solution)/shard_map/dense_layer/pallas_call | solution.py:208
  22.6 3.8 %collective-permute-start.9 = (bf16[656,256]{1,0:T(8,128)(2,1)S(1)}, bf16[656,256]{1,0:T(8,128)(2,1)S(1)}, u32[]{:S(2)}, u32[]{:S(2)}) collective-permute-start(bf16[656,256]{1,0:T(8,128)(2,1)S(1)} %get-tuple-element.25.own_sent), channel_id=1, source_target_pairs={{0,4},{4,0},{8,12},{12,8},{16,20},{20,16},{24,28},{28,24},{1,5},{5... | collective-permute-start | bytes 1007624 | tf_op jit(solution)/shard_map/ppermute | solution.py:28
  26.4 1.3 %collective-permute-done.9.came = bf16[656,256]{1,0:T(8,128)(2,1)S(1)} collective-permute-done((bf16[656,256]{1,0:T(8,128)(2,1)S(1)}, bf16[656,256]{1,0:T(8,128)(2,1)S(1)}, u32[]{:S(2)}, u32[]{:S(2)}) %collective-permute-start.9) | collective-permute-done | bytes 335904 | tf_op jit(solution)/shard_map/ppermute | solution.py:28
  27.8 2.9 %collective-permute-start.12 = (bf16[272,256]{1,0:T(8,128)(2,1)S(1)}, bf16[272,256]{1,0:T(8,128)(2,1)S(1)}, u32[]{:S(2)}, u32[]{:S(2)}) collective-permute-start(bf16[272,256]{1,0:T(8,128)(2,1)S(1)} %get-tuple-element.29), channel_id=1, source_target_pairs={{0,24},{4,28},{8,16},{12,20},{16,8},{20,12},{24,0},{28,4},{1,25},{... | collective-permute-start | bytes 417800 | tf_op jit(solution)/shard_map/ppermute | solution.py:28
  30.7 0.6 %collective-permute-start.10 = (bf16[272,256]{1,0:T(8,128)(2,1)S(1)}, bf16[272,256]{1,0:T(8,128)(2,1)S(1)}, u32[]{:S(2)}, u32[]{:S(2)}) collective-permute-start(bf16[272,256]{1,0:T(8,128)(2,1)S(1)} %get-tuple-element.27.refs_0_), channel_id=1, source_target_pairs={{0,8},{4,12},{8,0},{12,4},{16,24},{20,28},{24,16},{28,20},{1,9},{5... | collective-permute-start | bytes 417800 | tf_op jit(solution)/shard_map/ppermute | solution.py:28
  31.3 1.2 %collective-permute-start.13 = (bf16[272,256]{1,0:T(8,128)(2,1)S(1)}, bf16[272,256]{1,0:T(8,128)(2,1)S(1)}, u32[]{:S(2)}, u32[]{:S(2)}) collective-permute-start(bf16[272,256]{1,0:T(8,128)(2,1)S(1)} %get-tuple-element.27.refs_0_), channel_id=1, source_target_pairs={{0,4},{4,0},{8,12},{12,8},{16,20},{20,16},{24,28},{28,24},{1,5},{5... | collective-permute-start | bytes 417800 | tf_op jit(solution)/shard_map/ppermute | solution.py:28
  32.5 3.7 %collective-permute-done.11.refs_2_ = bf16[272,256]{1,0:T(8,128)(2,1)S(1)} collective-permute-done((bf16[272,256]{1,0:T(8,128)(2,1)S(1)}, bf16[272,256]{1,0:T(8,128)(2,1)S(1)}, u32[]{:S(2)}, u32[]{:S(2)}) %collective-permute-start.11) | collective-permute-done | bytes 139296 | tf_op jit(solution)/shard_map/ppermute | solution.py:28
  36.2 2.2 %collective-permute-start.15 = (bf16[272,256]{1,0:T(8,128)(2,1)S(1)}, bf16[272,256]{1,0:T(8,128)(2,1)S(1)}, u32[]{:S(2)}, u32[]{:S(2)}) collective-permute-start(bf16[272,256]{1,0:T(8,128)(2,1)S(1)} %collective-permute-done.11.refs_2_), channel_id=1, source_target_pairs={{0,4},{4,0},{8,12},{12,8},{16,20},{20,16},{24,28},{28,24},{1,5},{5... | collective-permute-start | bytes 417800 | tf_op jit(solution)/shard_map/ppermute | solution.py:28
  38.4 4.8 %collective-permute-done.12.refs_3_ = bf16[272,256]{1,0:T(8,128)(2,1)S(1)} collective-permute-done((bf16[272,256]{1,0:T(8,128)(2,1)S(1)}, bf16[272,256]{1,0:T(8,128)(2,1)S(1)}, u32[]{:S(2)}, u32[]{:S(2)}) %collective-permute-start.12) | collective-permute-done | bytes 139296 | tf_op jit(solution)/shard_map/ppermute | solution.py:28
  43.3 0.5 %collective-permute-start.16 = (bf16[272,256]{1,0:T(8,128)(2,1)S(1)}, bf16[272,256]{1,0:T(8,128)(2,1)S(1)}, u32[]{:S(2)}, u32[]{:S(2)}) collective-permute-start(bf16[272,256]{1,0:T(8,128)(2,1)S(1)} %collective-permute-done.12.refs_3_), channel_id=1, source_target_pairs={{0,4},{4,0},{8,12},{12,8},{16,20},{20,16},{24,28},{28,24},{1,5},{5... | collective-permute-start | bytes 417800 | tf_op jit(solution)/shard_map/ppermute | solution.py:28
  43.8 1.0 %collective-permute-done.16.refs_7_ = bf16[272,256]{1,0:T(8,128)(2,1)S(1)} collective-permute-done((bf16[272,256]{1,0:T(8,128)(2,1)S(1)}, bf16[272,256]{1,0:T(8,128)(2,1)S(1)}, u32[]{:S(2)}, u32[]{:S(2)}) %collective-permute-start.16) | collective-permute-done | bytes 139296 | tf_op jit(solution)/shard_map/ppermute | solution.py:28
  44.7 0.4 collective-permute-done.14.refs_5_
  45.1 0.8 %line_sums.1 = (bf16[128,256]{1,0:T(8,128)(2,1)}, bf16[128,256]{1,0:T(8,128)(2,1)}, f32[256,256]{1,0:T(8,128)}, f32[1,256]{1,0:T(1,128)}) custom-call(bf16[128,256]{1,0:T(8,128)(2,1)S(1)} %get-tuple-element.22.own_hidden, f32[128,256]{1,0:T(8,128)S(1)} %get-tuple-element.26.mine, bf16[272,256]{1,0:T(8,128)(2,1)S(1)} %get-tuple-element.27.refs_0_, ...), custom_call_target="tpu_custom_call" | custom-call | tf_op jit(solution)/shard_map/line_sums/pallas_call | solution.py:208
  (23 shorter events, 0.2 us)
Async XLA Ops:
  0.6 6.4 %copy-start.2 = (bf16[1,128,256]{2,1,0:T(8,128)(2,1)S(1)}, bf16[1,128,256]{2,1,0:T(8,128)(2,1)}, u32[]{:S(2)}) copy-start(bf16[1,128,256]{2,1,0:T(8,128)(2,1)} %param.9) | copy-start | bytes 196612
  0.6 7.9 %collective-permute-start.5 = (bf16[128,256]{1,0:T(8,128)(2,1)}, bf16[128,256]{1,0:T(8,128)(2,1)S(1)}, u32[]{:S(2)}, u32[]{:S(2)}) collective-permute-start(bf16[128,256]{1,0:T(8,128)(2,1)} %bitcast.13), channel_id=1, source_target_pairs={{0,24},{4,28},{8,16},{12,20},{16,8},{20,12},{24,0},{28,4},{1,25},{... | collective-permute-start | bytes 196616 | tf_op jit(solution)/shard_map/ppermute | solution.py:28
  0.9 7.9 %collective-permute-start.3 = (bf16[128,256]{1,0:T(8,128)(2,1)}, bf16[128,256]{1,0:T(8,128)(2,1)S(1)}, u32[]{:S(2)}, u32[]{:S(2)}) collective-permute-start(bf16[128,256]{1,0:T(8,128)(2,1)} %bitcast.14), channel_id=1, source_target_pairs={{0,16},{4,20},{8,24},{12,28},{16,0},{20,4},{24,8},{28,12},{1,17},{... | collective-permute-start | bytes 196616 | tf_op jit(solution)/shard_map/ppermute | solution.py:28
  4.1 5.4 %collective-permute-start.1 = (bf16[128,256]{1,0:T(8,128)(2,1)}, bf16[128,256]{1,0:T(8,128)(2,1)S(1)}, u32[]{:S(2)}, u32[]{:S(2)}) collective-permute-start(bf16[128,256]{1,0:T(8,128)(2,1)} %bitcast.15), channel_id=1, source_target_pairs={{0,8},{4,12},{8,0},{12,4},{16,24},{20,28},{24,16},{28,20},{1,9},{5... | collective-permute-start | bytes 196616 | tf_op jit(solution)/shard_map/ppermute | solution.py:28
  5.7 5.4 %copy-start = (bf16[1,1,3,128,128]{4,3,2,1,0:T(8,128)(2,1)S(1)}, bf16[1,1,3,128,128]{4,3,2,1,0:T(8,128)(2,1)}, u32[]{:S(2)}) copy-start(bf16[1,1,3,128,128]{4,3,2,1,0:T(8,128)(2,1)} %param.10) | copy-start | bytes 294916
  5.8 4.0 %collective-permute-start.7 = (bf16[144,256]{1,0:T(8,128)(2,1)S(1)}, bf16[144,256]{1,0:T(8,128)(2,1)S(1)}, u32[]{:S(2)}, u32[]{:S(2)}) collective-permute-start(bf16[144,256]{1,0:T(8,128)(2,1)S(1)} %get-tuple-element.21.refs_0_.refs_5_), channel_id=1, source_target_pairs={{0,1},{1,0},{2,3},{3,2},{4,5},{5,4},{6,7},{7,6},{8,9},{9,8},{10,11... | collective-permute-start | bytes 221192 | tf_op jit(solution)/shard_map/ppermute | solution.py:28
  7.0 4.1 %collective-permute-start = (bf16[128,256]{1,0:T(8,128)(2,1)S(1)}, bf16[128,256]{1,0:T(8,128)(2,1)S(1)}, u32[]{:S(2)}, u32[]{:S(2)}) collective-permute-start(bf16[128,256]{1,0:T(8,128)(2,1)S(1)} %bitcast.16), channel_id=1, source_target_pairs={{0,4},{4,0},{8,12},{12,8},{16,20},{20,16},{24,28},{28,24},{1,5},{5... | collective-permute-start | bytes 196616 | tf_op jit(solution)/shard_map/ppermute | solution.py:28
  8.6 2.6 %collective-permute-start.6 = (bf16[128,256]{1,0:T(8,128)(2,1)S(1)}, bf16[128,256]{1,0:T(8,128)(2,1)S(1)}, u32[]{:S(2)}, u32[]{:S(2)}) collective-permute-start(bf16[128,256]{1,0:T(8,128)(2,1)S(1)} %collective-permute-done.5.refs_6_), channel_id=1, source_target_pairs={{0,4},{4,0},{8,12},{12,8},{16,20},{20,16},{24,28},{28,24},{1,5},{5... | collective-permute-start | bytes 196616 | tf_op jit(solution)/shard_map/ppermute | solution.py:28
  8.8 2.4 %collective-permute-start.4 = (bf16[128,256]{1,0:T(8,128)(2,1)S(1)}, bf16[128,256]{1,0:T(8,128)(2,1)S(1)}, u32[]{:S(2)}, u32[]{:S(2)}) collective-permute-start(bf16[128,256]{1,0:T(8,128)(2,1)S(1)} %collective-permute-done.3.refs_4_), channel_id=1, source_target_pairs={{0,4},{4,0},{8,12},{12,8},{16,20},{20,16},{24,28},{28,24},{1,5},{5... | collective-permute-start | bytes 196616 | tf_op jit(solution)/shard_map/ppermute | solution.py:28
  9.5 1.6 %collective-permute-start.2 = (bf16[128,256]{1,0:T(8,128)(2,1)S(1)}, bf16[128,256]{1,0:T(8,128)(2,1)S(1)}, u32[]{:S(2)}, u32[]{:S(2)}) collective-permute-start(bf16[128,256]{1,0:T(8,128)(2,1)S(1)} %collective-permute-done.1.refs_2_), channel_id=1, source_target_pairs={{0,4},{4,0},{8,12},{12,8},{16,20},{20,16},{24,28},{28,24},{1,5},{5... | collective-permute-start | bytes 196616 | tf_op jit(solution)/shard_map/ppermute | solution.py:28
  9.8 11.5 %collective-permute-start.8 = (bf16[288,256]{1,0:T(8,128)(2,1)S(1)}, bf16[288,256]{1,0:T(8,128)(2,1)S(1)}, u32[]{:S(2)}, u32[]{:S(2)}) collective-permute-start(bf16[288,256]{1,0:T(8,128)(2,1)S(1)} %cotangents_so_far.1), channel_id=1, source_target_pairs={{0,2},{1,3},{2,0},{3,1},{4,6},{5,7},{6,4},{7,5},{8,10},{9,11},{10,... | collective-permute-start | bytes 442376 | tf_op jit(solution)/shard_map/ppermute | solution.py:28
  11.4 9.9 %copy-start.1 = (bf16[256,256]{1,0:T(8,128)(2,1)S(1)}, bf16[256,256]{1,0:T(8,128)(2,1)}, u32[]{:S(2)}) copy-start(bf16[256,256]{1,0:T(8,128)(2,1)} %refs_1_.1) | copy-start | bytes 393220
  22.6 5.1 %collective-permute-start.9 = (bf16[656,256]{1,0:T(8,128)(2,1)S(1)}, bf16[656,256]{1,0:T(8,128)(2,1)S(1)}, u32[]{:S(2)}, u32[]{:S(2)}) collective-permute-start(bf16[656,256]{1,0:T(8,128)(2,1)S(1)} %get-tuple-element.25.own_sent), channel_id=1, source_target_pairs={{0,4},{4,0},{8,12},{12,8},{16,20},{20,16},{24,28},{28,24},{1,5},{5... | collective-permute-start | bytes 1007624 | tf_op jit(solution)/shard_map/ppermute | solution.py:28
  27.7 8.5 %collective-permute-start.11 = (bf16[272,256]{1,0:T(8,128)(2,1)S(1)}, bf16[272,256]{1,0:T(8,128)(2,1)S(1)}, u32[]{:S(2)}, u32[]{:S(2)}) collective-permute-start(bf16[272,256]{1,0:T(8,128)(2,1)S(1)} %get-tuple-element.28), channel_id=1, source_target_pairs={{0,16},{4,20},{8,24},{12,28},{16,0},{20,4},{24,8},{28,12},{1,17},{... | collective-permute-start | bytes 417800 | tf_op jit(solution)/shard_map/ppermute | solution.py:28
  27.8 15.5 %collective-permute-start.12 = (bf16[272,256]{1,0:T(8,128)(2,1)S(1)}, bf16[272,256]{1,0:T(8,128)(2,1)S(1)}, u32[]{:S(2)}, u32[]{:S(2)}) collective-permute-start(bf16[272,256]{1,0:T(8,128)(2,1)S(1)} %get-tuple-element.29), channel_id=1, source_target_pairs={{0,24},{4,28},{8,16},{12,20},{16,8},{20,12},{24,0},{28,4},{1,25},{... | collective-permute-start | bytes 417800 | tf_op jit(solution)/shard_map/ppermute | solution.py:28
  30.7 13.1 %collective-permute-start.10 = (bf16[272,256]{1,0:T(8,128)(2,1)S(1)}, bf16[272,256]{1,0:T(8,128)(2,1)S(1)}, u32[]{:S(2)}, u32[]{:S(2)}) collective-permute-start(bf16[272,256]{1,0:T(8,128)(2,1)S(1)} %get-tuple-element.27.refs_0_), channel_id=1, source_target_pairs={{0,8},{4,12},{8,0},{12,4},{16,24},{20,28},{24,16},{28,20},{1,9},{5... | collective-permute-start | bytes 417800 | tf_op jit(solution)/shard_map/ppermute | solution.py:28
  31.3 12.5 %collective-permute-start.13 = (bf16[272,256]{1,0:T(8,128)(2,1)S(1)}, bf16[272,256]{1,0:T(8,128)(2,1)S(1)}, u32[]{:S(2)}, u32[]{:S(2)}) collective-permute-start(bf16[272,256]{1,0:T(8,128)(2,1)S(1)} %get-tuple-element.27.refs_0_), channel_id=1, source_target_pairs={{0,4},{4,0},{8,12},{12,8},{16,20},{20,16},{24,28},{28,24},{1,5},{5... | collective-permute-start | bytes 417800 | tf_op jit(solution)/shard_map/ppermute | solution.py:28
  36.2 7.5 %collective-permute-start.15 = (bf16[272,256]{1,0:T(8,128)(2,1)S(1)}, bf16[272,256]{1,0:T(8,128)(2,1)S(1)}, u32[]{:S(2)}, u32[]{:S(2)}) collective-permute-start(bf16[272,256]{1,0:T(8,128)(2,1)S(1)} %collective-permute-done.11.refs_2_), channel_id=1, source_target_pairs={{0,4},{4,0},{8,12},{12,8},{16,20},{20,16},{24,28},{28,24},{1,5},{5... | collective-permute-start | bytes 417800 | tf_op jit(solution)/shard_map/ppermute | solution.py:28
  43.3 1.5 %collective-permute-start.16 = (bf16[272,256]{1,0:T(8,128)(2,1)S(1)}, bf16[272,256]{1,0:T(8,128)(2,1)S(1)}, u32[]{:S(2)}, u32[]{:S(2)}) collective-permute-start(bf16[272,256]{1,0:T(8,128)(2,1)S(1)} %collective-permute-done.12.refs_3_), channel_id=1, source_target_pairs={{0,4},{4,0},{8,12},{12,8},{16,20},{20,16},{24,28},{28,24},{1,5},{5... | collective-permute-start | bytes 417800 | tf_op jit(solution)/shard_map/ppermute | solution.py:28
  43.8 1.4 %collective-permute-start.14 = (bf16[272,256]{1,0:T(8,128)(2,1)S(1)}, bf16[272,256]{1,0:T(8,128)(2,1)S(1)}, u32[]{:S(2)}, u32[]{:S(2)}) collective-permute-start(bf16[272,256]{1,0:T(8,128)(2,1)S(1)} %collective-permute-done.10.refs_1_), channel_id=1, source_target_pairs={{0,4},{4,0},{8,12},{12,8},{16,20},{20,16},{24,28},{28,24},{1,5},{5... | collective-permute-start | bytes 417800 | tf_op jit(solution)/shard_map/ppermute | solution.py:28

commit v5 on v4

--- a/solution.py
+++ b/solution.py
@@ -48,10 +48,9 @@
     return rows[0:1] + rows[1:2]
 
 
-def cotangent_kernel(blocks, tile_rows, tile_cols, count, mask, cotangent, bias, out, own_bias, ints):
+def cotangent_kernel(blocks, tile_rows, tile_cols, mask, cotangent, bias, out, own_bias, ints):
     own_bias[...] = bias[...]
     slots = tile_rows.shape[0]
-    ints[2 * slots] = jnp.max(count[...])
     for s in range(slots):
         ints[s] = tile_rows[s]
         ints[slots + s] = tile_cols[s]
@@ -75,13 +74,14 @@
         start += block.shape[0]
 
 
-def forward_kernel(slots, n_col, blocks, ints, tiles, *refs):
-    n_row = len(refs) - 3
-    sources, out, held, total = refs[:n_row], refs[n_row], refs[n_row + 1], refs[n_row + 2]
+def forward_kernel(slots, n_col, blocks, ints, counts, tiles, *refs):
+    n_row = len(refs) - 4
+    sources, (out, count, held, total) = refs[:n_row], refs[n_row:]
+    count[0] = jnp.max(counts[...])
     side = tiles.shape[-1]
     for q in range(n_row):
         held[q] = sources[q][...]
-    me_row, live = lax.axis_index("row"), ints[2 * slots]
+    me_row, live = lax.axis_index("row"), count[0]
 
     def product(s):
         taken = held[ints[slots + s] ^ me_row]
@@ -103,14 +103,14 @@
 
 
 def middle_kernel(slots, n_row, n_col, blocks, *refs):
-    ints, refs = refs[0], refs[1:]
+    (ints, count), refs = refs[:2], refs[2:]
     (weight, bias, tiles, products), refs = refs[:4], refs[4:]
     steps = n_col.bit_length()
     cots, refs = refs[:steps], refs[steps:]
     hidden, sent, kept, kept_weight, total, agg, grads, grad_agg, weights, back, target = refs
     side = tiles.shape[-1]
     half = weight.shape[0] // 2
-    me_row, me_col, live = lax.axis_index("row"), lax.axis_index("col"), ints[2 * slots]
+    me_row, me_col, live = lax.axis_index("row"), lax.axis_index("col"), count[0]
     each_rows = cots[0].shape[0]
 
     def cotangent(q, start, stop):
@@ -246,10 +246,9 @@
     with_places, own_bias, ints = call(
         functools.partial(cotangent_kernel, blocks),
         "masked_cotangent",
-        [((side + blocks + -blocks % PAD, width), BF16, True), ((1, width), F32, True), ((2 * slots + 1,), jnp.int32, True)],
+        [((side + blocks + -blocks % PAD, width), BF16, True), ((1, width), F32, True), ((2 * slots,), jnp.int32, True)],
         [],
         [far(tile_rows[0, 0]), far(tile_cols[0, 0])],
-        tile_count,
         far(label_mask),
         far(cotangent[0]),
         far(bias[None]),
@@ -267,13 +266,19 @@
         ) if reach > 1 else cots
         cots, reach = cots + [exchange(held, "col", reach)], 2 * reach
 
-    sources = [part for block in along for part in (block, exchange(block, "row", 1))]
-    (product,) = call(
+    sources = [own, exchange(own, "row", 1)]
+    tile_count, _ = lax.optimization_barrier((tile_count, sources[1]))
+    counts = jnp.broadcast_to(tile_count, (8, 128))
+    for block in along[1:]:
+        block, _ = lax.optimization_barrier((block, counts))
+        sources += [block, exchange(block, "row", 1)]
+    product, count = call(
         functools.partial(forward_kernel, slots, n_col, blocks),
         "tile_products",
-        [((blocks * side, width), BF16, True)],
+        [((blocks * side, width), BF16, True), ((2,), jnp.int32, True)],
         [((n_row, side, width), BF16), ((n_col, side, width), F32)],
         [ints],
+        near(counts),
         own_tiles,
         *map(near, sources),
     )
@@ -298,7 +303,7 @@
             ((n_row, side, width), F32),
             ((n_col, blocks), jnp.int32),
         ],
-        [ints],
+        [ints, pltpu.with_memory_space_constraint(count, pltpu.SMEM)],
         near(weight),
         near(own_bias),
         own_tiles,

time: 46.1 us -> 45.7 us (level)
  the two profiles are of different devices: /device:TPU:17 before, /device:TPU:0 now
where the time goes in v5:
time: 45.7 us; the launch traced here: 45 us
  starting transfers between devices  14.3 us (31%)
  waiting for transfers between devices  14.2 us (31%)
  blocking collectives  11.7 us (26%)
  Pallas kernels  3.36 us (7%)
  between operations  1.4 us (3%)
    ppermute x17, starting transfers between devices, exchange(): return lax.ppermute(value, axis, [(i, i ^ mask) for i in range(size)])  14.3 us
    ppermute x17, waiting for transfers between devices, exchange(): return lax.ppermute(value, axis, [(i, i ^ mask) for i in range(size)])  14.2 us
    all_gather x1, blocking collectives, on_device(): products = lax.all_gather(product, 'col')  11.7 us
    pallas_call x6, Pallas kernels, call(): pl.pallas_call(kernel, name=name, out_shape=[space(dtype)(shape, dtype) i...  3.36 us
  transfers between devices with their start and end apart: 17, of which 7 were waited for; matrix products, arithmetic and copies ran while one was open for 0% of the time, Pallas kernels for 3%

profile of v5, /device:TPU:0, one launch (start us, length us, event | category | flops | bytes accessed | tf_op | source)
XLA Modules:
  0.0 45.0 jit_solution(4636788273255094717)
XLA Ops:
  0.6 5.1 %collective-permute-start.5 = (bf16[128,256]{1,0:T(8,128)(2,1)}, bf16[128,256]{1,0:T(8,128)(2,1)S(1)}, u32[]{:S(2)}, u32[]{:S(2)}) collective-permute-start(bf16[128,256]{1,0:T(8,128)(2,1)} %bitcast.15), channel_id=1, source_target_pairs={{0,24},{4,28},{8,16},{12,20},{16,8},{20,12},{24,0},{28,4},{1,25},{... | collective-permute-start | bytes 196616 | tf_op jit(solution)/shard_map/ppermute | solution.py:28
  5.8 0.6 %collective-permute-start.1 = (bf16[128,256]{1,0:T(8,128)(2,1)}, bf16[128,256]{1,0:T(8,128)(2,1)S(1)}, u32[]{:S(2)}, u32[]{:S(2)}) collective-permute-start(bf16[128,256]{1,0:T(8,128)(2,1)} %bitcast.17), channel_id=1, source_target_pairs={{0,8},{4,12},{8,0},{12,4},{16,24},{20,28},{24,16},{28,20},{1,9},{5... | collective-permute-start | bytes 196616 | tf_op jit(solution)/shard_map/ppermute | solution.py:28
  6.4 1.0 %masked_cotangent.1 = (bf16[144,256]{1,0:T(8,128)(2,1)S(1)}, f32[1,256]{1,0:T(1,128)S(1)}, s32[6]{0:T(128)S(4)}) custom-call(s32[3]{0:T(128)} %bitcast.22, s32[3]{0:T(128)} %bitcast.23, s32[1,128]{1,0:T(1,128)} %mask.1, bf16[128,256]{1,0:T(8,128)(2,1)} %bitcast.20, f32[1,256]{1,0:T(1,128)} %bitcast.21), custom_call_target="tpu_custom_call" | custom-call | tf_op jit(solution)/shard_map/masked_cotangent/pallas_call | solution.py:208
  7.4 1.7 %collective-permute-start.7 = (bf16[144,256]{1,0:T(8,128)(2,1)S(1)}, bf16[144,256]{1,0:T(8,128)(2,1)S(1)}, u32[]{:S(2)}, u32[]{:S(2)}) collective-permute-start(bf16[144,256]{1,0:T(8,128)(2,1)S(1)} %get-tuple-element.33.refs_0_.refs_6_), channel_id=1, source_target_pairs={{0,1},{1,0},{2,3},{3,2},{4,5},{5,4},{6,7},{7,6},{8,9},{9,8},{10,11... | collective-permute-start | bytes 221192 | tf_op jit(solution)/shard_map/ppermute | solution.py:28
  9.8 0.6 %collective-permute-start.6 = (bf16[128,256]{1,0:T(8,128)(2,1)S(1)}, bf16[128,256]{1,0:T(8,128)(2,1)S(1)}, u32[]{:S(2)}, u32[]{:S(2)}) collective-permute-start(bf16[128,256]{1,0:T(8,128)(2,1)S(1)} %collective-permute-done.5.refs_6_), channel_id=1, source_target_pairs={{0,4},{4,0},{8,12},{12,8},{16,20},{20,16},{24,28},{28,24},{1,5},{5... | collective-permute-start | bytes 196616 | tf_op jit(solution)/shard_map/ppermute | solution.py:28
  10.4 1.2 %collective-permute-done.3.refs_4_ = bf16[128,256]{1,0:T(8,128)(2,1)S(1)} collective-permute-done((bf16[128,256]{1,0:T(8,128)(2,1)}, bf16[128,256]{1,0:T(8,128)(2,1)S(1)}, u32[]{:S(2)}, u32[]{:S(2)}) %collective-permute-start.3) | collective-permute-done | bytes 65568 | tf_op jit(solution)/shard_map/ppermute | solution.py:28
  11.6 0.5 %collective-permute-start.2 = (bf16[128,256]{1,0:T(8,128)(2,1)S(1)}, bf16[128,256]{1,0:T(8,128)(2,1)S(1)}, u32[]{:S(2)}, u32[]{:S(2)}) collective-permute-start(bf16[128,256]{1,0:T(8,128)(2,1)S(1)} %collective-permute-done.1.refs_2_), channel_id=1, source_target_pairs={{0,4},{4,0},{8,12},{12,8},{16,20},{20,16},{24,28},{28,24},{1,5},{5... | collective-permute-start | bytes 196616 | tf_op jit(solution)/shard_map/ppermute | solution.py:28
  12.1 1.6 %collective-permute-start.8 = (bf16[288,256]{1,0:T(8,128)(2,1)S(1)}, bf16[288,256]{1,0:T(8,128)(2,1)S(1)}, u32[]{:S(2)}, u32[]{:S(2)}) collective-permute-start(bf16[288,256]{1,0:T(8,128)(2,1)S(1)} %cotangents_so_far.1), channel_id=1, source_target_pairs={{0,2},{1,3},{2,0},{3,1},{4,6},{5,7},{6,4},{7,5},{8,10},{9,11},{10,... | collective-permute-start | bytes 442376 | tf_op jit(solution)/shard_map/ppermute | solution.py:28
  13.7 0.2 tile_products.1
  14.0 11.7 %all-gather = bf16[1536,256]{1,0:T(8,128)(2,1)S(1)} all-gather(bf16[384,256]{1,0:T(8,128)(2,1)S(1)} %get-tuple-element.32), channel_id=2, replica_groups=mesh['row'=8,'col'=4] {'col'}, dimensions={0}, use_global_device_ids=true | all-gather | bytes 983040 | tf_op jit(solution)/shard_map/all_gather | solution.py:285
  25.7 1.2 %dense_layer.1 = (bf16[128,256]{1,0:T(8,128)(2,1)S(1)}, bf16[656,256]{1,0:T(8,128)(2,1)S(1)}, f32[512,256]{1,0:T(8,128)S(1)}, f32[128,256]{1,0:T(8,128)S(1)}) custom-call(s32[6]{0:T(128)S(4)} %get-tuple-element.25.ints.refs_0_, s32[2]{0:T(128)S(4)} %get-tuple-element.30.refs_1_, bf16[256,256]{1,0:T(8,128)(2,1)S(1)} %copy-done.1, ...), custom_call_target="tpu_custom_call" | custom-call | tf_op jit(solution)/shard_map/dense_layer/pallas_call | solution.py:208
  26.9 0.1 collective-permute-start.9
  27.0 1.6 %collective-permute-done.9.came = bf16[656,256]{1,0:T(8,128)(2,1)S(1)} collective-permute-done((bf16[656,256]{1,0:T(8,128)(2,1)S(1)}, bf16[656,256]{1,0:T(8,128)(2,1)S(1)}, u32[]{:S(2)}, u32[]{:S(2)}) %collective-permute-start.9) | collective-permute-done | bytes 335904 | tf_op jit(solution)/shard_map/ppermute | solution.py:28
  28.7 0.1 chip_sums.1
  28.7 1.6 %collective-permute-start.11 = (bf16[272,256]{1,0:T(8,128)(2,1)S(1)}, bf16[272,256]{1,0:T(8,128)(2,1)S(1)}, u32[]{:S(2)}, u32[]{:S(2)}) collective-permute-start(bf16[272,256]{1,0:T(8,128)(2,1)S(1)} %get-tuple-element.40), channel_id=1, source_target_pairs={{0,16},{4,20},{8,24},{12,28},{16,0},{20,4},{24,8},{28,12},{1,17},{... | collective-permute-start | bytes 417800 | tf_op jit(solution)/shard_map/ppermute | solution.py:28
  30.3 1.6 %collective-permute-start.12 = (bf16[272,256]{1,0:T(8,128)(2,1)S(1)}, bf16[272,256]{1,0:T(8,128)(2,1)S(1)}, u32[]{:S(2)}, u32[]{:S(2)}) collective-permute-start(bf16[272,256]{1,0:T(8,128)(2,1)S(1)} %get-tuple-element.41), channel_id=1, source_target_pairs={{0,24},{4,28},{8,16},{12,20},{16,8},{20,12},{24,0},{28,4},{1,25},{... | collective-permute-start | bytes 417800 | tf_op jit(solution)/shard_map/ppermute | solution.py:28
  31.9 0.4 collective-permute-start.10
  32.3 9.5 %collective-permute-done.11.refs_2_ = bf16[272,256]{1,0:T(8,128)(2,1)S(1)} collective-permute-done((bf16[272,256]{1,0:T(8,128)(2,1)S(1)}, bf16[272,256]{1,0:T(8,128)(2,1)S(1)}, u32[]{:S(2)}, u32[]{:S(2)}) %collective-permute-start.11) | collective-permute-done | bytes 139296 | tf_op jit(solution)/shard_map/ppermute | solution.py:28
  41.8 0.5 %collective-permute-start.16 = (bf16[272,256]{1,0:T(8,128)(2,1)S(1)}, bf16[272,256]{1,0:T(8,128)(2,1)S(1)}, u32[]{:S(2)}, u32[]{:S(2)}) collective-permute-start(bf16[272,256]{1,0:T(8,128)(2,1)S(1)} %collective-permute-done.12.refs_3_), channel_id=1, source_target_pairs={{0,4},{4,0},{8,12},{12,8},{16,20},{20,16},{24,28},{28,24},{1,5},{5... | collective-permute-start | bytes 417800 | tf_op jit(solution)/shard_map/ppermute | solution.py:28
  42.3 0.5 %collective-permute-done.10.refs_1_ = bf16[272,256]{1,0:T(8,128)(2,1)S(1)} collective-permute-done((bf16[272,256]{1,0:T(8,128)(2,1)S(1)}, bf16[272,256]{1,0:T(8,128)(2,1)S(1)}, u32[]{:S(2)}, u32[]{:S(2)}) %collective-permute-start.10) | collective-permute-done | bytes 139296 | tf_op jit(solution)/shard_map/ppermute | solution.py:28
  42.8 0.4 collective-permute-done.15.refs_6_
  43.2 0.2 collective-permute-done.16.refs_7_
  43.4 0.8 %collective-permute-done.14.refs_5_ = bf16[272,256]{1,0:T(8,128)(2,1)S(1)} collective-permute-done((bf16[272,256]{1,0:T(8,128)(2,1)S(1)}, bf16[272,256]{1,0:T(8,128)(2,1)S(1)}, u32[]{:S(2)}, u32[]{:S(2)}) %collective-permute-start.14) | collective-permute-done | bytes 139296 | tf_op jit(solution)/shard_map/ppermute | solution.py:28
  44.2 0.8 %line_sums.1 = (bf16[128,256]{1,0:T(8,128)(2,1)}, bf16[128,256]{1,0:T(8,128)(2,1)}, f32[256,256]{1,0:T(8,128)}, f32[1,256]{1,0:T(1,128)}) custom-call(bf16[128,256]{1,0:T(8,128)(2,1)S(1)} %get-tuple-element.34.own_hidden, f32[128,256]{1,0:T(8,128)S(1)} %get-tuple-element.38.mine, bf16[272,256]{1,0:T(8,128)(2,1)S(1)} %get-tuple-element.39.refs_0_, ...), custom_call_target="tpu_custom_call" | custom-call | tf_op jit(solution)/shard_map/line_sums/pallas_call | solution.py:208
  (24 shorter events, 0.1 us)
Async XLA Ops:
  0.6 8.5 %copy-start.2 = (bf16[1,128,256]{2,1,0:T(8,128)(2,1)S(1)}, bf16[1,128,256]{2,1,0:T(8,128)(2,1)}, u32[]{:S(2)}) copy-start(bf16[1,128,256]{2,1,0:T(8,128)(2,1)} %param.9) | copy-start | bytes 196612
  0.6 9.1 %collective-permute-start.5 = (bf16[128,256]{1,0:T(8,128)(2,1)}, bf16[128,256]{1,0:T(8,128)(2,1)S(1)}, u32[]{:S(2)}, u32[]{:S(2)}) collective-permute-start(bf16[128,256]{1,0:T(8,128)(2,1)} %bitcast.15), channel_id=1, source_target_pairs={{0,24},{4,28},{8,16},{12,20},{16,8},{20,12},{24,0},{28,4},{1,25},{... | collective-permute-start | bytes 196616 | tf_op jit(solution)/shard_map/ppermute | solution.py:28
  5.8 5.8 %collective-permute-start.3 = (bf16[128,256]{1,0:T(8,128)(2,1)}, bf16[128,256]{1,0:T(8,128)(2,1)S(1)}, u32[]{:S(2)}, u32[]{:S(2)}) collective-permute-start(bf16[128,256]{1,0:T(8,128)(2,1)} %bitcast.16), channel_id=1, source_target_pairs={{0,16},{4,20},{8,24},{12,28},{16,0},{20,4},{24,8},{28,12},{1,17},{... | collective-permute-start | bytes 196616 | tf_op jit(solution)/shard_map/ppermute | solution.py:28
  5.8 5.8 %collective-permute-start.1 = (bf16[128,256]{1,0:T(8,128)(2,1)}, bf16[128,256]{1,0:T(8,128)(2,1)S(1)}, u32[]{:S(2)}, u32[]{:S(2)}) collective-permute-start(bf16[128,256]{1,0:T(8,128)(2,1)} %bitcast.17), channel_id=1, source_target_pairs={{0,8},{4,12},{8,0},{12,4},{16,24},{20,28},{24,16},{28,20},{1,9},{5... | collective-permute-start | bytes 196616 | tf_op jit(solution)/shard_map/ppermute | solution.py:28
  7.4 4.7 %collective-permute-start.7 = (bf16[144,256]{1,0:T(8,128)(2,1)S(1)}, bf16[144,256]{1,0:T(8,128)(2,1)S(1)}, u32[]{:S(2)}, u32[]{:S(2)}) collective-permute-start(bf16[144,256]{1,0:T(8,128)(2,1)S(1)} %get-tuple-element.33.refs_0_.refs_6_), channel_id=1, source_target_pairs={{0,1},{1,0},{2,3},{3,2},{4,5},{5,4},{6,7},{7,6},{8,9},{9,8},{10,11... | collective-permute-start | bytes 221192 | tf_op jit(solution)/shard_map/ppermute | solution.py:28
  9.1 4.6 %collective-permute-start = (bf16[128,256]{1,0:T(8,128)(2,1)S(1)}, bf16[128,256]{1,0:T(8,128)(2,1)S(1)}, u32[]{:S(2)}, u32[]{:S(2)}) collective-permute-start(bf16[128,256]{1,0:T(8,128)(2,1)S(1)} %bitcast.18), channel_id=1, source_target_pairs={{0,4},{4,0},{8,12},{12,8},{16,20},{20,16},{24,28},{28,24},{1,5},{5... | collective-permute-start | bytes 196616 | tf_op jit(solution)/shard_map/ppermute | solution.py:28
  9.8 3.9 %copy-start = (bf16[1,1,3,128,128]{4,3,2,1,0:T(8,128)(2,1)S(1)}, bf16[1,1,3,128,128]{4,3,2,1,0:T(8,128)(2,1)}, u32[]{:S(2)}) copy-start(bf16[1,1,3,128,128]{4,3,2,1,0:T(8,128)(2,1)} %param.10) | copy-start | bytes 294916
  9.8 3.9 %collective-permute-start.6 = (bf16[128,256]{1,0:T(8,128)(2,1)S(1)}, bf16[128,256]{1,0:T(8,128)(2,1)S(1)}, u32[]{:S(2)}, u32[]{:S(2)}) collective-permute-start(bf16[128,256]{1,0:T(8,128)(2,1)S(1)} %collective-permute-done.5.refs_6_), channel_id=1, source_target_pairs={{0,4},{4,0},{8,12},{12,8},{16,20},{20,16},{24,28},{28,24},{1,5},{5... | collective-permute-start | bytes 196616 | tf_op jit(solution)/shard_map/ppermute | solution.py:28
  11.6 2.1 %collective-permute-start.4 = (bf16[128,256]{1,0:T(8,128)(2,1)S(1)}, bf16[128,256]{1,0:T(8,128)(2,1)S(1)}, u32[]{:S(2)}, u32[]{:S(2)}) collective-permute-start(bf16[128,256]{1,0:T(8,128)(2,1)S(1)} %collective-permute-done.3.refs_4_), channel_id=1, source_target_pairs={{0,4},{4,0},{8,12},{12,8},{16,20},{20,16},{24,28},{28,24},{1,5},{5... | collective-permute-start | bytes 196616 | tf_op jit(solution)/shard_map/ppermute | solution.py:28
  11.6 2.1 %collective-permute-start.2 = (bf16[128,256]{1,0:T(8,128)(2,1)S(1)}, bf16[128,256]{1,0:T(8,128)(2,1)S(1)}, u32[]{:S(2)}, u32[]{:S(2)}) collective-permute-start(bf16[128,256]{1,0:T(8,128)(2,1)S(1)} %collective-permute-done.1.refs_2_), channel_id=1, source_target_pairs={{0,4},{4,0},{8,12},{12,8},{16,20},{20,16},{24,28},{28,24},{1,5},{5... | collective-permute-start | bytes 196616 | tf_op jit(solution)/shard_map/ppermute | solution.py:28
  12.1 13.6 %collective-permute-start.8 = (bf16[288,256]{1,0:T(8,128)(2,1)S(1)}, bf16[288,256]{1,0:T(8,128)(2,1)S(1)}, u32[]{:S(2)}, u32[]{:S(2)}) collective-permute-start(bf16[288,256]{1,0:T(8,128)(2,1)S(1)} %cotangents_so_far.1), channel_id=1, source_target_pairs={{0,2},{1,3},{2,0},{3,1},{4,6},{5,7},{6,4},{7,5},{8,10},{9,11},{10,... | collective-permute-start | bytes 442376 | tf_op jit(solution)/shard_map/ppermute | solution.py:28
  14.0 11.7 %copy-start.1 = (bf16[256,256]{1,0:T(8,128)(2,1)S(1)}, bf16[256,256]{1,0:T(8,128)(2,1)}, u32[]{:S(2)}) copy-start(bf16[256,256]{1,0:T(8,128)(2,1)} %refs_2_.1) | copy-start | bytes 393220
  26.9 1.7 %collective-permute-start.9 = (bf16[656,256]{1,0:T(8,128)(2,1)S(1)}, bf16[656,256]{1,0:T(8,128)(2,1)S(1)}, u32[]{:S(2)}, u32[]{:S(2)}) collective-permute-start(bf16[656,256]{1,0:T(8,128)(2,1)S(1)} %get-tuple-element.37.own_sent), channel_id=1, source_target_pairs={{0,4},{4,0},{8,12},{12,8},{16,20},{20,16},{24,28},{28,24},{1,5},{5... | collective-permute-start | bytes 1007624 | tf_op jit(solution)/shard_map/ppermute | solution.py:28
  28.7 13.1 %collective-permute-start.11 = (bf16[272,256]{1,0:T(8,128)(2,1)S(1)}, bf16[272,256]{1,0:T(8,128)(2,1)S(1)}, u32[]{:S(2)}, u32[]{:S(2)}) collective-permute-start(bf16[272,256]{1,0:T(8,128)(2,1)S(1)} %get-tuple-element.40), channel_id=1, source_target_pairs={{0,16},{4,20},{8,24},{12,28},{16,0},{20,4},{24,8},{28,12},{1,17},{... | collective-permute-start | bytes 417800 | tf_op jit(solution)/shard_map/ppermute | solution.py:28
  30.3 11.5 %collective-permute-start.12 = (bf16[272,256]{1,0:T(8,128)(2,1)S(1)}, bf16[272,256]{1,0:T(8,128)(2,1)S(1)}, u32[]{:S(2)}, u32[]{:S(2)}) collective-permute-start(bf16[272,256]{1,0:T(8,128)(2,1)S(1)} %get-tuple-element.41), channel_id=1, source_target_pairs={{0,24},{4,28},{8,16},{12,20},{16,8},{20,12},{24,0},{28,4},{1,25},{... | collective-permute-start | bytes 417800 | tf_op jit(solution)/shard_map/ppermute | solution.py:28
  31.9 10.9 %collective-permute-start.10 = (bf16[272,256]{1,0:T(8,128)(2,1)S(1)}, bf16[272,256]{1,0:T(8,128)(2,1)S(1)}, u32[]{:S(2)}, u32[]{:S(2)}) collective-permute-start(bf16[272,256]{1,0:T(8,128)(2,1)S(1)} %get-tuple-element.39.refs_0_), channel_id=1, source_target_pairs={{0,8},{4,12},{8,0},{12,4},{16,24},{20,28},{24,16},{28,20},{1,9},{5... | collective-permute-start | bytes 417800 | tf_op jit(solution)/shard_map/ppermute | solution.py:28
  32.3 10.5 %collective-permute-start.13 = (bf16[272,256]{1,0:T(8,128)(2,1)S(1)}, bf16[272,256]{1,0:T(8,128)(2,1)S(1)}, u32[]{:S(2)}, u32[]{:S(2)}) collective-permute-start(bf16[272,256]{1,0:T(8,128)(2,1)S(1)} %get-tuple-element.39.refs_0_), channel_id=1, source_target_pairs={{0,4},{4,0},{8,12},{12,8},{16,20},{20,16},{24,28},{28,24},{1,5},{5... | collective-permute-start | bytes 417800 | tf_op jit(solution)/shard_map/ppermute | solution.py:28
  41.8 1.4 %collective-permute-start.15 = (bf16[272,256]{1,0:T(8,128)(2,1)S(1)}, bf16[272,256]{1,0:T(8,128)(2,1)S(1)}, u32[]{:S(2)}, u32[]{:S(2)}) collective-permute-start(bf16[272,256]{1,0:T(8,128)(2,1)S(1)} %collective-permute-done.11.refs_2_), channel_id=1, source_target_pairs={{0,4},{4,0},{8,12},{12,8},{16,20},{20,16},{24,28},{28,24},{1,5},{5... | collective-permute-start | bytes 417800 | tf_op jit(solution)/shard_map/ppermute | solution.py:28
  41.8 1.6 %collective-permute-start.16 = (bf16[272,256]{1,0:T(8,128)(2,1)S(1)}, bf16[272,256]{1,0:T(8,128)(2,1)S(1)}, u32[]{:S(2)}, u32[]{:S(2)}) collective-permute-start(bf16[272,256]{1,0:T(8,128)(2,1)S(1)} %collective-permute-done.12.refs_3_), channel_id=1, source_target_pairs={{0,4},{4,0},{8,12},{12,8},{16,20},{20,16},{24,28},{28,24},{1,5},{5... | collective-permute-start | bytes 417800 | tf_op jit(solution)/shard_map/ppermute | solution.py:28
  42.8 1.4 %collective-permute-start.14 = (bf16[272,256]{1,0:T(8,128)(2,1)S(1)}, bf16[272,256]{1,0:T(8,128)(2,1)S(1)}, u32[]{:S(2)}, u32[]{:S(2)}) collective-permute-start(bf16[272,256]{1,0:T(8,128)(2,1)S(1)} %collective-permute-done.10.refs_1_), channel_id=1, source_target_pairs={{0,4},{4,0},{8,12},{12,8},{16,20},{20,16},{24,28},{28,24},{1,5},{5... | collective-permute-start | bytes 417800 | tf_op jit(solution)/shard_map/ppermute | solution.py:28

commit v6 on v5

--- a/solution.py
+++ b/solution.py
@@ -182,21 +182,31 @@
         out[side + half : side + half + PAD] = column_sum
 
 
-def line_kernel(scale, own_hidden, mine, *refs):
-    blocks, (hidden, grad_features, grad_weight, grad_bias) = refs[:-4], refs[-4:]
+def line_weight_kernel(scale, *refs):
+    blocks, out = refs[:-1], refs[-1]
+    half = out.shape[0] - 8
+    start = blocks[0].shape[0] - half - PAD
+    out[0:half] = scale * tree_sum(b[start : start + half].astype(F32) for b in blocks)
+    column_sum = scale * tree_sum(joined(b[start + half :]) for b in blocks)
+    out[half:] = jnp.broadcast_to(column_sum, (8, column_sum.shape[1]))
+
+
+def node_results_kernel(own_hidden, mine, *refs):
+    blocks, (hidden, grad_features) = refs[:-2], refs[-2:]
     hidden[...] = own_hidden[...]
-    side, half = mine.shape[0], grad_weight.shape[0] // 2
-    own, other = blocks[: len(blocks) // 2], blocks[len(blocks) // 2 :]
+    side = mine.shape[0]
     total = mine[...]
-    for block in own[1:]:
+    for block in blocks:
         total = total + block[0:side].astype(F32)
     grad_features[...] = total.astype(BF16)
-    for shift, group in enumerate((own, other)):
+
+
+def weight_results_kernel(own, other, grad_weight, grad_bias):
+    half = grad_weight.shape[0] // 2
+    for shift, block in enumerate((own, other)):
         start = pl.multiple_of((lax.axis_index("row") % 2 ^ shift) * half, half)
-        grad_weight[pl.ds(start, half), :] = scale * tree_sum(
-            b[side : side + half].astype(F32) for b in group
-        )
-    grad_bias[...] = scale * tree_sum(joined(b[side + half : side + half + PAD]) for b in own)
+        grad_weight[pl.ds(start, half), :] = block[0:half]
+    grad_bias[...] = own[half : half + 1]
 
 
 def call(kernel, name, outs, scratch, ints, *arrays):
@@ -320,20 +330,32 @@
         *map(near, (kept_back, kept_weight, sent, came)),
     )
     line = [parts[0]] + [exchange(part, "row", 2 * m) for m, part in enumerate(parts, 1)]
-    other = [exchange(block, "row", 1) for block in line]
     scale = 1.0 / math.sqrt(n_row * n_col * side)
-    hidden, grad_features, grad_weight, grad_bias = call(
-        functools.partial(line_kernel, scale),
-        "line_sums",
-        [
-            ((side, width), BF16, False),
-            ((side, width), BF16, False),
-            ((width, width), F32, False),
-            ((1, width), F32, False),
-        ],
-        [],
-        [],
-        *map(near, (hidden, mine, *line, *other)),
+    (weights,) = call(
+        functools.partial(line_weight_kernel, scale),
+        "line_weight",
+        [((half + 8, width), F32, True)],
+        [],
+        [],
+        *map(near, line),
+    )
+    other_weights = exchange(weights, "row", 1)
+    hidden, grad_features = call(
+        node_results_kernel,
+        "node_results",
+        [((side, width), BF16, False), ((side, width), BF16, False)],
+        [],
+        [],
+        *map(near, (hidden, mine, *line[1:])),
+    )
+    grad_weight, grad_bias = call(
+        weight_results_kernel,
+        "weight_results",
+        [((width, width), F32, False), ((1, width), F32, False)],
+        [],
+        [],
+        near(weights),
+        near(other_weights),
     )
     return (hidden[None], grad_weight, grad_bias[0], grad_features[None])
 

time: 45.7 us -> 45.4 us (level)
  Pallas kernels: 3.36 us -> 4 us
    pallas_call x6 -> x8, Pallas kernels: 3.36 us -> 4 us  [call(): pl.pallas_call(kernel, name=name, out_shape=[space(dtype)(shape, dtype) i...]
    ppermute x17 -> x14, starting transfers between devices: 14.3 us -> 13.9 us  [exchange(): return lax.ppermute(value, axis, [(i, i ^ mask) for i in range(size)])]
    ppermute x17 -> x14, waiting for transfers between devices: 14.2 us -> 14 us  [exchange(): return lax.ppermute(value, axis, [(i, i ^ mask) for i in range(size)])]
  transfers between devices with their start and end apart: 17 -> 14, of which waited for: 7 -> 5; matrix products, arithmetic and copies ran while one was open for 0% -> 0% of each run, Pallas kernels for 3% -> 4%
where the time goes in v6:
time: 45.4 us; the launch traced here: 45 us
  waiting for transfers between devices  14 us (31%)
  starting transfers between devices  13.9 us (31%)
  blocking collectives  11.7 us (26%)
  Pallas kernels  4 us (9%)
  between operations  1.41 us (3%)
    ppermute x14, waiting for transfers between devices, exchange(): return lax.ppermute(value, axis, [(i, i ^ mask) for i in range(size)])  14 us
    ppermute x14, starting transfers between devices, exchange(): return lax.ppermute(value, axis, [(i, i ^ mask) for i in range(size)])  13.9 us
    all_gather x1, blocking collectives, on_device(): products = lax.all_gather(product, 'col')  11.7 us
    pallas_call x8, Pallas kernels, call(): pl.pallas_call(kernel, name=name, out_shape=[space(dtype)(shape, dtype) i...  4 us
  transfers between devices with their start and end apart: 14, of which 5 were waited for; matrix products, arithmetic and copies ran while one was open for 0% of the time, Pallas kernels for 4%

profile of v6, /device:TPU:0, one launch (start us, length us, event | category | flops | bytes accessed | tf_op | source)
XLA Modules:
  0.0 45.0 jit_solution(17239217580238982539)
XLA Ops:
  0.6 5.1 %collective-permute-start.5 = (bf16[128,256]{1,0:T(8,128)(2,1)}, bf16[128,256]{1,0:T(8,128)(2,1)S(1)}, u32[]{:S(2)}, u32[]{:S(2)}) collective-permute-start(bf16[128,256]{1,0:T(8,128)(2,1)} %bitcast.15), channel_id=1, source_target_pairs={{0,24},{4,28},{8,16},{12,20},{16,8},{20,12},{24,0},{28,4},{1,25},{... | collective-permute-start | bytes 196616 | tf_op jit(solution)/shard_map/ppermute | solution.py:28
  5.8 0.6 %collective-permute-start.1 = (bf16[128,256]{1,0:T(8,128)(2,1)}, bf16[128,256]{1,0:T(8,128)(2,1)S(1)}, u32[]{:S(2)}, u32[]{:S(2)}) collective-permute-start(bf16[128,256]{1,0:T(8,128)(2,1)} %bitcast.17), channel_id=1, source_target_pairs={{0,8},{4,12},{8,0},{12,4},{16,24},{20,28},{24,16},{28,20},{1,9},{5... | collective-permute-start | bytes 196616 | tf_op jit(solution)/shard_map/ppermute | solution.py:28
  6.4 1.0 %masked_cotangent.1 = (bf16[144,256]{1,0:T(8,128)(2,1)S(1)}, f32[1,256]{1,0:T(1,128)S(1)}, s32[6]{0:T(128)S(4)}) custom-call(s32[3]{0:T(128)} %bitcast.22, s32[3]{0:T(128)} %bitcast.23, s32[1,128]{1,0:T(1,128)} %mask.1, bf16[128,256]{1,0:T(8,128)(2,1)} %bitcast.20, f32[1,256]{1,0:T(1,128)} %bitcast.21), custom_call_target="tpu_custom_call" | custom-call | tf_op jit(solution)/shard_map/masked_cotangent/pallas_call | solution.py:218
  7.4 1.7 %collective-permute-start.7 = (bf16[144,256]{1,0:T(8,128)(2,1)S(1)}, bf16[144,256]{1,0:T(8,128)(2,1)S(1)}, u32[]{:S(2)}, u32[]{:S(2)}) collective-permute-start(bf16[144,256]{1,0:T(8,128)(2,1)S(1)} %get-tuple-element.33.refs_0_.refs_6_), channel_id=1, source_target_pairs={{0,1},{1,0},{2,3},{3,2},{4,5},{5,4},{6,7},{7,6},{8,9},{9,8},{10,11... | collective-permute-start | bytes 221192 | tf_op jit(solution)/shard_map/ppermute | solution.py:28
  9.8 0.0 copy-start
  9.8 0.6 %collective-permute-start.6 = (bf16[128,256]{1,0:T(8,128)(2,1)S(1)}, bf16[128,256]{1,0:T(8,128)(2,1)S(1)}, u32[]{:S(2)}, u32[]{:S(2)}) collective-permute-start(bf16[128,256]{1,0:T(8,128)(2,1)S(1)} %collective-permute-done.5.refs_6_), channel_id=1, source_target_pairs={{0,4},{4,0},{8,12},{12,8},{16,20},{20,16},{24,28},{28,24},{1,5},{5... | collective-permute-start | bytes 196616 | tf_op jit(solution)/shard_map/ppermute | solution.py:28
  10.4 1.2 %collective-permute-done.3.refs_4_ = bf16[128,256]{1,0:T(8,128)(2,1)S(1)} collective-permute-done((bf16[128,256]{1,0:T(8,128)(2,1)}, bf16[128,256]{1,0:T(8,128)(2,1)S(1)}, u32[]{:S(2)}, u32[]{:S(2)}) %collective-permute-start.3) | collective-permute-done | bytes 65568 | tf_op jit(solution)/shard_map/ppermute | solution.py:28
  11.6 0.5 %collective-permute-start.2 = (bf16[128,256]{1,0:T(8,128)(2,1)S(1)}, bf16[128,256]{1,0:T(8,128)(2,1)S(1)}, u32[]{:S(2)}, u32[]{:S(2)}) collective-permute-start(bf16[128,256]{1,0:T(8,128)(2,1)S(1)} %collective-permute-done.1.refs_2_), channel_id=1, source_target_pairs={{0,4},{4,0},{8,12},{12,8},{16,20},{20,16},{24,28},{28,24},{1,5},{5... | collective-permute-start | bytes 196616 | tf_op jit(solution)/shard_map/ppermute | solution.py:28
  12.1 1.6 %collective-permute-start.8 = (bf16[288,256]{1,0:T(8,128)(2,1)S(1)}, bf16[288,256]{1,0:T(8,128)(2,1)S(1)}, u32[]{:S(2)}, u32[]{:S(2)}) collective-permute-start(bf16[288,256]{1,0:T(8,128)(2,1)S(1)} %cotangents_so_far.1), channel_id=1, source_target_pairs={{0,2},{1,3},{2,0},{3,1},{4,6},{5,7},{6,4},{7,5},{8,10},{9,11},{10,... | collective-permute-start | bytes 442376 | tf_op jit(solution)/shard_map/ppermute | solution.py:28
  13.7 0.2 tile_products.1
  14.0 11.7 %all-gather = bf16[1536,256]{1,0:T(8,128)(2,1)S(1)} all-gather(bf16[384,256]{1,0:T(8,128)(2,1)S(1)} %get-tuple-element.32), channel_id=2, replica_groups=mesh['row'=8,'col'=4] {'col'}, dimensions={0}, use_global_device_ids=true | all-gather | bytes 983040 | tf_op jit(solution)/shard_map/all_gather | solution.py:295
  25.7 1.2 %dense_layer.1 = (bf16[128,256]{1,0:T(8,128)(2,1)S(1)}, bf16[656,256]{1,0:T(8,128)(2,1)S(1)}, f32[512,256]{1,0:T(8,128)S(1)}, f32[128,256]{1,0:T(8,128)S(1)}) custom-call(s32[6]{0:T(128)S(4)} %get-tuple-element.25.ints.refs_0_, s32[2]{0:T(128)S(4)} %get-tuple-element.30.refs_1_, bf16[256,256]{1,0:T(8,128)(2,1)S(1)} %copy-done.1, ...), custom_call_target="tpu_custom_call" | custom-call | tf_op jit(solution)/shard_map/dense_layer/pallas_call | solution.py:218
  26.9 0.1 collective-permute-start.9
  27.0 1.6 %collective-permute-done.9.came = bf16[656,256]{1,0:T(8,128)(2,1)S(1)} collective-permute-done((bf16[656,256]{1,0:T(8,128)(2,1)S(1)}, bf16[656,256]{1,0:T(8,128)(2,1)S(1)}, u32[]{:S(2)}, u32[]{:S(2)}) %collective-permute-start.9) | collective-permute-done | bytes 335904 | tf_op jit(solution)/shard_map/ppermute | solution.py:28
  28.7 0.1 chip_sums.1
  28.7 1.6 %collective-permute-start.11 = (bf16[272,256]{1,0:T(8,128)(2,1)S(1)}, bf16[272,256]{1,0:T(8,128)(2,1)S(1)}, u32[]{:S(2)}, u32[]{:S(2)}) collective-permute-start(bf16[272,256]{1,0:T(8,128)(2,1)S(1)} %get-tuple-element.40), channel_id=1, source_target_pairs={{0,16},{4,20},{8,24},{12,28},{16,0},{20,4},{24,8},{28,12},{1,17},{... | collective-permute-start | bytes 417800 | tf_op jit(solution)/shard_map/ppermute | solution.py:28
  30.3 1.6 %collective-permute-start.12 = (bf16[272,256]{1,0:T(8,128)(2,1)S(1)}, bf16[272,256]{1,0:T(8,128)(2,1)S(1)}, u32[]{:S(2)}, u32[]{:S(2)}) collective-permute-start(bf16[272,256]{1,0:T(8,128)(2,1)S(1)} %get-tuple-element.41), channel_id=1, source_target_pairs={{0,24},{4,28},{8,16},{12,20},{16,8},{20,12},{24,0},{28,4},{1,25},{... | collective-permute-start | bytes 417800 | tf_op jit(solution)/shard_map/ppermute | solution.py:28
  31.9 0.4 collective-permute-start.10
  32.3 9.5 %collective-permute-done.11.refs_1_.refs_2_ = bf16[272,256]{1,0:T(8,128)(2,1)S(1)} collective-permute-done((bf16[272,256]{1,0:T(8,128)(2,1)S(1)}, bf16[272,256]{1,0:T(8,128)(2,1)S(1)}, u32[]{:S(2)}, u32[]{:S(2)}) %collective-permute-start.11) | collective-permute-done | bytes 139296 | tf_op jit(solution)/shard_map/ppermute | solution.py:28
  41.8 1.0 %collective-permute-done.10.refs_0_.refs_1_ = bf16[272,256]{1,0:T(8,128)(2,1)S(1)} collective-permute-done((bf16[272,256]{1,0:T(8,128)(2,1)S(1)}, bf16[272,256]{1,0:T(8,128)(2,1)S(1)}, u32[]{:S(2)}, u32[]{:S(2)}) %collective-permute-start.10) | collective-permute-done | bytes 139296 | tf_op jit(solution)/shard_map/ppermute | solution.py:28
  42.9 0.1 collective-permute-start.13
  42.9 0.7 %node_results.1 = (bf16[128,256]{1,0:T(8,128)(2,1)}, bf16[128,256]{1,0:T(8,128)(2,1)}) custom-call(bf16[128,256]{1,0:T(8,128)(2,1)S(1)} %get-tuple-element.34.own_hidden, f32[128,256]{1,0:T(8,128)S(1)} %get-tuple-element.38.mine, bf16[272,256]{1,0:T(8,128)(2,1)S(1)} %collective-permute-done.10.refs_0_.refs_1_, ...), custom_call_target="tpu_custom_call" | custom-call | tf_op jit(solution)/shard_map/node_results/pallas_call | solution.py:218
  43.6 0.7 %collective-permute-done.13.other = f32[136,256]{1,0:T(8,128)S(1)} collective-permute-done((f32[136,256]{1,0:T(8,128)S(1)}, f32[136,256]{1,0:T(8,128)S(1)}, u32[]{:S(2)}, u32[]{:S(2)}) %collective-permute-start.13) | collective-permute-done | bytes 139296 | tf_op jit(solution)/shard_map/ppermute | solution.py:28
  44.3 0.7 %weight_results.1 = (f32[256,256]{1,0:T(8,128)}, f32[1,256]{1,0:T(1,128)}) custom-call(f32[136,256]{1,0:T(8,128)S(1)} %line_weight.1.own, f32[136,256]{1,0:T(8,128)S(1)} %collective-permute-done.13.other), custom_call_target="tpu_custom_call" | custom-call | tf_op jit(solution)/shard_map/weight_results/pallas_call | solution.py:218
  (20 shorter events, 0.1 us)
Async XLA Ops:
  0.6 8.5 %copy-start.2 = (bf16[1,128,256]{2,1,0:T(8,128)(2,1)S(1)}, bf16[1,128,256]{2,1,0:T(8,128)(2,1)}, u32[]{:S(2)}) copy-start(bf16[1,128,256]{2,1,0:T(8,128)(2,1)} %param.9) | copy-start | bytes 196612
  0.6 9.1 %collective-permute-start.5 = (bf16[128,256]{1,0:T(8,128)(2,1)}, bf16[128,256]{1,0:T(8,128)(2,1)S(1)}, u32[]{:S(2)}, u32[]{:S(2)}) collective-permute-start(bf16[128,256]{1,0:T(8,128)(2,1)} %bitcast.15), channel_id=1, source_target_pairs={{0,24},{4,28},{8,16},{12,20},{16,8},{20,12},{24,0},{28,4},{1,25},{... | collective-permute-start | bytes 196616 | tf_op jit(solution)/shard_map/ppermute | solution.py:28
  5.8 5.8 %collective-permute-start.3 = (bf16[128,256]{1,0:T(8,128)(2,1)}, bf16[128,256]{1,0:T(8,128)(2,1)S(1)}, u32[]{:S(2)}, u32[]{:S(2)}) collective-permute-start(bf16[128,256]{1,0:T(8,128)(2,1)} %bitcast.16), channel_id=1, source_target_pairs={{0,16},{4,20},{8,24},{12,28},{16,0},{20,4},{24,8},{28,12},{1,17},{... | collective-permute-start | bytes 196616 | tf_op jit(solution)/shard_map/ppermute | solution.py:28
  5.8 5.8 %collective-permute-start.1 = (bf16[128,256]{1,0:T(8,128)(2,1)}, bf16[128,256]{1,0:T(8,128)(2,1)S(1)}, u32[]{:S(2)}, u32[]{:S(2)}) collective-permute-start(bf16[128,256]{1,0:T(8,128)(2,1)} %bitcast.17), channel_id=1, source_target_pairs={{0,8},{4,12},{8,0},{12,4},{16,24},{20,28},{24,16},{28,20},{1,9},{5... | collective-permute-start | bytes 196616 | tf_op jit(solution)/shard_map/ppermute | solution.py:28
  7.4 4.7 %collective-permute-start.7 = (bf16[144,256]{1,0:T(8,128)(2,1)S(1)}, bf16[144,256]{1,0:T(8,128)(2,1)S(1)}, u32[]{:S(2)}, u32[]{:S(2)}) collective-permute-start(bf16[144,256]{1,0:T(8,128)(2,1)S(1)} %get-tuple-element.33.refs_0_.refs_6_), channel_id=1, source_target_pairs={{0,1},{1,0},{2,3},{3,2},{4,5},{5,4},{6,7},{7,6},{8,9},{9,8},{10,11... | collective-permute-start | bytes 221192 | tf_op jit(solution)/shard_map/ppermute | solution.py:28
  9.1 4.6 %collective-permute-start = (bf16[128,256]{1,0:T(8,128)(2,1)S(1)}, bf16[128,256]{1,0:T(8,128)(2,1)S(1)}, u32[]{:S(2)}, u32[]{:S(2)}) collective-permute-start(bf16[128,256]{1,0:T(8,128)(2,1)S(1)} %bitcast.18), channel_id=1, source_target_pairs={{0,4},{4,0},{8,12},{12,8},{16,20},{20,16},{24,28},{28,24},{1,5},{5... | collective-permute-start | bytes 196616 | tf_op jit(solution)/shard_map/ppermute | solution.py:28
  9.8 3.9 %copy-start = (bf16[1,1,3,128,128]{4,3,2,1,0:T(8,128)(2,1)S(1)}, bf16[1,1,3,128,128]{4,3,2,1,0:T(8,128)(2,1)}, u32[]{:S(2)}) copy-start(bf16[1,1,3,128,128]{4,3,2,1,0:T(8,128)(2,1)} %param.10) | copy-start | bytes 294916
  9.8 3.9 %collective-permute-start.6 = (bf16[128,256]{1,0:T(8,128)(2,1)S(1)}, bf16[128,256]{1,0:T(8,128)(2,1)S(1)}, u32[]{:S(2)}, u32[]{:S(2)}) collective-permute-start(bf16[128,256]{1,0:T(8,128)(2,1)S(1)} %collective-permute-done.5.refs_6_), channel_id=1, source_target_pairs={{0,4},{4,0},{8,12},{12,8},{16,20},{20,16},{24,28},{28,24},{1,5},{5... | collective-permute-start | bytes 196616 | tf_op jit(solution)/shard_map/ppermute | solution.py:28
  11.6 2.1 %collective-permute-start.4 = (bf16[128,256]{1,0:T(8,128)(2,1)S(1)}, bf16[128,256]{1,0:T(8,128)(2,1)S(1)}, u32[]{:S(2)}, u32[]{:S(2)}) collective-permute-start(bf16[128,256]{1,0:T(8,128)(2,1)S(1)} %collective-permute-done.3.refs_4_), channel_id=1, source_target_pairs={{0,4},{4,0},{8,12},{12,8},{16,20},{20,16},{24,28},{28,24},{1,5},{5... | collective-permute-start | bytes 196616 | tf_op jit(solution)/shard_map/ppermute | solution.py:28
  11.6 2.1 %collective-permute-start.2 = (bf16[128,256]{1,0:T(8,128)(2,1)S(1)}, bf16[128,256]{1,0:T(8,128)(2,1)S(1)}, u32[]{:S(2)}, u32[]{:S(2)}) collective-permute-start(bf16[128,256]{1,0:T(8,128)(2,1)S(1)} %collective-permute-done.1.refs_2_), channel_id=1, source_target_pairs={{0,4},{4,0},{8,12},{12,8},{16,20},{20,16},{24,28},{28,24},{1,5},{5... | collective-permute-start | bytes 196616 | tf_op jit(solution)/shard_map/ppermute | solution.py:28
  12.1 13.6 %collective-permute-start.8 = (bf16[288,256]{1,0:T(8,128)(2,1)S(1)}, bf16[288,256]{1,0:T(8,128)(2,1)S(1)}, u32[]{:S(2)}, u32[]{:S(2)}) collective-permute-start(bf16[288,256]{1,0:T(8,128)(2,1)S(1)} %cotangents_so_far.1), channel_id=1, source_target_pairs={{0,2},{1,3},{2,0},{3,1},{4,6},{5,7},{6,4},{7,5},{8,10},{9,11},{10,... | collective-permute-start | bytes 442376 | tf_op jit(solution)/shard_map/ppermute | solution.py:28
  14.0 11.7 %copy-start.1 = (bf16[256,256]{1,0:T(8,128)(2,1)S(1)}, bf16[256,256]{1,0:T(8,128)(2,1)}, u32[]{:S(2)}) copy-start(bf16[256,256]{1,0:T(8,128)(2,1)} %refs_2_.1) | copy-start | bytes 393220
  26.9 1.7 %collective-permute-start.9 = (bf16[656,256]{1,0:T(8,128)(2,1)S(1)}, bf16[656,256]{1,0:T(8,128)(2,1)S(1)}, u32[]{:S(2)}, u32[]{:S(2)}) collective-permute-start(bf16[656,256]{1,0:T(8,128)(2,1)S(1)} %get-tuple-element.37.own_sent), channel_id=1, source_target_pairs={{0,4},{4,0},{8,12},{12,8},{16,20},{20,16},{24,28},{28,24},{1,5},{5... | collective-permute-start | bytes 1007624 | tf_op jit(solution)/shard_map/ppermute | solution.py:28
  28.7 13.1 %collective-permute-start.11 = (bf16[272,256]{1,0:T(8,128)(2,1)S(1)}, bf16[272,256]{1,0:T(8,128)(2,1)S(1)}, u32[]{:S(2)}, u32[]{:S(2)}) collective-permute-start(bf16[272,256]{1,0:T(8,128)(2,1)S(1)} %get-tuple-element.40), channel_id=1, source_target_pairs={{0,16},{4,20},{8,24},{12,28},{16,0},{20,4},{24,8},{28,12},{1,17},{... | collective-permute-start | bytes 417800 | tf_op jit(solution)/shard_map/ppermute | solution.py:28
  30.3 11.5 %collective-permute-start.12 = (bf16[272,256]{1,0:T(8,128)(2,1)S(1)}, bf16[272,256]{1,0:T(8,128)(2,1)S(1)}, u32[]{:S(2)}, u32[]{:S(2)}) collective-permute-start(bf16[272,256]{1,0:T(8,128)(2,1)S(1)} %get-tuple-element.41), channel_id=1, source_target_pairs={{0,24},{4,28},{8,16},{12,20},{16,8},{20,12},{24,0},{28,4},{1,25},{... | collective-permute-start | bytes 417800 | tf_op jit(solution)/shard_map/ppermute | solution.py:28
  31.9 10.9 %collective-permute-start.10 = (bf16[272,256]{1,0:T(8,128)(2,1)S(1)}, bf16[272,256]{1,0:T(8,128)(2,1)S(1)}, u32[]{:S(2)}, u32[]{:S(2)}) collective-permute-start(bf16[272,256]{1,0:T(8,128)(2,1)S(1)} %get-tuple-element.39.refs_0_), channel_id=1, source_target_pairs={{0,8},{4,12},{8,0},{12,4},{16,24},{20,28},{24,16},{28,20},{1,9},{5... | collective-permute-start | bytes 417800 | tf_op jit(solution)/shard_map/ppermute | solution.py:28
  42.9 1.4 %collective-permute-start.13 = (f32[136,256]{1,0:T(8,128)S(1)}, f32[136,256]{1,0:T(8,128)S(1)}, u32[]{:S(2)}, u32[]{:S(2)}) collective-permute-start(f32[136,256]{1,0:T(8,128)S(1)} %line_weight.1.own), channel_id=1, source_target_pairs={{0,4},{4,0},{8,12},{12,8},{16,20},{20,16},{24,28},{28,24},{1,5},{5... | collective-permute-start | bytes 417800 | tf_op jit(solution)/shard_map/ppermute | solution.py:28

commit v7 on v6

--- a/solution.py
+++ b/solution.py
@@ -26,6 +26,30 @@
 def exchange(value, axis, mask):
     size = lax.axis_size(axis)
     return lax.ppermute(value, axis, [(i, i ^ mask) for i in range(size)])
+
+
+def column_mask(core, q, n_col):
+    if n_col < 4 or core == 0:
+        return q
+    return q - q % 4 + (0, 2, 1, 3)[q % 4]
+
+
+def column_exchange(value, q):
+    rows, cols = lax.axis_size("row"), lax.axis_size("col")
+    pairs = [(r * cols + c, r * cols + (c ^ column_mask(r % 2, q, cols))) for r in range(rows) for c in range(cols)]
+    return lax.ppermute(value, ("row", "col"), pairs)
+
+
+def line_mask(core, m, n_line):
+    if n_line < 4 or core == 0:
+        return m
+    return m - m % 4 + (0, 1, 3, 2)[m % 4]
+
+
+def line_exchange(value, m):
+    size = lax.axis_size("row")
+    pairs = [(i, i ^ 2 * line_mask(i % 2, m, size // 2)) for i in range(size)]
+    return lax.ppermute(value, "row", pairs)
 
 
 def tree_sum(terms):
@@ -118,20 +142,24 @@
         first = (q - (1 << step >> 1)) * each_rows
         return cots[step][first + start : first + stop]
 
+    second = me_row % 2
+    places_of = [
+        me_col ^ jnp.where(second == 1, column_mask(1, q, n_col), column_mask(0, q, n_col))
+        for q in range(n_col)
+    ]
     for q in range(n_col):
         places = cotangent(q, side, each_rows)[:, 0:128].astype(F32).astype(jnp.int32)
         for p in range(blocks):
-            target[q, p] = jnp.max(places[p : p + 1])
+            target[places_of[q], p] = jnp.max(places[p : p + 1])
     total[...] = jnp.zeros_like(total)
 
     def add(i):
         c, p = i // blocks, i % blocks
-        q = me_col ^ c
-        total[target[q, p]] += products[c, pl.ds(p * side, side), :].astype(F32)
+        total[target[c, p]] += products[c, pl.ds(p * side, side), :].astype(F32)
 
     each(n_col * blocks, add)
     for q in range(n_col):
-        t = me_col ^ q
+        t = places_of[q]
         rows = pl.ds(pl.multiple_of(t * side, side), side)
         aggregated = total[t].astype(BF16)
         agg[rows, :] = aggregated
@@ -175,9 +203,11 @@
     weights = (kept_weight[...] + came[after : after + half].astype(F32)).astype(BF16)
     ends = slice(after + half, after + half + PAD)
     column_sum = two_halves(joined(own_sent[ends]) + joined(came[ends]))
+    n_line, second = len(outs) + 1, lax.axis_index("row") % 2
     for m, out in enumerate(outs, 1):
-        part = slice(m * side, (m + 1) * side)
-        out[0:side] = (kept[part] + came[part].astype(F32)).astype(BF16)
+        chosen = jnp.where(second == 1, line_mask(1, m, n_line), line_mask(0, m, n_line))
+        part = pl.ds(pl.multiple_of(chosen * side, side), side)
+        out[0:side] = (kept[part, :] + came[part, :].astype(F32)).astype(BF16)
         out[side : side + half] = weights
         out[side + half : side + half + PAD] = column_sum
 
@@ -274,7 +304,7 @@
             [],
             *map(near, cots),
         ) if reach > 1 else cots
-        cots, reach = cots + [exchange(held, "col", reach)], 2 * reach
+        cots, reach = cots + [column_exchange(held, reach)], 2 * reach
 
     sources = [own, exchange(own, "row", 1)]
     tile_count, _ = lax.optimization_barrier((tile_count, sources[1]))
@@ -329,7 +359,7 @@
         [],
         *map(near, (kept_back, kept_weight, sent, came)),
     )
-    line = [parts[0]] + [exchange(part, "row", 2 * m) for m, part in enumerate(parts, 1)]
+    line = [parts[0]] + [line_exchange(part, m) for m, part in enumerate(parts, 1)]
     scale = 1.0 / math.sqrt(n_row * n_col * side)
     (weights,) = call(
         functools.partial(line_weight_kernel, scale),

time: 45.4 us -> 44.6 us (0.982)
  waiting for transfers between devices: 14 us -> 13.4 us
  blocking collectives: 11.7 us -> 11.2 us
  starting transfers between devices: 13.9 us -> 14.4 us
    ppermute x14 -> x9, waiting for transfers between devices: 14 us -> 3.52 us  [exchange(): return lax.ppermute(value, axis, [(i, i ^ mask) for i in range(size)])]
    ppermute x0 -> x5, waiting for transfers between devices: none -> 9.84 us  [the longest x3 9.84 us: line_exchange(): return lax.ppermute(value, 'row', pairs)]
    ppermute x0 -> x5, starting transfers between devices: none -> 7.4 us  [the longest x3 4.11 us: line_exchange(): return lax.ppermute(value, 'row', pairs)]
    ppermute x14 -> x9, starting transfers between devices: 13.9 us -> 6.98 us  [exchange(): return lax.ppermute(value, axis, [(i, i ^ mask) for i in range(size)])]
    all_gather x1, blocking collectives: 11.7 us -> 11.2 us  [on_device(): products = lax.all_gather(product, 'col')]
where the time goes in v7:
time: 44.6 us; the launch traced here: 44.4 us
  starting transfers between devices  14.4 us (32%)
  waiting for transfers between devices  13.4 us (30%)
  blocking collectives  11.2 us (25%)
  Pallas kernels  4 us (9%)
  between operations  1.4 us (3%)
    all_gather x1, blocking collectives, on_device(): products = lax.all_gather(product, 'col')  11.2 us
    ppermute x3, waiting for transfers between devices, line_exchange(): return lax.ppermute(value, 'row', pairs)  9.84 us
    ppermute x9, starting transfers between devices, exchange(): return lax.ppermute(value, axis, [(i, i ^ mask) for i in range(size)])  6.98 us
    ppermute x3, starting transfers between devices, line_exchange(): return lax.ppermute(value, 'row', pairs)  4.11 us
    pallas_call x8, Pallas kernels, call(): pl.pallas_call(kernel, name=name, out_shape=[space(dtype)(shape, dtype) i...  4 us
    ppermute x9, waiting for transfers between devices, exchange(): return lax.ppermute(value, axis, [(i, i ^ mask) for i in range(size)])  3.52 us
    ppermute x2, starting transfers between devices, column_exchange(): return lax.ppermute(value, ('row', 'col'), pairs)  3.29 us
  transfers between devices with their start and end apart: 14, of which 5 were waited for; matrix products, arithmetic and copies ran while one was open for 0% of the time, Pallas kernels for 4%

profile of v7, /device:TPU:0, one launch (start us, length us, event | category | flops | bytes accessed | tf_op | source)
XLA Modules:
  0.0 44.4 jit_solution(9105341397767400794)
XLA Ops:
  0.6 5.1 %collective-permute-start.5 = (bf16[128,256]{1,0:T(8,128)(2,1)}, bf16[128,256]{1,0:T(8,128)(2,1)S(1)}, u32[]{:S(2)}, u32[]{:S(2)}) collective-permute-start(bf16[128,256]{1,0:T(8,128)(2,1)} %bitcast.15), channel_id=1, source_target_pairs={{0,24},{4,28},{8,16},{12,20},{16,8},{20,12},{24,0},{28,4},{1,25},{... | collective-permute-start | bytes 196616 | tf_op jit(solution)/shard_map/ppermute | solution.py:28
  5.8 0.6 %collective-permute-start.1 = (bf16[128,256]{1,0:T(8,128)(2,1)}, bf16[128,256]{1,0:T(8,128)(2,1)S(1)}, u32[]{:S(2)}, u32[]{:S(2)}) collective-permute-start(bf16[128,256]{1,0:T(8,128)(2,1)} %bitcast.17), channel_id=1, source_target_pairs={{0,8},{4,12},{8,0},{12,4},{16,24},{20,28},{24,16},{28,20},{1,9},{5... | collective-permute-start | bytes 196616 | tf_op jit(solution)/shard_map/ppermute | solution.py:28
  6.4 1.0 %masked_cotangent.1 = (bf16[144,256]{1,0:T(8,128)(2,1)S(1)}, f32[1,256]{1,0:T(1,128)S(1)}, s32[6]{0:T(128)S(4)}) custom-call(s32[3]{0:T(128)} %bitcast.22, s32[3]{0:T(128)} %bitcast.23, s32[1,128]{1,0:T(1,128)} %mask.1, bf16[128,256]{1,0:T(8,128)(2,1)} %bitcast.20, f32[1,256]{1,0:T(1,128)} %bitcast.21), custom_call_target="tpu_custom_call" | custom-call | tf_op jit(solution)/shard_map/masked_cotangent/pallas_call | solution.py:248
  7.4 1.7 %collective-permute-start.7 = (bf16[144,256]{1,0:T(8,128)(2,1)S(1)}, bf16[144,256]{1,0:T(8,128)(2,1)S(1)}, u32[]{:S(2)}, u32[]{:S(2)}) collective-permute-start(bf16[144,256]{1,0:T(8,128)(2,1)S(1)} %get-tuple-element.33.refs_0_.refs_6_), channel_id=1, source_target_pairs={{0,1},{1,0},{2,3},{3,2},{4,6},{5,7},{6,4},{7,5},{8,9},{9,8},{10,11... | collective-permute-start | bytes 221192 | tf_op jit(solution)/shard_map/ppermute | solution.py:40
  9.8 0.0 copy-start
  9.8 0.6 %collective-permute-start.6 = (bf16[128,256]{1,0:T(8,128)(2,1)S(1)}, bf16[128,256]{1,0:T(8,128)(2,1)S(1)}, u32[]{:S(2)}, u32[]{:S(2)}) collective-permute-start(bf16[128,256]{1,0:T(8,128)(2,1)S(1)} %collective-permute-done.5.refs_6_), channel_id=1, source_target_pairs={{0,4},{4,0},{8,12},{12,8},{16,20},{20,16},{24,28},{28,24},{1,5},{5... | collective-permute-start | bytes 196616 | tf_op jit(solution)/shard_map/ppermute | solution.py:28
  10.4 1.2 %collective-permute-done.3.refs_4_ = bf16[128,256]{1,0:T(8,128)(2,1)S(1)} collective-permute-done((bf16[128,256]{1,0:T(8,128)(2,1)}, bf16[128,256]{1,0:T(8,128)(2,1)S(1)}, u32[]{:S(2)}, u32[]{:S(2)}) %collective-permute-start.3) | collective-permute-done | bytes 65568 | tf_op jit(solution)/shard_map/ppermute | solution.py:28
  11.6 0.5 %collective-permute-start.2 = (bf16[128,256]{1,0:T(8,128)(2,1)S(1)}, bf16[128,256]{1,0:T(8,128)(2,1)S(1)}, u32[]{:S(2)}, u32[]{:S(2)}) collective-permute-start(bf16[128,256]{1,0:T(8,128)(2,1)S(1)} %collective-permute-done.1.refs_2_), channel_id=1, source_target_pairs={{0,4},{4,0},{8,12},{12,8},{16,20},{20,16},{24,28},{28,24},{1,5},{5... | collective-permute-start | bytes 196616 | tf_op jit(solution)/shard_map/ppermute | solution.py:28
  12.1 1.6 %collective-permute-start.8 = (bf16[288,256]{1,0:T(8,128)(2,1)S(1)}, bf16[288,256]{1,0:T(8,128)(2,1)S(1)}, u32[]{:S(2)}, u32[]{:S(2)}) collective-permute-start(bf16[288,256]{1,0:T(8,128)(2,1)S(1)} %cotangents_so_far.1), channel_id=1, source_target_pairs={{0,2},{1,3},{2,0},{3,1},{4,5},{5,4},{6,7},{7,6},{8,10},{9,11},{10,... | collective-permute-start | bytes 442376 | tf_op jit(solution)/shard_map/ppermute | solution.py:40
  13.7 0.2 tile_products.1
  14.0 11.2 %all-gather = bf16[1536,256]{1,0:T(8,128)(2,1)S(1)} all-gather(bf16[384,256]{1,0:T(8,128)(2,1)S(1)} %get-tuple-element.32), channel_id=2, replica_groups=mesh['row'=8,'col'=4] {'col'}, dimensions={0}, use_global_device_ids=true | all-gather | bytes 983040 | tf_op jit(solution)/shard_map/all_gather | solution.py:325
  25.2 1.2 %dense_layer.1 = (bf16[128,256]{1,0:T(8,128)(2,1)S(1)}, bf16[656,256]{1,0:T(8,128)(2,1)S(1)}, f32[512,256]{1,0:T(8,128)S(1)}, f32[128,256]{1,0:T(8,128)S(1)}) custom-call(s32[6]{0:T(128)S(4)} %get-tuple-element.25.ints.refs_0_, s32[2]{0:T(128)S(4)} %get-tuple-element.30.refs_1_, bf16[256,256]{1,0:T(8,128)(2,1)S(1)} %copy-done.1, ...), custom_call_target="tpu_custom_call" | custom-call | tf_op jit(solution)/shard_map/dense_layer/pallas_call | solution.py:248
  26.5 0.1 collective-permute-start.9
  26.5 1.6 %collective-permute-done.9.came = bf16[656,256]{1,0:T(8,128)(2,1)S(1)} collective-permute-done((bf16[656,256]{1,0:T(8,128)(2,1)S(1)}, bf16[656,256]{1,0:T(8,128)(2,1)S(1)}, u32[]{:S(2)}, u32[]{:S(2)}) %collective-permute-start.9) | collective-permute-done | bytes 335904 | tf_op jit(solution)/shard_map/ppermute | solution.py:28
  28.2 0.1 chip_sums.1
  28.2 2.1 %collective-permute-start.11 = (bf16[272,256]{1,0:T(8,128)(2,1)S(1)}, bf16[272,256]{1,0:T(8,128)(2,1)S(1)}, u32[]{:S(2)}, u32[]{:S(2)}) collective-permute-start(bf16[272,256]{1,0:T(8,128)(2,1)S(1)} %get-tuple-element.40), channel_id=1, source_target_pairs={{0,16},{4,28},{8,24},{12,20},{16,0},{20,12},{24,8},{28,4},{1,17},{... | collective-permute-start | bytes 417800 | tf_op jit(solution)/shard_map/ppermute | solution.py:52
  30.3 1.5 %collective-permute-start.12 = (bf16[272,256]{1,0:T(8,128)(2,1)S(1)}, bf16[272,256]{1,0:T(8,128)(2,1)S(1)}, u32[]{:S(2)}, u32[]{:S(2)}) collective-permute-start(bf16[272,256]{1,0:T(8,128)(2,1)S(1)} %get-tuple-element.41), channel_id=1, source_target_pairs={{0,24},{4,20},{8,16},{12,28},{16,8},{20,4},{24,0},{28,12},{1,25},{... | collective-permute-start | bytes 417800 | tf_op jit(solution)/shard_map/ppermute | solution.py:52
  31.8 0.5 %collective-permute-start.10 = (bf16[272,256]{1,0:T(8,128)(2,1)S(1)}, bf16[272,256]{1,0:T(8,128)(2,1)S(1)}, u32[]{:S(2)}, u32[]{:S(2)}) collective-permute-start(bf16[272,256]{1,0:T(8,128)(2,1)S(1)} %get-tuple-element.39.refs_0_), channel_id=1, source_target_pairs={{0,8},{4,12},{8,0},{12,4},{16,24},{20,28},{24,16},{28,20},{1,9},{5... | collective-permute-start | bytes 417800 | tf_op jit(solution)/shard_map/ppermute | solution.py:52
  32.3 9.4 %collective-permute-done.11.refs_1_.refs_2_ = bf16[272,256]{1,0:T(8,128)(2,1)S(1)} collective-permute-done((bf16[272,256]{1,0:T(8,128)(2,1)S(1)}, bf16[272,256]{1,0:T(8,128)(2,1)S(1)}, u32[]{:S(2)}, u32[]{:S(2)}) %collective-permute-start.11) | collective-permute-done | bytes 139296 | tf_op jit(solution)/shard_map/ppermute | solution.py:52
  41.8 0.4 collective-permute-done.10.refs_0_.refs_1_
  42.2 0.1 collective-permute-start.13
  42.3 0.7 %node_results.1 = (bf16[128,256]{1,0:T(8,128)(2,1)}, bf16[128,256]{1,0:T(8,128)(2,1)}) custom-call(bf16[128,256]{1,0:T(8,128)(2,1)S(1)} %get-tuple-element.34.own_hidden, f32[128,256]{1,0:T(8,128)S(1)} %get-tuple-element.38.mine, bf16[272,256]{1,0:T(8,128)(2,1)S(1)} %collective-permute-done.10.refs_0_.refs_1_, ...), custom_call_target="tpu_custom_call" | custom-call | tf_op jit(solution)/shard_map/node_results/pallas_call | solution.py:248
  43.0 0.7 %collective-permute-done.13.other = f32[136,256]{1,0:T(8,128)S(1)} collective-permute-done((f32[136,256]{1,0:T(8,128)S(1)}, f32[136,256]{1,0:T(8,128)S(1)}, u32[]{:S(2)}, u32[]{:S(2)}) %collective-permute-start.13) | collective-permute-done | bytes 139296 | tf_op jit(solution)/shard_map/ppermute | solution.py:28
  43.6 0.7 %weight_results.1 = (f32[256,256]{1,0:T(8,128)}, f32[1,256]{1,0:T(1,128)}) custom-call(f32[136,256]{1,0:T(8,128)S(1)} %line_weight.1.own, f32[136,256]{1,0:T(8,128)S(1)} %collective-permute-done.13.other), custom_call_target="tpu_custom_call" | custom-call | tf_op jit(solution)/shard_map/weight_results/pallas_call | solution.py:248
  (20 shorter events, 0.1 us)
Async XLA Ops:
  0.6 8.5 %copy-start.2 = (bf16[1,128,256]{2,1,0:T(8,128)(2,1)S(1)}, bf16[1,128,256]{2,1,0:T(8,128)(2,1)}, u32[]{:S(2)}) copy-start(bf16[1,128,256]{2,1,0:T(8,128)(2,1)} %param.9) | copy-start | bytes 196612
  0.6 9.1 %collective-permute-start.5 = (bf16[128,256]{1,0:T(8,128)(2,1)}, bf16[128,256]{1,0:T(8,128)(2,1)S(1)}, u32[]{:S(2)}, u32[]{:S(2)}) collective-permute-start(bf16[128,256]{1,0:T(8,128)(2,1)} %bitcast.15), channel_id=1, source_target_pairs={{0,24},{4,28},{8,16},{12,20},{16,8},{20,12},{24,0},{28,4},{1,25},{... | collective-permute-start | bytes 196616 | tf_op jit(solution)/shard_map/ppermute | solution.py:28
  5.8 5.8 %collective-permute-start.3 = (bf16[128,256]{1,0:T(8,128)(2,1)}, bf16[128,256]{1,0:T(8,128)(2,1)S(1)}, u32[]{:S(2)}, u32[]{:S(2)}) collective-permute-start(bf16[128,256]{1,0:T(8,128)(2,1)} %bitcast.16), channel_id=1, source_target_pairs={{0,16},{4,20},{8,24},{12,28},{16,0},{20,4},{24,8},{28,12},{1,17},{... | collective-permute-start | bytes 196616 | tf_op jit(solution)/shard_map/ppermute | solution.py:28
  5.8 5.8 %collective-permute-start.1 = (bf16[128,256]{1,0:T(8,128)(2,1)}, bf16[128,256]{1,0:T(8,128)(2,1)S(1)}, u32[]{:S(2)}, u32[]{:S(2)}) collective-permute-start(bf16[128,256]{1,0:T(8,128)(2,1)} %bitcast.17), channel_id=1, source_target_pairs={{0,8},{4,12},{8,0},{12,4},{16,24},{20,28},{24,16},{28,20},{1,9},{5... | collective-permute-start | bytes 196616 | tf_op jit(solution)/shard_map/ppermute | solution.py:28
  7.4 4.7 %collective-permute-start.7 = (bf16[144,256]{1,0:T(8,128)(2,1)S(1)}, bf16[144,256]{1,0:T(8,128)(2,1)S(1)}, u32[]{:S(2)}, u32[]{:S(2)}) collective-permute-start(bf16[144,256]{1,0:T(8,128)(2,1)S(1)} %get-tuple-element.33.refs_0_.refs_6_), channel_id=1, source_target_pairs={{0,1},{1,0},{2,3},{3,2},{4,6},{5,7},{6,4},{7,5},{8,9},{9,8},{10,11... | collective-permute-start | bytes 221192 | tf_op jit(solution)/shard_map/ppermute | solution.py:40
  9.1 4.6 %collective-permute-start = (bf16[128,256]{1,0:T(8,128)(2,1)S(1)}, bf16[128,256]{1,0:T(8,128)(2,1)S(1)}, u32[]{:S(2)}, u32[]{:S(2)}) collective-permute-start(bf16[128,256]{1,0:T(8,128)(2,1)S(1)} %bitcast.18), channel_id=1, source_target_pairs={{0,4},{4,0},{8,12},{12,8},{16,20},{20,16},{24,28},{28,24},{1,5},{5... | collective-permute-start | bytes 196616 | tf_op jit(solution)/shard_map/ppermute | solution.py:28
  9.8 3.9 %copy-start = (bf16[1,1,3,128,128]{4,3,2,1,0:T(8,128)(2,1)S(1)}, bf16[1,1,3,128,128]{4,3,2,1,0:T(8,128)(2,1)}, u32[]{:S(2)}) copy-start(bf16[1,1,3,128,128]{4,3,2,1,0:T(8,128)(2,1)} %param.10) | copy-start | bytes 294916
  9.8 3.9 %collective-permute-start.6 = (bf16[128,256]{1,0:T(8,128)(2,1)S(1)}, bf16[128,256]{1,0:T(8,128)(2,1)S(1)}, u32[]{:S(2)}, u32[]{:S(2)}) collective-permute-start(bf16[128,256]{1,0:T(8,128)(2,1)S(1)} %collective-permute-done.5.refs_6_), channel_id=1, source_target_pairs={{0,4},{4,0},{8,12},{12,8},{16,20},{20,16},{24,28},{28,24},{1,5},{5... | collective-permute-start | bytes 196616 | tf_op jit(solution)/shard_map/ppermute | solution.py:28
  11.6 2.1 %collective-permute-start.4 = (bf16[128,256]{1,0:T(8,128)(2,1)S(1)}, bf16[128,256]{1,0:T(8,128)(2,1)S(1)}, u32[]{:S(2)}, u32[]{:S(2)}) collective-permute-start(bf16[128,256]{1,0:T(8,128)(2,1)S(1)} %collective-permute-done.3.refs_4_), channel_id=1, source_target_pairs={{0,4},{4,0},{8,12},{12,8},{16,20},{20,16},{24,28},{28,24},{1,5},{5... | collective-permute-start | bytes 196616 | tf_op jit(solution)/shard_map/ppermute | solution.py:28
  11.6 2.1 %collective-permute-start.2 = (bf16[128,256]{1,0:T(8,128)(2,1)S(1)}, bf16[128,256]{1,0:T(8,128)(2,1)S(1)}, u32[]{:S(2)}, u32[]{:S(2)}) collective-permute-start(bf16[128,256]{1,0:T(8,128)(2,1)S(1)} %collective-permute-done.1.refs_2_), channel_id=1, source_target_pairs={{0,4},{4,0},{8,12},{12,8},{16,20},{20,16},{24,28},{28,24},{1,5},{5... | collective-permute-start | bytes 196616 | tf_op jit(solution)/shard_map/ppermute | solution.py:28
  12.1 13.1 %collective-permute-start.8 = (bf16[288,256]{1,0:T(8,128)(2,1)S(1)}, bf16[288,256]{1,0:T(8,128)(2,1)S(1)}, u32[]{:S(2)}, u32[]{:S(2)}) collective-permute-start(bf16[288,256]{1,0:T(8,128)(2,1)S(1)} %cotangents_so_far.1), channel_id=1, source_target_pairs={{0,2},{1,3},{2,0},{3,1},{4,5},{5,4},{6,7},{7,6},{8,10},{9,11},{10,... | collective-permute-start | bytes 442376 | tf_op jit(solution)/shard_map/ppermute | solution.py:40
  14.0 11.2 %copy-start.1 = (bf16[256,256]{1,0:T(8,128)(2,1)S(1)}, bf16[256,256]{1,0:T(8,128)(2,1)}, u32[]{:S(2)}) copy-start(bf16[256,256]{1,0:T(8,128)(2,1)} %refs_2_.1) | copy-start | bytes 393220
  26.5 1.7 %collective-permute-start.9 = (bf16[656,256]{1,0:T(8,128)(2,1)S(1)}, bf16[656,256]{1,0:T(8,128)(2,1)S(1)}, u32[]{:S(2)}, u32[]{:S(2)}) collective-permute-start(bf16[656,256]{1,0:T(8,128)(2,1)S(1)} %get-tuple-element.37.own_sent), channel_id=1, source_target_pairs={{0,4},{4,0},{8,12},{12,8},{16,20},{20,16},{24,28},{28,24},{1,5},{5... | collective-permute-start | bytes 1007624 | tf_op jit(solution)/shard_map/ppermute | solution.py:28
  28.2 13.6 %collective-permute-start.11 = (bf16[272,256]{1,0:T(8,128)(2,1)S(1)}, bf16[272,256]{1,0:T(8,128)(2,1)S(1)}, u32[]{:S(2)}, u32[]{:S(2)}) collective-permute-start(bf16[272,256]{1,0:T(8,128)(2,1)S(1)} %get-tuple-element.40), channel_id=1, source_target_pairs={{0,16},{4,28},{8,24},{12,20},{16,0},{20,12},{24,8},{28,4},{1,17},{... | collective-permute-start | bytes 417800 | tf_op jit(solution)/shard_map/ppermute | solution.py:52
  30.3 11.5 %collective-permute-start.12 = (bf16[272,256]{1,0:T(8,128)(2,1)S(1)}, bf16[272,256]{1,0:T(8,128)(2,1)S(1)}, u32[]{:S(2)}, u32[]{:S(2)}) collective-permute-start(bf16[272,256]{1,0:T(8,128)(2,1)S(1)} %get-tuple-element.41), channel_id=1, source_target_pairs={{0,24},{4,20},{8,16},{12,28},{16,8},{20,4},{24,0},{28,12},{1,25},{... | collective-permute-start | bytes 417800 | tf_op jit(solution)/shard_map/ppermute | solution.py:52
  31.8 10.3 %collective-permute-start.10 = (bf16[272,256]{1,0:T(8,128)(2,1)S(1)}, bf16[272,256]{1,0:T(8,128)(2,1)S(1)}, u32[]{:S(2)}, u32[]{:S(2)}) collective-permute-start(bf16[272,256]{1,0:T(8,128)(2,1)S(1)} %get-tuple-element.39.refs_0_), channel_id=1, source_target_pairs={{0,8},{4,12},{8,0},{12,4},{16,24},{20,28},{24,16},{28,20},{1,9},{5... | collective-permute-start | bytes 417800 | tf_op jit(solution)/shard_map/ppermute | solution.py:52
  42.2 1.4 %collective-permute-start.13 = (f32[136,256]{1,0:T(8,128)S(1)}, f32[136,256]{1,0:T(8,128)S(1)}, u32[]{:S(2)}, u32[]{:S(2)}) collective-permute-start(f32[136,256]{1,0:T(8,128)S(1)} %line_weight.1.own), channel_id=1, source_target_pairs={{0,4},{4,0},{8,12},{12,8},{16,20},{20,16},{24,28},{28,24},{1,5},{5... | collective-permute-start | bytes 417800 | tf_op jit(solution)/shard_map/ppermute | solution.py:28

commit v8 on v7

--- a/solution.py
+++ b/solution.py
@@ -44,6 +44,10 @@
     if n_line < 4 or core == 0:
         return m
     return m - m % 4 + (0, 1, 3, 2)[m % 4]
+
+
+def carries_bias(m, n_line):
+    return n_line < 4 or m % 4 != 3
 
 
 def line_exchange(value, m):
@@ -209,16 +213,23 @@
         part = pl.ds(pl.multiple_of(chosen * side, side), side)
         out[0:side] = (kept[part, :] + came[part, :].astype(F32)).astype(BF16)
         out[side : side + half] = weights
-        out[side + half : side + half + PAD] = column_sum
-
-
-def line_weight_kernel(scale, *refs):
+        if carries_bias(m, n_line):
+            out[side + half : side + half + PAD] = column_sum
+
+
+def line_weight_kernel(scale, side, *refs):
     blocks, out = refs[:-1], refs[-1]
-    half = out.shape[0] - 8
-    start = blocks[0].shape[0] - half - PAD
-    out[0:half] = scale * tree_sum(b[start : start + half].astype(F32) for b in blocks)
-    column_sum = scale * tree_sum(joined(b[start + half :]) for b in blocks)
-    out[half:] = jnp.broadcast_to(column_sum, (8, column_sum.shape[1]))
+    n_line, half = len(blocks), out.shape[0] - 8
+    start, ends = side + half, slice(side + half, side + half + PAD)
+    out[0:half] = scale * tree_sum(b[side:start].astype(F32) for b in blocks)
+    place = lax.broadcasted_iota(jnp.int32, (8, out.shape[1]), 0)
+    rows = jnp.zeros((8, out.shape[1]), F32)
+    for first in range(0, n_line, 4):
+        heard = [joined(b[ends]) for m, b in enumerate(blocks) if first <= m < first + 4 and carries_bias(m, n_line)]
+        rows = jnp.where(place == first // 2, scale * tree_sum(heard[:2]), rows)
+        for block in heard[2:]:
+            rows = jnp.where(place == first // 2 + 1, scale * block, rows)
+    out[half:] = rows
 
 
 def node_results_kernel(own_hidden, mine, *refs):
@@ -231,12 +242,15 @@
     grad_features[...] = total.astype(BF16)
 
 
-def weight_results_kernel(own, other, grad_weight, grad_bias):
+def weight_results_kernel(n_line, own, other, grad_weight, grad_bias):
     half = grad_weight.shape[0] // 2
     for shift, block in enumerate((own, other)):
         start = pl.multiple_of((lax.axis_index("row") % 2 ^ shift) * half, half)
         grad_weight[pl.ds(start, half), :] = block[0:half]
-    grad_bias[...] = own[half : half + 1]
+    ours, theirs = own[half:], other[half:]
+    grad_bias[...] = tree_sum(
+        ours[i : i + 1] + (ours[i + 1 : i + 2] + theirs[i + 1 : i + 2]) for i in range(0, max(n_line // 2, 1), 2)
+    )
 
 
 def call(kernel, name, outs, scratch, ints, *arrays):
@@ -354,7 +368,8 @@
     mine, *parts = call(
         chip_kernel,
         "chip_sums",
-        [((side, width), F32, True)] + [((side + half + PAD, width), BF16, True)] * (n_line - 1),
+        [((side, width), F32, True)]
+        + [((side + half + PAD * carries_bias(m, n_line), width), BF16, True) for m in range(1, n_line)],
         [],
         [],
         *map(near, (kept_back, kept_weight, sent, came)),
@@ -362,7 +377,7 @@
     line = [parts[0]] + [line_exchange(part, m) for m, part in enumerate(parts, 1)]
     scale = 1.0 / math.sqrt(n_row * n_col * side)
     (weights,) = call(
-        functools.partial(line_weight_kernel, scale),
+        functools.partial(line_weight_kernel, scale, side),
         "line_weight",
         [((half + 8, width), F32, True)],
         [],
@@ -379,7 +394,7 @@
         *map(near, (hidden, mine, *line[1:])),
     )
     grad_weight, grad_bias = call(
-        weight_results_kernel,
+        functools.partial(weight_results_kernel, n_line),
         "weight_results",
         [((width, width), F32, False), ((1, width), F32, False)],
         [],

time: 44.6 us -> 44.2 us (level)
  waiting for transfers between devices: 13.4 us -> 12.6 us
    ppermute x3, waiting for transfers between devices: 9.84 us -> 9.09 us  [line_exchange(): return lax.ppermute(value, 'row', pairs)]
  transfers between devices with their start and end apart: 14 -> 14, of which waited for: 5 -> 4; matrix products, arithmetic and copies ran while one was open for 0% -> 0% of each run, Pallas kernels for 4% -> 4%
where the time goes in v8:
time: 44.2 us; the launch traced here: 44 us
  starting transfers between devices  14.8 us (33%)
  waiting for transfers between devices  12.6 us (29%)
  blocking collectives  11.2 us (25%)
  Pallas kernels  4 us (9%)
  between operations  1.4 us (3%)
    all_gather x1, blocking collectives, on_device(): products = lax.all_gather(product, 'col')  11.2 us
    ppermute x3, waiting for transfers between devices, line_exchange(): return lax.ppermute(value, 'row', pairs)  9.09 us
    ppermute x9, starting transfers between devices, exchange(): return lax.ppermute(value, axis, [(i, i ^ mask) for i in range(size)])  7.03 us
    ppermute x3, starting transfers between devices, line_exchange(): return lax.ppermute(value, 'row', pairs)  4.45 us
    pallas_call x8, Pallas kernels, call(): pl.pallas_call(kernel, name=name, out_shape=[space(dtype)(shape, dtype) i...  4 us
    ppermute x9, waiting for transfers between devices, exchange(): return lax.ppermute(value, axis, [(i, i ^ mask) for i in range(size)])  3.49 us
    ppermute x2, starting transfers between devices, column_exchange(): return lax.ppermute(value, ('row', 'col'), pairs)  3.29 us
  transfers between devices with their start and end apart: 14, of which 4 were waited for; matrix products, arithmetic and copies ran while one was open for 0% of the time, Pallas kernels for 4%

profile of v8, /device:TPU:0, one launch (start us, length us, event | category | flops | bytes accessed | tf_op | source)
XLA Modules:
  0.0 44.0 jit_solution(14341474417271567144)
XLA Ops:
  0.6 5.1 %collective-permute-start.5 = (bf16[128,256]{1,0:T(8,128)(2,1)}, bf16[128,256]{1,0:T(8,128)(2,1)S(1)}, u32[]{:S(2)}, u32[]{:S(2)}) collective-permute-start(bf16[128,256]{1,0:T(8,128)(2,1)} %bitcast.15), channel_id=1, source_target_pairs={{0,24},{4,28},{8,16},{12,20},{16,8},{20,12},{24,0},{28,4},{1,25},{... | collective-permute-start | bytes 196616 | tf_op jit(solution)/shard_map/ppermute | solution.py:28
  5.8 0.6 %collective-permute-start.1 = (bf16[128,256]{1,0:T(8,128)(2,1)}, bf16[128,256]{1,0:T(8,128)(2,1)S(1)}, u32[]{:S(2)}, u32[]{:S(2)}) collective-permute-start(bf16[128,256]{1,0:T(8,128)(2,1)} %bitcast.17), channel_id=1, source_target_pairs={{0,8},{4,12},{8,0},{12,4},{16,24},{20,28},{24,16},{28,20},{1,9},{5... | collective-permute-start | bytes 196616 | tf_op jit(solution)/shard_map/ppermute | solution.py:28
  6.4 1.0 %masked_cotangent.1 = (bf16[144,256]{1,0:T(8,128)(2,1)S(1)}, f32[1,256]{1,0:T(1,128)S(1)}, s32[6]{0:T(128)S(4)}) custom-call(s32[3]{0:T(128)} %bitcast.22, s32[3]{0:T(128)} %bitcast.23, s32[1,128]{1,0:T(1,128)} %mask.1, bf16[128,256]{1,0:T(8,128)(2,1)} %bitcast.20, f32[1,256]{1,0:T(1,128)} %bitcast.21), custom_call_target="tpu_custom_call" | custom-call | tf_op jit(solution)/shard_map/masked_cotangent/pallas_call | solution.py:262
  7.4 1.7 %collective-permute-start.7 = (bf16[144,256]{1,0:T(8,128)(2,1)S(1)}, bf16[144,256]{1,0:T(8,128)(2,1)S(1)}, u32[]{:S(2)}, u32[]{:S(2)}) collective-permute-start(bf16[144,256]{1,0:T(8,128)(2,1)S(1)} %get-tuple-element.33.refs_0_.refs_6_), channel_id=1, source_target_pairs={{0,1},{1,0},{2,3},{3,2},{4,6},{5,7},{6,4},{7,5},{8,9},{9,8},{10,11... | collective-permute-start | bytes 221192 | tf_op jit(solution)/shard_map/ppermute | solution.py:40
  9.8 0.0 copy-start
  9.8 0.6 %collective-permute-start.6 = (bf16[128,256]{1,0:T(8,128)(2,1)S(1)}, bf16[128,256]{1,0:T(8,128)(2,1)S(1)}, u32[]{:S(2)}, u32[]{:S(2)}) collective-permute-start(bf16[128,256]{1,0:T(8,128)(2,1)S(1)} %collective-permute-done.5.refs_6_), channel_id=1, source_target_pairs={{0,4},{4,0},{8,12},{12,8},{16,20},{20,16},{24,28},{28,24},{1,5},{5... | collective-permute-start | bytes 196616 | tf_op jit(solution)/shard_map/ppermute | solution.py:28
  10.4 1.2 %collective-permute-done.3.refs_4_ = bf16[128,256]{1,0:T(8,128)(2,1)S(1)} collective-permute-done((bf16[128,256]{1,0:T(8,128)(2,1)}, bf16[128,256]{1,0:T(8,128)(2,1)S(1)}, u32[]{:S(2)}, u32[]{:S(2)}) %collective-permute-start.3) | collective-permute-done | bytes 65568 | tf_op jit(solution)/shard_map/ppermute | solution.py:28
  11.6 0.5 %collective-permute-start.2 = (bf16[128,256]{1,0:T(8,128)(2,1)S(1)}, bf16[128,256]{1,0:T(8,128)(2,1)S(1)}, u32[]{:S(2)}, u32[]{:S(2)}) collective-permute-start(bf16[128,256]{1,0:T(8,128)(2,1)S(1)} %collective-permute-done.1.refs_2_), channel_id=1, source_target_pairs={{0,4},{4,0},{8,12},{12,8},{16,20},{20,16},{24,28},{28,24},{1,5},{5... | collective-permute-start | bytes 196616 | tf_op jit(solution)/shard_map/ppermute | solution.py:28
  12.1 1.6 %collective-permute-start.8 = (bf16[288,256]{1,0:T(8,128)(2,1)S(1)}, bf16[288,256]{1,0:T(8,128)(2,1)S(1)}, u32[]{:S(2)}, u32[]{:S(2)}) collective-permute-start(bf16[288,256]{1,0:T(8,128)(2,1)S(1)} %cotangents_so_far.1), channel_id=1, source_target_pairs={{0,2},{1,3},{2,0},{3,1},{4,5},{5,4},{6,7},{7,6},{8,10},{9,11},{10,... | collective-permute-start | bytes 442376 | tf_op jit(solution)/shard_map/ppermute | solution.py:40
  13.7 0.2 tile_products.1
  14.0 0.0 copy-start.1
  14.0 11.2 %all-gather = bf16[1536,256]{1,0:T(8,128)(2,1)S(1)} all-gather(bf16[384,256]{1,0:T(8,128)(2,1)S(1)} %get-tuple-element.32), channel_id=2, replica_groups=mesh['row'=8,'col'=4] {'col'}, dimensions={0}, use_global_device_ids=true | all-gather | bytes 983040 | tf_op jit(solution)/shard_map/all_gather | solution.py:339
  25.2 1.2 %dense_layer.1 = (bf16[128,256]{1,0:T(8,128)(2,1)S(1)}, bf16[656,256]{1,0:T(8,128)(2,1)S(1)}, f32[512,256]{1,0:T(8,128)S(1)}, f32[128,256]{1,0:T(8,128)S(1)}) custom-call(s32[6]{0:T(128)S(4)} %get-tuple-element.25.ints.refs_0_, s32[2]{0:T(128)S(4)} %get-tuple-element.30.refs_1_, bf16[256,256]{1,0:T(8,128)(2,1)S(1)} %copy-done.1, ...), custom_call_target="tpu_custom_call" | custom-call | tf_op jit(solution)/shard_map/dense_layer/pallas_call | solution.py:262
  26.5 0.1 collective-permute-start.9
  26.5 1.6 %collective-permute-done.9.came = bf16[656,256]{1,0:T(8,128)(2,1)S(1)} collective-permute-done((bf16[656,256]{1,0:T(8,128)(2,1)S(1)}, bf16[656,256]{1,0:T(8,128)(2,1)S(1)}, u32[]{:S(2)}, u32[]{:S(2)}) %collective-permute-start.9) | collective-permute-done | bytes 335904 | tf_op jit(solution)/shard_map/ppermute | solution.py:28
  28.2 0.1 chip_sums.1
  28.2 2.1 %collective-permute-start.11 = (bf16[272,256]{1,0:T(8,128)(2,1)S(1)}, bf16[272,256]{1,0:T(8,128)(2,1)S(1)}, u32[]{:S(2)}, u32[]{:S(2)}) collective-permute-start(bf16[272,256]{1,0:T(8,128)(2,1)S(1)} %get-tuple-element.40), channel_id=1, source_target_pairs={{0,16},{4,28},{8,24},{12,20},{16,0},{20,12},{24,8},{28,4},{1,17},{... | collective-permute-start | bytes 417800 | tf_op jit(solution)/shard_map/ppermute | solution.py:56
  30.3 2.0 %collective-permute-start.10 = (bf16[272,256]{1,0:T(8,128)(2,1)S(1)}, bf16[272,256]{1,0:T(8,128)(2,1)S(1)}, u32[]{:S(2)}, u32[]{:S(2)}) collective-permute-start(bf16[272,256]{1,0:T(8,128)(2,1)S(1)} %get-tuple-element.39.refs_0_), channel_id=1, source_target_pairs={{0,8},{4,12},{8,0},{12,4},{16,24},{20,28},{24,16},{28,20},{1,9},{5... | collective-permute-start | bytes 417800 | tf_op jit(solution)/shard_map/ppermute | solution.py:56
  32.3 0.3 collective-permute-start.12
  32.7 9.1 %collective-permute-done.12.refs_2_.refs_3_ = bf16[256,256]{1,0:T(8,128)(2,1)S(1)} collective-permute-done((bf16[256,256]{1,0:T(8,128)(2,1)S(1)}, bf16[256,256]{1,0:T(8,128)(2,1)S(1)}, u32[]{:S(2)}, u32[]{:S(2)}) %collective-permute-start.12) | collective-permute-done | bytes 131104 | tf_op jit(solution)/shard_map/ppermute | solution.py:56
  41.8 0.1 collective-permute-start.13
  41.9 0.7 %node_results.1 = (bf16[128,256]{1,0:T(8,128)(2,1)}, bf16[128,256]{1,0:T(8,128)(2,1)}) custom-call(bf16[128,256]{1,0:T(8,128)(2,1)S(1)} %get-tuple-element.34.own_hidden, f32[128,256]{1,0:T(8,128)S(1)} %get-tuple-element.38.mine, bf16[272,256]{1,0:T(8,128)(2,1)S(1)} %collective-permute-done.10.refs_0_.refs_1_, ...), custom_call_target="tpu_custom_call" | custom-call | tf_op jit(solution)/shard_map/node_results/pallas_call | solution.py:262
  42.6 0.6 %collective-permute-done.13.other = f32[136,256]{1,0:T(8,128)S(1)} collective-permute-done((f32[136,256]{1,0:T(8,128)S(1)}, f32[136,256]{1,0:T(8,128)S(1)}, u32[]{:S(2)}, u32[]{:S(2)}) %collective-permute-start.13) | collective-permute-done | bytes 139296 | tf_op jit(solution)/shard_map/ppermute | solution.py:28
  43.2 0.7 %weight_results.1 = (f32[256,256]{1,0:T(8,128)}, f32[1,256]{1,0:T(1,128)}) custom-call(f32[136,256]{1,0:T(8,128)S(1)} %line_weight.1.own, f32[136,256]{1,0:T(8,128)S(1)} %collective-permute-done.13.other), custom_call_target="tpu_custom_call" | custom-call | tf_op jit(solution)/shard_map/weight_results/pallas_call | solution.py:262
  (20 shorter events, 0.1 us)
Async XLA Ops:
  0.6 8.5 %copy-start.2 = (bf16[1,128,256]{2,1,0:T(8,128)(2,1)S(1)}, bf16[1,128,256]{2,1,0:T(8,128)(2,1)}, u32[]{:S(2)}) copy-start(bf16[1,128,256]{2,1,0:T(8,128)(2,1)} %param.9) | copy-start | bytes 196612
  0.6 9.1 %collective-permute-start.5 = (bf16[128,256]{1,0:T(8,128)(2,1)}, bf16[128,256]{1,0:T(8,128)(2,1)S(1)}, u32[]{:S(2)}, u32[]{:S(2)}) collective-permute-start(bf16[128,256]{1,0:T(8,128)(2,1)} %bitcast.15), channel_id=1, source_target_pairs={{0,24},{4,28},{8,16},{12,20},{16,8},{20,12},{24,0},{28,4},{1,25},{... | collective-permute-start | bytes 196616 | tf_op jit(solution)/shard_map/ppermute | solution.py:28
  5.8 5.8 %collective-permute-start.3 = (bf16[128,256]{1,0:T(8,128)(2,1)}, bf16[128,256]{1,0:T(8,128)(2,1)S(1)}, u32[]{:S(2)}, u32[]{:S(2)}) collective-permute-start(bf16[128,256]{1,0:T(8,128)(2,1)} %bitcast.16), channel_id=1, source_target_pairs={{0,16},{4,20},{8,24},{12,28},{16,0},{20,4},{24,8},{28,12},{1,17},{... | collective-permute-start | bytes 196616 | tf_op jit(solution)/shard_map/ppermute | solution.py:28
  5.8 5.8 %collective-permute-start.1 = (bf16[128,256]{1,0:T(8,128)(2,1)}, bf16[128,256]{1,0:T(8,128)(2,1)S(1)}, u32[]{:S(2)}, u32[]{:S(2)}) collective-permute-start(bf16[128,256]{1,0:T(8,128)(2,1)} %bitcast.17), channel_id=1, source_target_pairs={{0,8},{4,12},{8,0},{12,4},{16,24},{20,28},{24,16},{28,20},{1,9},{5... | collective-permute-start | bytes 196616 | tf_op jit(solution)/shard_map/ppermute | solution.py:28
  7.4 4.7 %collective-permute-start.7 = (bf16[144,256]{1,0:T(8,128)(2,1)S(1)}, bf16[144,256]{1,0:T(8,128)(2,1)S(1)}, u32[]{:S(2)}, u32[]{:S(2)}) collective-permute-start(bf16[144,256]{1,0:T(8,128)(2,1)S(1)} %get-tuple-element.33.refs_0_.refs_6_), channel_id=1, source_target_pairs={{0,1},{1,0},{2,3},{3,2},{4,6},{5,7},{6,4},{7,5},{8,9},{9,8},{10,11... | collective-permute-start | bytes 221192 | tf_op jit(solution)/shard_map/ppermute | solution.py:40
  9.1 4.6 %collective-permute-start = (bf16[128,256]{1,0:T(8,128)(2,1)S(1)}, bf16[128,256]{1,0:T(8,128)(2,1)S(1)}, u32[]{:S(2)}, u32[]{:S(2)}) collective-permute-start(bf16[128,256]{1,0:T(8,128)(2,1)S(1)} %bitcast.18), channel_id=1, source_target_pairs={{0,4},{4,0},{8,12},{12,8},{16,20},{20,16},{24,28},{28,24},{1,5},{5... | collective-permute-start | bytes 196616 | tf_op jit(solution)/shard_map/ppermute | solution.py:28
  9.8 3.9 %copy-start = (bf16[1,1,3,128,128]{4,3,2,1,0:T(8,128)(2,1)S(1)}, bf16[1,1,3,128,128]{4,3,2,1,0:T(8,128)(2,1)}, u32[]{:S(2)}) copy-start(bf16[1,1,3,128,128]{4,3,2,1,0:T(8,128)(2,1)} %param.10) | copy-start | bytes 294916
  9.8 3.9 %collective-permute-start.6 = (bf16[128,256]{1,0:T(8,128)(2,1)S(1)}, bf16[128,256]{1,0:T(8,128)(2,1)S(1)}, u32[]{:S(2)}, u32[]{:S(2)}) collective-permute-start(bf16[128,256]{1,0:T(8,128)(2,1)S(1)} %collective-permute-done.5.refs_6_), channel_id=1, source_target_pairs={{0,4},{4,0},{8,12},{12,8},{16,20},{20,16},{24,28},{28,24},{1,5},{5... | collective-permute-start | bytes 196616 | tf_op jit(solution)/shard_map/ppermute | solution.py:28
  11.6 2.1 %collective-permute-start.4 = (bf16[128,256]{1,0:T(8,128)(2,1)S(1)}, bf16[128,256]{1,0:T(8,128)(2,1)S(1)}, u32[]{:S(2)}, u32[]{:S(2)}) collective-permute-start(bf16[128,256]{1,0:T(8,128)(2,1)S(1)} %collective-permute-done.3.refs_4_), channel_id=1, source_target_pairs={{0,4},{4,0},{8,12},{12,8},{16,20},{20,16},{24,28},{28,24},{1,5},{5... | collective-permute-start | bytes 196616 | tf_op jit(solution)/shard_map/ppermute | solution.py:28
  11.6 2.1 %collective-permute-start.2 = (bf16[128,256]{1,0:T(8,128)(2,1)S(1)}, bf16[128,256]{1,0:T(8,128)(2,1)S(1)}, u32[]{:S(2)}, u32[]{:S(2)}) collective-permute-start(bf16[128,256]{1,0:T(8,128)(2,1)S(1)} %collective-permute-done.1.refs_2_), channel_id=1, source_target_pairs={{0,4},{4,0},{8,12},{12,8},{16,20},{20,16},{24,28},{28,24},{1,5},{5... | collective-permute-start | bytes 196616 | tf_op jit(solution)/shard_map/ppermute | solution.py:28
  12.1 13.1 %collective-permute-start.8 = (bf16[288,256]{1,0:T(8,128)(2,1)S(1)}, bf16[288,256]{1,0:T(8,128)(2,1)S(1)}, u32[]{:S(2)}, u32[]{:S(2)}) collective-permute-start(bf16[288,256]{1,0:T(8,128)(2,1)S(1)} %cotangents_so_far.1), channel_id=1, source_target_pairs={{0,2},{1,3},{2,0},{3,1},{4,5},{5,4},{6,7},{7,6},{8,10},{9,11},{10,... | collective-permute-start | bytes 442376 | tf_op jit(solution)/shard_map/ppermute | solution.py:40
  14.0 11.2 %copy-start.1 = (bf16[256,256]{1,0:T(8,128)(2,1)S(1)}, bf16[256,256]{1,0:T(8,128)(2,1)}, u32[]{:S(2)}) copy-start(bf16[256,256]{1,0:T(8,128)(2,1)} %refs_2_.1) | copy-start | bytes 393220
  26.5 1.7 %collective-permute-start.9 = (bf16[656,256]{1,0:T(8,128)(2,1)S(1)}, bf16[656,256]{1,0:T(8,128)(2,1)S(1)}, u32[]{:S(2)}, u32[]{:S(2)}) collective-permute-start(bf16[656,256]{1,0:T(8,128)(2,1)S(1)} %get-tuple-element.37.own_sent), channel_id=1, source_target_pairs={{0,4},{4,0},{8,12},{12,8},{16,20},{20,16},{24,28},{28,24},{1,5},{5... | collective-permute-start | bytes 1007624 | tf_op jit(solution)/shard_map/ppermute | solution.py:28
  28.2 13.5 %collective-permute-start.11 = (bf16[272,256]{1,0:T(8,128)(2,1)S(1)}, bf16[272,256]{1,0:T(8,128)(2,1)S(1)}, u32[]{:S(2)}, u32[]{:S(2)}) collective-permute-start(bf16[272,256]{1,0:T(8,128)(2,1)S(1)} %get-tuple-element.40), channel_id=1, source_target_pairs={{0,16},{4,28},{8,24},{12,20},{16,0},{20,12},{24,8},{28,4},{1,17},{... | collective-permute-start | bytes 417800 | tf_op jit(solution)/shard_map/ppermute | solution.py:56
  30.3 11.5 %collective-permute-start.10 = (bf16[272,256]{1,0:T(8,128)(2,1)S(1)}, bf16[272,256]{1,0:T(8,128)(2,1)S(1)}, u32[]{:S(2)}, u32[]{:S(2)}) collective-permute-start(bf16[272,256]{1,0:T(8,128)(2,1)S(1)} %get-tuple-element.39.refs_0_), channel_id=1, source_target_pairs={{0,8},{4,12},{8,0},{12,4},{16,24},{20,28},{24,16},{28,20},{1,9},{5... | collective-permute-start | bytes 417800 | tf_op jit(solution)/shard_map/ppermute | solution.py:56
  32.3 9.4 %collective-permute-start.12 = (bf16[256,256]{1,0:T(8,128)(2,1)S(1)}, bf16[256,256]{1,0:T(8,128)(2,1)S(1)}, u32[]{:S(2)}, u32[]{:S(2)}) collective-permute-start(bf16[256,256]{1,0:T(8,128)(2,1)S(1)} %get-tuple-element.41), channel_id=1, source_target_pairs={{0,24},{4,20},{8,16},{12,28},{16,8},{20,4},{24,0},{28,12},{1,25},{... | collective-permute-start | bytes 393224 | tf_op jit(solution)/shard_map/ppermute | solution.py:56
  41.8 1.4 %collective-permute-start.13 = (f32[136,256]{1,0:T(8,128)S(1)}, f32[136,256]{1,0:T(8,128)S(1)}, u32[]{:S(2)}, u32[]{:S(2)}) collective-permute-start(f32[136,256]{1,0:T(8,128)S(1)} %line_weight.1.own), channel_id=1, source_target_pairs={{0,4},{4,0},{8,12},{12,8},{16,20},{20,16},{24,28},{28,24},{1,5},{5... | collective-permute-start | bytes 417800 | tf_op jit(solution)/shard_map/ppermute | solution.py:28

commit v9 on v8

--- a/solution.py
+++ b/solution.py
@@ -152,9 +152,9 @@
         for q in range(n_col)
     ]
     for q in range(n_col):
-        places = cotangent(q, side, each_rows)[:, 0:128].astype(F32).astype(jnp.int32)
+        places = jnp.max(cotangent(q, side, each_rows)[:, 0:128].astype(F32), axis=1, keepdims=True)
         for p in range(blocks):
-            target[places_of[q], p] = jnp.max(places[p : p + 1])
+            target[places_of[q], p] = places[p, 0].astype(jnp.int32)
     total[...] = jnp.zeros_like(total)
 
     def add(i):

time: 44.2 us -> 44.1 us (level)
  no operation moved by 1% of the time
where the time goes in v9:
time: 44.1 us; the launch traced here: 43.9 us
  starting transfers between devices  14.8 us (34%)
  waiting for transfers between devices  12.6 us (29%)
  blocking collectives  11.2 us (25%)
  Pallas kernels  3.95 us (9%)
  between operations  1.4 us (3%)
    all_gather x1, blocking collectives, on_device(): products = lax.all_gather(product, 'col')  11.2 us
    ppermute x3, waiting for transfers between devices, line_exchange(): return lax.ppermute(value, 'row', pairs)  9.09 us
    ppermute x9, starting transfers between devices, exchange(): return lax.ppermute(value, axis, [(i, i ^ mask) for i in range(size)])  7.03 us
    ppermute x3, starting transfers between devices, line_exchange(): return lax.ppermute(value, 'row', pairs)  4.45 us
    pallas_call x8, Pallas kernels, call(): pl.pallas_call(kernel, name=name, out_shape=[space(dtype)(shape, dtype) i...  3.95 us
    ppermute x9, waiting for transfers between devices, exchange(): return lax.ppermute(value, axis, [(i, i ^ mask) for i in range(size)])  3.49 us
    ppermute x2, starting transfers between devices, column_exchange(): return lax.ppermute(value, ('row', 'col'), pairs)  3.29 us
  transfers between devices with their start and end apart: 14, of which 4 were waited for; matrix products, arithmetic and copies ran while one was open for 0% of the time, Pallas kernels for 4%

profile of v9, /device:TPU:0, one launch (start us, length us, event | category | flops | bytes accessed | tf_op | source)
XLA Modules:
  0.0 43.9 jit_solution(682055692333036404)
XLA Ops:
  0.6 5.1 %collective-permute-start.5 = (bf16[128,256]{1,0:T(8,128)(2,1)}, bf16[128,256]{1,0:T(8,128)(2,1)S(1)}, u32[]{:S(2)}, u32[]{:S(2)}) collective-permute-start(bf16[128,256]{1,0:T(8,128)(2,1)} %bitcast.15), channel_id=1, source_target_pairs={{0,24},{4,28},{8,16},{12,20},{16,8},{20,12},{24,0},{28,4},{1,25},{... | collective-permute-start | bytes 196616 | tf_op jit(solution)/shard_map/ppermute | solution.py:28
  5.8 0.6 %collective-permute-start.1 = (bf16[128,256]{1,0:T(8,128)(2,1)}, bf16[128,256]{1,0:T(8,128)(2,1)S(1)}, u32[]{:S(2)}, u32[]{:S(2)}) collective-permute-start(bf16[128,256]{1,0:T(8,128)(2,1)} %bitcast.17), channel_id=1, source_target_pairs={{0,8},{4,12},{8,0},{12,4},{16,24},{20,28},{24,16},{28,20},{1,9},{5... | collective-permute-start | bytes 196616 | tf_op jit(solution)/shard_map/ppermute | solution.py:28
  6.4 1.0 %masked_cotangent.1 = (bf16[144,256]{1,0:T(8,128)(2,1)S(1)}, f32[1,256]{1,0:T(1,128)S(1)}, s32[6]{0:T(128)S(4)}) custom-call(s32[3]{0:T(128)} %bitcast.22, s32[3]{0:T(128)} %bitcast.23, s32[1,128]{1,0:T(1,128)} %mask.1, bf16[128,256]{1,0:T(8,128)(2,1)} %bitcast.20, f32[1,256]{1,0:T(1,128)} %bitcast.21), custom_call_target="tpu_custom_call" | custom-call | tf_op jit(solution)/shard_map/masked_cotangent/pallas_call | solution.py:262
  7.4 1.7 %collective-permute-start.7 = (bf16[144,256]{1,0:T(8,128)(2,1)S(1)}, bf16[144,256]{1,0:T(8,128)(2,1)S(1)}, u32[]{:S(2)}, u32[]{:S(2)}) collective-permute-start(bf16[144,256]{1,0:T(8,128)(2,1)S(1)} %get-tuple-element.33.refs_0_.refs_6_), channel_id=1, source_target_pairs={{0,1},{1,0},{2,3},{3,2},{4,6},{5,7},{6,4},{7,5},{8,9},{9,8},{10,11... | collective-permute-start | bytes 221192 | tf_op jit(solution)/shard_map/ppermute | solution.py:40
  9.8 0.0 copy-start
  9.8 0.6 %collective-permute-start.6 = (bf16[128,256]{1,0:T(8,128)(2,1)S(1)}, bf16[128,256]{1,0:T(8,128)(2,1)S(1)}, u32[]{:S(2)}, u32[]{:S(2)}) collective-permute-start(bf16[128,256]{1,0:T(8,128)(2,1)S(1)} %collective-permute-done.5.refs_6_), channel_id=1, source_target_pairs={{0,4},{4,0},{8,12},{12,8},{16,20},{20,16},{24,28},{28,24},{1,5},{5... | collective-permute-start | bytes 196616 | tf_op jit(solution)/shard_map/ppermute | solution.py:28
  10.4 1.2 %collective-permute-done.3.refs_4_ = bf16[128,256]{1,0:T(8,128)(2,1)S(1)} collective-permute-done((bf16[128,256]{1,0:T(8,128)(2,1)}, bf16[128,256]{1,0:T(8,128)(2,1)S(1)}, u32[]{:S(2)}, u32[]{:S(2)}) %collective-permute-start.3) | collective-permute-done | bytes 65568 | tf_op jit(solution)/shard_map/ppermute | solution.py:28
  11.6 0.5 %collective-permute-start.2 = (bf16[128,256]{1,0:T(8,128)(2,1)S(1)}, bf16[128,256]{1,0:T(8,128)(2,1)S(1)}, u32[]{:S(2)}, u32[]{:S(2)}) collective-permute-start(bf16[128,256]{1,0:T(8,128)(2,1)S(1)} %collective-permute-done.1.refs_2_), channel_id=1, source_target_pairs={{0,4},{4,0},{8,12},{12,8},{16,20},{20,16},{24,28},{28,24},{1,5},{5... | collective-permute-start | bytes 196616 | tf_op jit(solution)/shard_map/ppermute | solution.py:28
  12.1 1.6 %collective-permute-start.8 = (bf16[288,256]{1,0:T(8,128)(2,1)S(1)}, bf16[288,256]{1,0:T(8,128)(2,1)S(1)}, u32[]{:S(2)}, u32[]{:S(2)}) collective-permute-start(bf16[288,256]{1,0:T(8,128)(2,1)S(1)} %cotangents_so_far.1), channel_id=1, source_target_pairs={{0,2},{1,3},{2,0},{3,1},{4,5},{5,4},{6,7},{7,6},{8,10},{9,11},{10,... | collective-permute-start | bytes 442376 | tf_op jit(solution)/shard_map/ppermute | solution.py:40
  13.7 0.2 tile_products.1
  14.0 0.0 copy-start.1
  14.0 11.2 %all-gather = bf16[1536,256]{1,0:T(8,128)(2,1)S(1)} all-gather(bf16[384,256]{1,0:T(8,128)(2,1)S(1)} %get-tuple-element.32), channel_id=2, replica_groups=mesh['row'=8,'col'=4] {'col'}, dimensions={0}, use_global_device_ids=true | all-gather | bytes 983040 | tf_op jit(solution)/shard_map/all_gather | solution.py:339
  25.2 1.2 %dense_layer.1 = (bf16[128,256]{1,0:T(8,128)(2,1)S(1)}, bf16[656,256]{1,0:T(8,128)(2,1)S(1)}, f32[512,256]{1,0:T(8,128)S(1)}, f32[128,256]{1,0:T(8,128)S(1)}) custom-call(s32[6]{0:T(128)S(4)} %get-tuple-element.25.ints.refs_0_, s32[2]{0:T(128)S(4)} %get-tuple-element.30.refs_1_, bf16[256,256]{1,0:T(8,128)(2,1)S(1)} %copy-done.1, ...), custom_call_target="tpu_custom_call" | custom-call | tf_op jit(solution)/shard_map/dense_layer/pallas_call | solution.py:262
  26.4 0.1 collective-permute-start.9
  26.5 1.6 %collective-permute-done.9.came = bf16[656,256]{1,0:T(8,128)(2,1)S(1)} collective-permute-done((bf16[656,256]{1,0:T(8,128)(2,1)S(1)}, bf16[656,256]{1,0:T(8,128)(2,1)S(1)}, u32[]{:S(2)}, u32[]{:S(2)}) %collective-permute-start.9) | collective-permute-done | bytes 335904 | tf_op jit(solution)/shard_map/ppermute | solution.py:28
  28.1 0.1 chip_sums.1
  28.2 2.1 %collective-permute-start.11 = (bf16[272,256]{1,0:T(8,128)(2,1)S(1)}, bf16[272,256]{1,0:T(8,128)(2,1)S(1)}, u32[]{:S(2)}, u32[]{:S(2)}) collective-permute-start(bf16[272,256]{1,0:T(8,128)(2,1)S(1)} %get-tuple-element.40), channel_id=1, source_target_pairs={{0,16},{4,28},{8,24},{12,20},{16,0},{20,12},{24,8},{28,4},{1,17},{... | collective-permute-start | bytes 417800 | tf_op jit(solution)/shard_map/ppermute | solution.py:56
  30.3 2.0 %collective-permute-start.10 = (bf16[272,256]{1,0:T(8,128)(2,1)S(1)}, bf16[272,256]{1,0:T(8,128)(2,1)S(1)}, u32[]{:S(2)}, u32[]{:S(2)}) collective-permute-start(bf16[272,256]{1,0:T(8,128)(2,1)S(1)} %get-tuple-element.39.refs_0_), channel_id=1, source_target_pairs={{0,8},{4,12},{8,0},{12,4},{16,24},{20,28},{24,16},{28,20},{1,9},{5... | collective-permute-start | bytes 417800 | tf_op jit(solution)/shard_map/ppermute | solution.py:56
  32.3 0.3 collective-permute-start.12
  32.6 9.1 %collective-permute-done.12.refs_2_.refs_3_ = bf16[256,256]{1,0:T(8,128)(2,1)S(1)} collective-permute-done((bf16[256,256]{1,0:T(8,128)(2,1)S(1)}, bf16[256,256]{1,0:T(8,128)(2,1)S(1)}, u32[]{:S(2)}, u32[]{:S(2)}) %collective-permute-start.12) | collective-permute-done | bytes 131104 | tf_op jit(solution)/shard_map/ppermute | solution.py:56
  41.8 0.1 collective-permute-start.13
  41.9 0.7 %node_results.1 = (bf16[128,256]{1,0:T(8,128)(2,1)}, bf16[128,256]{1,0:T(8,128)(2,1)}) custom-call(bf16[128,256]{1,0:T(8,128)(2,1)S(1)} %get-tuple-element.34.own_hidden, f32[128,256]{1,0:T(8,128)S(1)} %get-tuple-element.38.mine, bf16[272,256]{1,0:T(8,128)(2,1)S(1)} %collective-permute-done.10.refs_0_.refs_1_, ...), custom_call_target="tpu_custom_call" | custom-call | tf_op jit(solution)/shard_map/node_results/pallas_call | solution.py:262
  42.6 0.6 %collective-permute-done.13.other = f32[136,256]{1,0:T(8,128)S(1)} collective-permute-done((f32[136,256]{1,0:T(8,128)S(1)}, f32[136,256]{1,0:T(8,128)S(1)}, u32[]{:S(2)}, u32[]{:S(2)}) %collective-permute-start.13) | collective-permute-done | bytes 139296 | tf_op jit(solution)/shard_map/ppermute | solution.py:28
  43.2 0.7 %weight_results.1 = (f32[256,256]{1,0:T(8,128)}, f32[1,256]{1,0:T(1,128)}) custom-call(f32[136,256]{1,0:T(8,128)S(1)} %line_weight.1.own, f32[136,256]{1,0:T(8,128)S(1)} %collective-permute-done.13.other), custom_call_target="tpu_custom_call" | custom-call | tf_op jit(solution)/shard_map/weight_results/pallas_call | solution.py:262
  (20 shorter events, 0.1 us)
Async XLA Ops:
  0.6 8.5 %copy-start.2 = (bf16[1,128,256]{2,1,0:T(8,128)(2,1)S(1)}, bf16[1,128,256]{2,1,0:T(8,128)(2,1)}, u32[]{:S(2)}) copy-start(bf16[1,128,256]{2,1,0:T(8,128)(2,1)} %param.9) | copy-start | bytes 196612
  0.6 9.1 %collective-permute-start.5 = (bf16[128,256]{1,0:T(8,128)(2,1)}, bf16[128,256]{1,0:T(8,128)(2,1)S(1)}, u32[]{:S(2)}, u32[]{:S(2)}) collective-permute-start(bf16[128,256]{1,0:T(8,128)(2,1)} %bitcast.15), channel_id=1, source_target_pairs={{0,24},{4,28},{8,16},{12,20},{16,8},{20,12},{24,0},{28,4},{1,25},{... | collective-permute-start | bytes 196616 | tf_op jit(solution)/shard_map/ppermute | solution.py:28
  5.8 5.8 %collective-permute-start.3 = (bf16[128,256]{1,0:T(8,128)(2,1)}, bf16[128,256]{1,0:T(8,128)(2,1)S(1)}, u32[]{:S(2)}, u32[]{:S(2)}) collective-permute-start(bf16[128,256]{1,0:T(8,128)(2,1)} %bitcast.16), channel_id=1, source_target_pairs={{0,16},{4,20},{8,24},{12,28},{16,0},{20,4},{24,8},{28,12},{1,17},{... | collective-permute-start | bytes 196616 | tf_op jit(solution)/shard_map/ppermute | solution.py:28
  5.8 5.8 %collective-permute-start.1 = (bf16[128,256]{1,0:T(8,128)(2,1)}, bf16[128,256]{1,0:T(8,128)(2,1)S(1)}, u32[]{:S(2)}, u32[]{:S(2)}) collective-permute-start(bf16[128,256]{1,0:T(8,128)(2,1)} %bitcast.17), channel_id=1, source_target_pairs={{0,8},{4,12},{8,0},{12,4},{16,24},{20,28},{24,16},{28,20},{1,9},{5... | collective-permute-start | bytes 196616 | tf_op jit(solution)/shard_map/ppermute | solution.py:28
  7.4 4.7 %collective-permute-start.7 = (bf16[144,256]{1,0:T(8,128)(2,1)S(1)}, bf16[144,256]{1,0:T(8,128)(2,1)S(1)}, u32[]{:S(2)}, u32[]{:S(2)}) collective-permute-start(bf16[144,256]{1,0:T(8,128)(2,1)S(1)} %get-tuple-element.33.refs_0_.refs_6_), channel_id=1, source_target_pairs={{0,1},{1,0},{2,3},{3,2},{4,6},{5,7},{6,4},{7,5},{8,9},{9,8},{10,11... | collective-permute-start | bytes 221192 | tf_op jit(solution)/shard_map/ppermute | solution.py:40
  9.1 4.6 %collective-permute-start = (bf16[128,256]{1,0:T(8,128)(2,1)S(1)}, bf16[128,256]{1,0:T(8,128)(2,1)S(1)}, u32[]{:S(2)}, u32[]{:S(2)}) collective-permute-start(bf16[128,256]{1,0:T(8,128)(2,1)S(1)} %bitcast.18), channel_id=1, source_target_pairs={{0,4},{4,0},{8,12},{12,8},{16,20},{20,16},{24,28},{28,24},{1,5},{5... | collective-permute-start | bytes 196616 | tf_op jit(solution)/shard_map/ppermute | solution.py:28
  9.8 3.9 %copy-start = (bf16[1,1,3,128,128]{4,3,2,1,0:T(8,128)(2,1)S(1)}, bf16[1,1,3,128,128]{4,3,2,1,0:T(8,128)(2,1)}, u32[]{:S(2)}) copy-start(bf16[1,1,3,128,128]{4,3,2,1,0:T(8,128)(2,1)} %param.10) | copy-start | bytes 294916
  9.8 3.9 %collective-permute-start.6 = (bf16[128,256]{1,0:T(8,128)(2,1)S(1)}, bf16[128,256]{1,0:T(8,128)(2,1)S(1)}, u32[]{:S(2)}, u32[]{:S(2)}) collective-permute-start(bf16[128,256]{1,0:T(8,128)(2,1)S(1)} %collective-permute-done.5.refs_6_), channel_id=1, source_target_pairs={{0,4},{4,0},{8,12},{12,8},{16,20},{20,16},{24,28},{28,24},{1,5},{5... | collective-permute-start | bytes 196616 | tf_op jit(solution)/shard_map/ppermute | solution.py:28
  11.6 2.1 %collective-permute-start.4 = (bf16[128,256]{1,0:T(8,128)(2,1)S(1)}, bf16[128,256]{1,0:T(8,128)(2,1)S(1)}, u32[]{:S(2)}, u32[]{:S(2)}) collective-permute-start(bf16[128,256]{1,0:T(8,128)(2,1)S(1)} %collective-permute-done.3.refs_4_), channel_id=1, source_target_pairs={{0,4},{4,0},{8,12},{12,8},{16,20},{20,16},{24,28},{28,24},{1,5},{5... | collective-permute-start | bytes 196616 | tf_op jit(solution)/shard_map/ppermute | solution.py:28
  11.6 2.1 %collective-permute-start.2 = (bf16[128,256]{1,0:T(8,128)(2,1)S(1)}, bf16[128,256]{1,0:T(8,128)(2,1)S(1)}, u32[]{:S(2)}, u32[]{:S(2)}) collective-permute-start(bf16[128,256]{1,0:T(8,128)(2,1)S(1)} %collective-permute-done.1.refs_2_), channel_id=1, source_target_pairs={{0,4},{4,0},{8,12},{12,8},{16,20},{20,16},{24,28},{28,24},{1,5},{5... | collective-permute-start | bytes 196616 | tf_op jit(solution)/shard_map/ppermute | solution.py:28
  12.1 13.1 %collective-permute-start.8 = (bf16[288,256]{1,0:T(8,128)(2,1)S(1)}, bf16[288,256]{1,0:T(8,128)(2,1)S(1)}, u32[]{:S(2)}, u32[]{:S(2)}) collective-permute-start(bf16[288,256]{1,0:T(8,128)(2,1)S(1)} %cotangents_so_far.1), channel_id=1, source_target_pairs={{0,2},{1,3},{2,0},{3,1},{4,5},{5,4},{6,7},{7,6},{8,10},{9,11},{10,... | collective-permute-start | bytes 442376 | tf_op jit(solution)/shard_map/ppermute | solution.py:40
  14.0 11.2 %copy-start.1 = (bf16[256,256]{1,0:T(8,128)(2,1)S(1)}, bf16[256,256]{1,0:T(8,128)(2,1)}, u32[]{:S(2)}) copy-start(bf16[256,256]{1,0:T(8,128)(2,1)} %refs_2_.1) | copy-start | bytes 393220
  26.4 1.7 %collective-permute-start.9 = (bf16[656,256]{1,0:T(8,128)(2,1)S(1)}, bf16[656,256]{1,0:T(8,128)(2,1)S(1)}, u32[]{:S(2)}, u32[]{:S(2)}) collective-permute-start(bf16[656,256]{1,0:T(8,128)(2,1)S(1)} %get-tuple-element.37.own_sent), channel_id=1, source_target_pairs={{0,4},{4,0},{8,12},{12,8},{16,20},{20,16},{24,28},{28,24},{1,5},{5... | collective-permute-start | bytes 1007624 | tf_op jit(solution)/shard_map/ppermute | solution.py:28
  28.2 13.5 %collective-permute-start.11 = (bf16[272,256]{1,0:T(8,128)(2,1)S(1)}, bf16[272,256]{1,0:T(8,128)(2,1)S(1)}, u32[]{:S(2)}, u32[]{:S(2)}) collective-permute-start(bf16[272,256]{1,0:T(8,128)(2,1)S(1)} %get-tuple-element.40), channel_id=1, source_target_pairs={{0,16},{4,28},{8,24},{12,20},{16,0},{20,12},{24,8},{28,4},{1,17},{... | collective-permute-start | bytes 417800 | tf_op jit(solution)/shard_map/ppermute | solution.py:56
  30.3 11.5 %collective-permute-start.10 = (bf16[272,256]{1,0:T(8,128)(2,1)S(1)}, bf16[272,256]{1,0:T(8,128)(2,1)S(1)}, u32[]{:S(2)}, u32[]{:S(2)}) collective-permute-start(bf16[272,256]{1,0:T(8,128)(2,1)S(1)} %get-tuple-element.39.refs_0_), channel_id=1, source_target_pairs={{0,8},{4,12},{8,0},{12,4},{16,24},{20,28},{24,16},{28,20},{1,9},{5... | collective-permute-start | bytes 417800 | tf_op jit(solution)/shard_map/ppermute | solution.py:56
  32.3 9.4 %collective-permute-start.12 = (bf16[256,256]{1,0:T(8,128)(2,1)S(1)}, bf16[256,256]{1,0:T(8,128)(2,1)S(1)}, u32[]{:S(2)}, u32[]{:S(2)}) collective-permute-start(bf16[256,256]{1,0:T(8,128)(2,1)S(1)} %get-tuple-element.41), channel_id=1, source_target_pairs={{0,24},{4,20},{8,16},{12,28},{16,8},{20,4},{24,0},{28,12},{1,25},{... | collective-permute-start | bytes 393224 | tf_op jit(solution)/shard_map/ppermute | solution.py:56
  41.8 1.4 %collective-permute-start.13 = (f32[136,256]{1,0:T(8,128)S(1)}, f32[136,256]{1,0:T(8,128)S(1)}, u32[]{:S(2)}, u32[]{:S(2)}) collective-permute-start(f32[136,256]{1,0:T(8,128)S(1)} %line_weight.1.own), channel_id=1, source_target_pairs={{0,4},{4,0},{8,12},{12,8},{16,20},{20,16},{24,28},{28,24},{1,5},{5... | collective-permute-start | bytes 417800 | tf_op jit(solution)/shard_map/ppermute | solution.py:28

commit v10 on v9

--- a/solution.py
+++ b/solution.py
@@ -270,6 +270,7 @@
         + [pl.BlockSpec(memory_space=pltpu.VMEM)] * len(arrays),
         out_specs=[pl.BlockSpec(memory_space=space(dtype)) for _, dtype, _ in outs],
         scratch_shapes=[space(dtype)(shape, dtype) for shape, dtype in scratch],
+        cost_estimate=pl.CostEstimate(flops=0, bytes_accessed=0, transcendentals=0),
         compiler_params=pltpu.CompilerParams(vmem_limit_bytes=need + 8 * 1024 * 1024),
     )(*ints, *arrays)
 

time: 44.1 us -> 44.1 us (level)
  no operation moved by 1% of the time
where the time goes in v10:
time: 44.1 us; the launch traced here: 43.9 us
  starting transfers between devices  14.8 us (34%)
  waiting for transfers between devices  12.6 us (29%)
  blocking collectives  11.2 us (25%)
  Pallas kernels  3.95 us (9%)
  between operations  1.4 us (3%)
    all_gather x1, blocking collectives, on_device(): products = lax.all_gather(product, 'col')  11.2 us
    ppermute x3, waiting for transfers between devices, line_exchange(): return lax.ppermute(value, 'row', pairs)  9.1 us
    ppermute x9, starting transfers between devices, exchange(): return lax.ppermute(value, axis, [(i, i ^ mask) for i in range(size)])  7.02 us
    ppermute x3, starting transfers between devices, line_exchange(): return lax.ppermute(value, 'row', pairs)  4.45 us
    pallas_call x8, Pallas kernels, call(): pl.pallas_call(kernel, name=name, out_shape=[space(dtype)(shape, dtype) i...  3.95 us
    ppermute x9, waiting for transfers between devices, exchange(): return lax.ppermute(value, axis, [(i, i ^ mask) for i in range(size)])  3.5 us
    ppermute x2, starting transfers between devices, column_exchange(): return lax.ppermute(value, ('row', 'col'), pairs)  3.29 us
  transfers between devices with their start and end apart: 14, of which 4 were waited for; matrix products, arithmetic and copies ran while one was open for 0% of the time, Pallas kernels for 4%

profile of v10, /device:TPU:0, one launch (start us, length us, event | category | flops | bytes accessed | tf_op | source)
XLA Modules:
  0.0 43.9 jit_solution(682055692333036404)
XLA Ops:
  0.6 5.1 %collective-permute-start.5 = (bf16[128,256]{1,0:T(8,128)(2,1)}, bf16[128,256]{1,0:T(8,128)(2,1)S(1)}, u32[]{:S(2)}, u32[]{:S(2)}) collective-permute-start(bf16[128,256]{1,0:T(8,128)(2,1)} %bitcast.15), channel_id=1, source_target_pairs={{0,24},{4,28},{8,16},{12,20},{16,8},{20,12},{24,0},{28,4},{1,25},{... | collective-permute-start | bytes 196616 | tf_op jit(solution)/shard_map/ppermute | solution.py:28
  5.8 0.6 %collective-permute-start.1 = (bf16[128,256]{1,0:T(8,128)(2,1)}, bf16[128,256]{1,0:T(8,128)(2,1)S(1)}, u32[]{:S(2)}, u32[]{:S(2)}) collective-permute-start(bf16[128,256]{1,0:T(8,128)(2,1)} %bitcast.17), channel_id=1, source_target_pairs={{0,8},{4,12},{8,0},{12,4},{16,24},{20,28},{24,16},{28,20},{1,9},{5... | collective-permute-start | bytes 196616 | tf_op jit(solution)/shard_map/ppermute | solution.py:28
  6.4 1.0 %masked_cotangent.1 = (bf16[144,256]{1,0:T(8,128)(2,1)S(1)}, f32[1,256]{1,0:T(1,128)S(1)}, s32[6]{0:T(128)S(4)}) custom-call(s32[3]{0:T(128)} %bitcast.22, s32[3]{0:T(128)} %bitcast.23, s32[1,128]{1,0:T(1,128)} %mask.1, bf16[128,256]{1,0:T(8,128)(2,1)} %bitcast.20, f32[1,256]{1,0:T(1,128)} %bitcast.21), custom_call_target="tpu_custom_call" | custom-call | tf_op jit(solution)/shard_map/masked_cotangent/pallas_call | solution.py:262
  7.4 1.7 %collective-permute-start.7 = (bf16[144,256]{1,0:T(8,128)(2,1)S(1)}, bf16[144,256]{1,0:T(8,128)(2,1)S(1)}, u32[]{:S(2)}, u32[]{:S(2)}) collective-permute-start(bf16[144,256]{1,0:T(8,128)(2,1)S(1)} %get-tuple-element.33.refs_0_.refs_6_), channel_id=1, source_target_pairs={{0,1},{1,0},{2,3},{3,2},{4,6},{5,7},{6,4},{7,5},{8,9},{9,8},{10,11... | collective-permute-start | bytes 221192 | tf_op jit(solution)/shard_map/ppermute | solution.py:40
  9.8 0.0 copy-start
  9.8 0.6 %collective-permute-start.6 = (bf16[128,256]{1,0:T(8,128)(2,1)S(1)}, bf16[128,256]{1,0:T(8,128)(2,1)S(1)}, u32[]{:S(2)}, u32[]{:S(2)}) collective-permute-start(bf16[128,256]{1,0:T(8,128)(2,1)S(1)} %collective-permute-done.5.refs_6_), channel_id=1, source_target_pairs={{0,4},{4,0},{8,12},{12,8},{16,20},{20,16},{24,28},{28,24},{1,5},{5... | collective-permute-start | bytes 196616 | tf_op jit(solution)/shard_map/ppermute | solution.py:28
  10.4 1.2 %collective-permute-done.3.refs_4_ = bf16[128,256]{1,0:T(8,128)(2,1)S(1)} collective-permute-done((bf16[128,256]{1,0:T(8,128)(2,1)}, bf16[128,256]{1,0:T(8,128)(2,1)S(1)}, u32[]{:S(2)}, u32[]{:S(2)}) %collective-permute-start.3) | collective-permute-done | bytes 65568 | tf_op jit(solution)/shard_map/ppermute | solution.py:28
  11.6 0.5 %collective-permute-start.2 = (bf16[128,256]{1,0:T(8,128)(2,1)S(1)}, bf16[128,256]{1,0:T(8,128)(2,1)S(1)}, u32[]{:S(2)}, u32[]{:S(2)}) collective-permute-start(bf16[128,256]{1,0:T(8,128)(2,1)S(1)} %collective-permute-done.1.refs_2_), channel_id=1, source_target_pairs={{0,4},{4,0},{8,12},{12,8},{16,20},{20,16},{24,28},{28,24},{1,5},{5... | collective-permute-start | bytes 196616 | tf_op jit(solution)/shard_map/ppermute | solution.py:28
  12.1 1.6 %collective-permute-start.8 = (bf16[288,256]{1,0:T(8,128)(2,1)S(1)}, bf16[288,256]{1,0:T(8,128)(2,1)S(1)}, u32[]{:S(2)}, u32[]{:S(2)}) collective-permute-start(bf16[288,256]{1,0:T(8,128)(2,1)S(1)} %cotangents_so_far.1), channel_id=1, source_target_pairs={{0,2},{1,3},{2,0},{3,1},{4,5},{5,4},{6,7},{7,6},{8,10},{9,11},{10,... | collective-permute-start | bytes 442376 | tf_op jit(solution)/shard_map/ppermute | solution.py:40
  13.7 0.2 tile_products.1
  14.0 0.0 copy-start.1
  14.0 11.2 %all-gather = bf16[1536,256]{1,0:T(8,128)(2,1)S(1)} all-gather(bf16[384,256]{1,0:T(8,128)(2,1)S(1)} %get-tuple-element.32), channel_id=2, replica_groups=mesh['row'=8,'col'=4] {'col'}, dimensions={0}, use_global_device_ids=true | all-gather | bytes 983040 | tf_op jit(solution)/shard_map/all_gather | solution.py:340
  25.2 1.2 %dense_layer.1 = (bf16[128,256]{1,0:T(8,128)(2,1)S(1)}, bf16[656,256]{1,0:T(8,128)(2,1)S(1)}, f32[512,256]{1,0:T(8,128)S(1)}, f32[128,256]{1,0:T(8,128)S(1)}) custom-call(s32[6]{0:T(128)S(4)} %get-tuple-element.25.ints.refs_0_, s32[2]{0:T(128)S(4)} %get-tuple-element.30.refs_1_, bf16[256,256]{1,0:T(8,128)(2,1)S(1)} %copy-done.1, ...), custom_call_target="tpu_custom_call" | custom-call | tf_op jit(solution)/shard_map/dense_layer/pallas_call | solution.py:262
  26.4 0.1 collective-permute-start.9
  26.5 1.6 %collective-permute-done.9.came = bf16[656,256]{1,0:T(8,128)(2,1)S(1)} collective-permute-done((bf16[656,256]{1,0:T(8,128)(2,1)S(1)}, bf16[656,256]{1,0:T(8,128)(2,1)S(1)}, u32[]{:S(2)}, u32[]{:S(2)}) %collective-permute-start.9) | collective-permute-done | bytes 335904 | tf_op jit(solution)/shard_map/ppermute | solution.py:28
  28.1 0.1 chip_sums.1
  28.2 2.1 %collective-permute-start.11 = (bf16[272,256]{1,0:T(8,128)(2,1)S(1)}, bf16[272,256]{1,0:T(8,128)(2,1)S(1)}, u32[]{:S(2)}, u32[]{:S(2)}) collective-permute-start(bf16[272,256]{1,0:T(8,128)(2,1)S(1)} %get-tuple-element.40), channel_id=1, source_target_pairs={{0,16},{4,28},{8,24},{12,20},{16,0},{20,12},{24,8},{28,4},{1,17},{... | collective-permute-start | bytes 417800 | tf_op jit(solution)/shard_map/ppermute | solution.py:56
  30.3 2.0 %collective-permute-start.10 = (bf16[272,256]{1,0:T(8,128)(2,1)S(1)}, bf16[272,256]{1,0:T(8,128)(2,1)S(1)}, u32[]{:S(2)}, u32[]{:S(2)}) collective-permute-start(bf16[272,256]{1,0:T(8,128)(2,1)S(1)} %get-tuple-element.39.refs_0_), channel_id=1, source_target_pairs={{0,8},{4,12},{8,0},{12,4},{16,24},{20,28},{24,16},{28,20},{1,9},{5... | collective-permute-start | bytes 417800 | tf_op jit(solution)/shard_map/ppermute | solution.py:56
  32.3 0.4 collective-permute-start.12
  32.6 9.1 %collective-permute-done.12.refs_2_.refs_3_ = bf16[256,256]{1,0:T(8,128)(2,1)S(1)} collective-permute-done((bf16[256,256]{1,0:T(8,128)(2,1)S(1)}, bf16[256,256]{1,0:T(8,128)(2,1)S(1)}, u32[]{:S(2)}, u32[]{:S(2)}) %collective-permute-start.12) | collective-permute-done | bytes 131104 | tf_op jit(solution)/shard_map/ppermute | solution.py:56
  41.8 0.1 collective-permute-start.13
  41.9 0.7 %node_results.1 = (bf16[128,256]{1,0:T(8,128)(2,1)}, bf16[128,256]{1,0:T(8,128)(2,1)}) custom-call(bf16[128,256]{1,0:T(8,128)(2,1)S(1)} %get-tuple-element.34.own_hidden, f32[128,256]{1,0:T(8,128)S(1)} %get-tuple-element.38.mine, bf16[272,256]{1,0:T(8,128)(2,1)S(1)} %collective-permute-done.10.refs_0_.refs_1_, ...), custom_call_target="tpu_custom_call" | custom-call | tf_op jit(solution)/shard_map/node_results/pallas_call | solution.py:262
  42.6 0.6 %collective-permute-done.13.other = f32[136,256]{1,0:T(8,128)S(1)} collective-permute-done((f32[136,256]{1,0:T(8,128)S(1)}, f32[136,256]{1,0:T(8,128)S(1)}, u32[]{:S(2)}, u32[]{:S(2)}) %collective-permute-start.13) | collective-permute-done | bytes 139296 | tf_op jit(solution)/shard_map/ppermute | solution.py:28
  43.2 0.7 %weight_results.1 = (f32[256,256]{1,0:T(8,128)}, f32[1,256]{1,0:T(1,128)}) custom-call(f32[136,256]{1,0:T(8,128)S(1)} %line_weight.1.own, f32[136,256]{1,0:T(8,128)S(1)} %collective-permute-done.13.other), custom_call_target="tpu_custom_call" | custom-call | tf_op jit(solution)/shard_map/weight_results/pallas_call | solution.py:262
  (20 shorter events, 0.1 us)
Async XLA Ops:
  0.6 8.5 %copy-start.2 = (bf16[1,128,256]{2,1,0:T(8,128)(2,1)S(1)}, bf16[1,128,256]{2,1,0:T(8,128)(2,1)}, u32[]{:S(2)}) copy-start(bf16[1,128,256]{2,1,0:T(8,128)(2,1)} %param.9) | copy-start | bytes 196612
  0.6 9.1 %collective-permute-start.5 = (bf16[128,256]{1,0:T(8,128)(2,1)}, bf16[128,256]{1,0:T(8,128)(2,1)S(1)}, u32[]{:S(2)}, u32[]{:S(2)}) collective-permute-start(bf16[128,256]{1,0:T(8,128)(2,1)} %bitcast.15), channel_id=1, source_target_pairs={{0,24},{4,28},{8,16},{12,20},{16,8},{20,12},{24,0},{28,4},{1,25},{... | collective-permute-start | bytes 196616 | tf_op jit(solution)/shard_map/ppermute | solution.py:28
  5.8 5.8 %collective-permute-start.3 = (bf16[128,256]{1,0:T(8,128)(2,1)}, bf16[128,256]{1,0:T(8,128)(2,1)S(1)}, u32[]{:S(2)}, u32[]{:S(2)}) collective-permute-start(bf16[128,256]{1,0:T(8,128)(2,1)} %bitcast.16), channel_id=1, source_target_pairs={{0,16},{4,20},{8,24},{12,28},{16,0},{20,4},{24,8},{28,12},{1,17},{... | collective-permute-start | bytes 196616 | tf_op jit(solution)/shard_map/ppermute | solution.py:28
  5.8 5.8 %collective-permute-start.1 = (bf16[128,256]{1,0:T(8,128)(2,1)}, bf16[128,256]{1,0:T(8,128)(2,1)S(1)}, u32[]{:S(2)}, u32[]{:S(2)}) collective-permute-start(bf16[128,256]{1,0:T(8,128)(2,1)} %bitcast.17), channel_id=1, source_target_pairs={{0,8},{4,12},{8,0},{12,4},{16,24},{20,28},{24,16},{28,20},{1,9},{5... | collective-permute-start | bytes 196616 | tf_op jit(solution)/shard_map/ppermute | solution.py:28
  7.4 4.7 %collective-permute-start.7 = (bf16[144,256]{1,0:T(8,128)(2,1)S(1)}, bf16[144,256]{1,0:T(8,128)(2,1)S(1)}, u32[]{:S(2)}, u32[]{:S(2)}) collective-permute-start(bf16[144,256]{1,0:T(8,128)(2,1)S(1)} %get-tuple-element.33.refs_0_.refs_6_), channel_id=1, source_target_pairs={{0,1},{1,0},{2,3},{3,2},{4,6},{5,7},{6,4},{7,5},{8,9},{9,8},{10,11... | collective-permute-start | bytes 221192 | tf_op jit(solution)/shard_map/ppermute | solution.py:40
  9.1 4.6 %collective-permute-start = (bf16[128,256]{1,0:T(8,128)(2,1)S(1)}, bf16[128,256]{1,0:T(8,128)(2,1)S(1)}, u32[]{:S(2)}, u32[]{:S(2)}) collective-permute-start(bf16[128,256]{1,0:T(8,128)(2,1)S(1)} %bitcast.18), channel_id=1, source_target_pairs={{0,4},{4,0},{8,12},{12,8},{16,20},{20,16},{24,28},{28,24},{1,5},{5... | collective-permute-start | bytes 196616 | tf_op jit(solution)/shard_map/ppermute | solution.py:28
  9.8 3.9 %copy-start = (bf16[1,1,3,128,128]{4,3,2,1,0:T(8,128)(2,1)S(1)}, bf16[1,1,3,128,128]{4,3,2,1,0:T(8,128)(2,1)}, u32[]{:S(2)}) copy-start(bf16[1,1,3,128,128]{4,3,2,1,0:T(8,128)(2,1)} %param.10) | copy-start | bytes 294916
  9.8 3.9 %collective-permute-start.6 = (bf16[128,256]{1,0:T(8,128)(2,1)S(1)}, bf16[128,256]{1,0:T(8,128)(2,1)S(1)}, u32[]{:S(2)}, u32[]{:S(2)}) collective-permute-start(bf16[128,256]{1,0:T(8,128)(2,1)S(1)} %collective-permute-done.5.refs_6_), channel_id=1, source_target_pairs={{0,4},{4,0},{8,12},{12,8},{16,20},{20,16},{24,28},{28,24},{1,5},{5... | collective-permute-start | bytes 196616 | tf_op jit(solution)/shard_map/ppermute | solution.py:28
  11.6 2.1 %collective-permute-start.4 = (bf16[128,256]{1,0:T(8,128)(2,1)S(1)}, bf16[128,256]{1,0:T(8,128)(2,1)S(1)}, u32[]{:S(2)}, u32[]{:S(2)}) collective-permute-start(bf16[128,256]{1,0:T(8,128)(2,1)S(1)} %collective-permute-done.3.refs_4_), channel_id=1, source_target_pairs={{0,4},{4,0},{8,12},{12,8},{16,20},{20,16},{24,28},{28,24},{1,5},{5... | collective-permute-start | bytes 196616 | tf_op jit(solution)/shard_map/ppermute | solution.py:28
  11.6 2.1 %collective-permute-start.2 = (bf16[128,256]{1,0:T(8,128)(2,1)S(1)}, bf16[128,256]{1,0:T(8,128)(2,1)S(1)}, u32[]{:S(2)}, u32[]{:S(2)}) collective-permute-start(bf16[128,256]{1,0:T(8,128)(2,1)S(1)} %collective-permute-done.1.refs_2_), channel_id=1, source_target_pairs={{0,4},{4,0},{8,12},{12,8},{16,20},{20,16},{24,28},{28,24},{1,5},{5... | collective-permute-start | bytes 196616 | tf_op jit(solution)/shard_map/ppermute | solution.py:28
  12.1 13.1 %collective-permute-start.8 = (bf16[288,256]{1,0:T(8,128)(2,1)S(1)}, bf16[288,256]{1,0:T(8,128)(2,1)S(1)}, u32[]{:S(2)}, u32[]{:S(2)}) collective-permute-start(bf16[288,256]{1,0:T(8,128)(2,1)S(1)} %cotangents_so_far.1), channel_id=1, source_target_pairs={{0,2},{1,3},{2,0},{3,1},{4,5},{5,4},{6,7},{7,6},{8,10},{9,11},{10,... | collective-permute-start | bytes 442376 | tf_op jit(solution)/shard_map/ppermute | solution.py:40
  14.0 11.2 %copy-start.1 = (bf16[256,256]{1,0:T(8,128)(2,1)S(1)}, bf16[256,256]{1,0:T(8,128)(2,1)}, u32[]{:S(2)}) copy-start(bf16[256,256]{1,0:T(8,128)(2,1)} %refs_2_.1) | copy-start | bytes 393220
  26.4 1.7 %collective-permute-start.9 = (bf16[656,256]{1,0:T(8,128)(2,1)S(1)}, bf16[656,256]{1,0:T(8,128)(2,1)S(1)}, u32[]{:S(2)}, u32[]{:S(2)}) collective-permute-start(bf16[656,256]{1,0:T(8,128)(2,1)S(1)} %get-tuple-element.37.own_sent), channel_id=1, source_target_pairs={{0,4},{4,0},{8,12},{12,8},{16,20},{20,16},{24,28},{28,24},{1,5},{5... | collective-permute-start | bytes 1007624 | tf_op jit(solution)/shard_map/ppermute | solution.py:28
  28.2 13.5 %collective-permute-start.11 = (bf16[272,256]{1,0:T(8,128)(2,1)S(1)}, bf16[272,256]{1,0:T(8,128)(2,1)S(1)}, u32[]{:S(2)}, u32[]{:S(2)}) collective-permute-start(bf16[272,256]{1,0:T(8,128)(2,1)S(1)} %get-tuple-element.40), channel_id=1, source_target_pairs={{0,16},{4,28},{8,24},{12,20},{16,0},{20,12},{24,8},{28,4},{1,17},{... | collective-permute-start | bytes 417800 | tf_op jit(solution)/shard_map/ppermute | solution.py:56
  30.3 11.5 %collective-permute-start.10 = (bf16[272,256]{1,0:T(8,128)(2,1)S(1)}, bf16[272,256]{1,0:T(8,128)(2,1)S(1)}, u32[]{:S(2)}, u32[]{:S(2)}) collective-permute-start(bf16[272,256]{1,0:T(8,128)(2,1)S(1)} %get-tuple-element.39.refs_0_), channel_id=1, source_target_pairs={{0,8},{4,12},{8,0},{12,4},{16,24},{20,28},{24,16},{28,20},{1,9},{5... | collective-permute-start | bytes 417800 | tf_op jit(solution)/shard_map/ppermute | solution.py:56
  32.3 9.4 %collective-permute-start.12 = (bf16[256,256]{1,0:T(8,128)(2,1)S(1)}, bf16[256,256]{1,0:T(8,128)(2,1)S(1)}, u32[]{:S(2)}, u32[]{:S(2)}) collective-permute-start(bf16[256,256]{1,0:T(8,128)(2,1)S(1)} %get-tuple-element.41), channel_id=1, source_target_pairs={{0,24},{4,20},{8,16},{12,28},{16,8},{20,4},{24,0},{28,12},{1,25},{... | collective-permute-start | bytes 393224 | tf_op jit(solution)/shard_map/ppermute | solution.py:56
  41.8 1.4 %collective-permute-start.13 = (f32[136,256]{1,0:T(8,128)S(1)}, f32[136,256]{1,0:T(8,128)S(1)}, u32[]{:S(2)}, u32[]{:S(2)}) collective-permute-start(f32[136,256]{1,0:T(8,128)S(1)} %line_weight.1.own), channel_id=1, source_target_pairs={{0,4},{4,0},{8,12},{12,8},{16,20},{20,16},{24,28},{28,24},{1,5},{5... | collective-permute-start | bytes 417800 | tf_op jit(solution)/shard_map/ppermute | solution.py:28
